TPU v7x, 32 devices: a whole 2x2x4 slice. The times are simulated.
32 devices in a mesh: samp: 4 (over z), arow: 4 (over y, x), acol: 2 (over core).
Axes of the slice: x: 2, y: 2, z: 4, core: 2. Of those that a mesh axis runs over, the one named last changes fastest.
Arguments:
- embeddings: bfloat16 [49152, 768], P(('samp', 'arow', 'acol')), may hold values from -6 to 6
- anchors: bfloat16 [16384, 768], P(('arow', 'acol')), may hold values from -6 to 6
- subspace: bfloat16 [16384, 64], P(('arow', 'acol')), may hold values from -3 to 3
- nearest: int32 [49152, 8], P(('samp', 'arow', 'acol')), may hold values from 0 to 16383, as said below
Outputs:
- gram_product: float32 [16384, 64], P(('arow', 'acol'))
Inputs may be any that keep to these rules, and one draw needn't show every extreme that they name: `nearest`: anchor shard o holds anchors 2048 * o to 2048 * (o + 1) - 1. The rows of one device name anchors of every one of the 8 shards, and within each of them only anchors of one aligned block of 128. The 8 anchors of a row are distinct.
All inputs are finite; a program needn't handle non-finite values.
Results may differ from a plain program's by a relative error of at most 0.0003.
Values may be sent and summed in bfloat16 or wider, within the bound.
No kernel may reach another device: no remote copies, remote signals or barrier semaphores. Data moves between devices by JAX's collectives and lax.ppermute only.
A program may use at most 128 MiB of HBM per device.

v0:
```python
import jax
import jax.numpy as jnp
from jax import lax
from jax.sharding import PartitionSpec as P

D = 768
COLS = 64
CAND = 8
BA = 128


def per_device(embeddings, anchors, subspace, nearest):
    grid_rows = lax.axis_size("arow")
    grid_cols = lax.axis_size("acol")
    owners = grid_rows * grid_cols
    self_index = lax.axis_index("arow") * grid_cols + lax.axis_index("acol")
    shard_size = anchors.shape[0]
    shard_blocks = shard_size // BA
    owner_of = nearest // shard_size
    block_of = nearest % shard_size // BA
    slot_of = owner_of * BA + nearest % BA
    matches = owner_of.reshape(-1)[:, None] == jnp.arange(owners, dtype=jnp.int32)[None, :]
    wanted = jnp.max(jnp.where(matches, block_of.reshape(-1)[:, None], -1), axis=0)
    table = lax.all_gather(wanted[None, :], ("arow", "acol"), axis=0, tiled=True)
    asked = lax.dynamic_index_in_dim(table, self_index, axis=1, keepdims=False)
    anchor_out = anchors.reshape(shard_blocks, BA, D)[asked]
    panel_out = subspace.reshape(shard_blocks, BA, COLS)[asked]
    anchor_in, panel_in = (
        lax.all_to_all(anchor_out, ("arow", "acol"), split_axis=0, concat_axis=0, tiled=True),
        lax.all_to_all(panel_out, ("arow", "acol"), split_axis=0, concat_axis=0, tiled=True),
    )
    total_slots = owners * BA
    flat_anchor = anchor_in.reshape(total_slots, D)
    flat_panel = panel_in.reshape(total_slots, COLS).astype(jnp.float32)
    anchor_scale = lax.rsqrt(jnp.mean(jnp.square(flat_anchor.astype(jnp.float32)), axis=1) + 1e-06)
    slot_iota = jnp.arange(total_slots, dtype=jnp.int32)
    row_total = embeddings.shape[0]
    block_rows = min(256, row_total)
    block_count = row_total // block_rows

    def one_block(outgoing, inputs):
        group_rows, group_slots = inputs
        rows_float = group_rows.astype(jnp.float32)
        row_scale = lax.rsqrt(jnp.mean(rows_float * rows_float, axis=1) + 1e-06)
        dense = lax.dot_general(
            group_rows, flat_anchor, (((1,), (1,)), ((), ())), preferred_element_type=jnp.float32
        )
        equal_list = [group_slots[:, k : k + 1] == slot_iota[None, :] for k in range(CAND)]
        dots = jnp.stack(
            [jnp.sum(jnp.where(equal, dense, 0.0), axis=1) for equal in equal_list], axis=1
        )
        scales = jnp.stack(
            [jnp.sum(jnp.where(equal, anchor_scale[None, :], 0.0), axis=1) for equal in equal_list],
            axis=1,
        )
        cosine = dots * row_scale[:, None] * scales / D
        kernel = jnp.exp((cosine - 1.0) / 0.05)
        weights = kernel / jnp.sum(kernel, axis=1, keepdims=True)
        zmatrix = jnp.zeros((group_rows.shape[0], total_slots), jnp.float32)
        for k in range(CAND):
            zmatrix = zmatrix + jnp.where(equal_list[k], weights[:, k : k + 1], 0.0)
        projected = jnp.dot(
            zmatrix, flat_panel, precision=lax.Precision.HIGHEST, preferred_element_type=jnp.float32
        )
        update = lax.dot_general(
            zmatrix,
            projected,
            (((0,), (0,)), ((), ())),
            precision=lax.Precision.HIGHEST,
            preferred_element_type=jnp.float32,
        )
        return (outgoing + update, None)

    outgoing, _ = lax.scan(
        one_block,
        jnp.zeros((total_slots, COLS), jnp.float32),
        (
            embeddings.reshape(block_count, block_rows, D),
            slot_of.reshape(block_count, block_rows, CAND),
        ),
    )
    returned = lax.all_to_all(
        outgoing.reshape(owners, BA, COLS),
        ("arow", "acol"),
        split_axis=0,
        concat_axis=0,
        tiled=True,
    )
    selector = (asked[None, :] == jnp.arange(shard_blocks, dtype=jnp.int32)[:, None]).astype(
        jnp.float32
    )
    mine = jnp.dot(
        selector,
        returned.reshape(owners, BA * COLS),
        precision=lax.Precision.HIGHEST,
        preferred_element_type=jnp.float32,
    )
    return lax.psum(mine.reshape(shard_size, COLS), "samp")


def solution(mesh):
    in_specs = (
        P(("samp", "arow", "acol"), None),
        P(("arow", "acol"), None),
        P(("arow", "acol"), None),
        P(("samp", "arow", "acol"), None),
    )
    out_specs = P(("arow", "acol"), None)
    return jax.shard_map(
        per_device, mesh=mesh, in_specs=in_specs, out_specs=out_specs, check_vma=False
    )
```

profile of v0, /device:TPU:0, one launch (start us, length us, event | category | flops | bytes accessed | tf_op | source)
XLA Modules:
  0.0 217.8 jit_solution(9778297361400288294)
XLA Ops:
  6.5 1.6 add_select_fusion.3
  9.3 1.4 broadcast_in_dim.214
  15.2 9.5 %all-reduce.1 = s32[8,8]{1,0:T(8,128)S(1)} all-reduce(s32[8,8]{1,0:T(8,128)S(1)} %reshape.71), channel_id=2, replica_groups=mesh['samp'=4,'arow'=4,'acol'=2] {'arow','acol'}, use_global_device_ids=true, to_apply=%add | all-reduce | flops 64 | bytes 512
  27.1 3.4 %all-to-all-start.1 = ((bf16[8,128,64]{1,2,0:T(8,128)(2,1)}), bf16[8,128,64]{1,2,0:T(8,128)(2,1)S(1)}, u32[]{:S(2)}, u32[]{:S(2)}) async-start(bf16[8,128,64]{1,2,0:T(8,128)(2,1)} %gather_fusion.1), calls=%async_computation.1 | async-start | bytes 262144 | tf_op jit(solution)/shard_map/all_to_all | solution.py:30
  30.5 1.8 gather_fusion
  32.2 3.7 %all-to-all-done.1 = bf16[8,128,64]{1,2,0:T(8,128)(2,1)S(1)} async-done(((bf16[8,128,64]{1,2,0:T(8,128)(2,1)}), bf16[8,128,64]{1,2,0:T(8,128)(2,1)S(1)}, u32[]{:S(2)}, u32[]{:S(2)}) %all-to-all-start.1) | async-done | bytes 131104 | tf_op jit(solution)/shard_map/all_to_all | solution.py:30
  35.9 4.3 %all-to-all-start = ((bf16[8,128,768]{2,1,0:T(8,128)(2,1)}), bf16[8,128,768]{2,1,0:T(8,128)(2,1)}, u32[]{:S(2)}, u32[]{:S(2)}) async-start(bf16[8,128,768]{2,1,0:T(8,128)(2,1)} %gather_fusion), calls=%async_computation | async-start | bytes 3145728 | tf_op jit(solution)/shard_map/all_to_all | solution.py:29
  41.2 20.0 %all-to-all-done = bf16[8,128,768]{2,1,0:T(8,128)(2,1)} async-done(((bf16[8,128,768]{2,1,0:T(8,128)(2,1)}), bf16[8,128,768]{2,1,0:T(8,128)(2,1)}, u32[]{:S(2)}, u32[]{:S(2)}) %all-to-all-start) | async-done | bytes 1572896 | tf_op jit(solution)/shard_map/all_to_all | solution.py:29
  61.2 1.8 multiply_reduce_fusion.1
  63.0 78.9 %while.14 = (s32[]{:T(128)}, f32[1024,64]{0,1:T(8,128)S(1)}, s32[6,256,8]{1,2,0:T(8,128)}, bf16[6,256,768]{2,1,0:T(8,128)(2,1)}, bf16[1024,768]{1,0:T(8,128)(2,1...) while((s32[]{:T(128)}, f32[1024,64]{0,1:T(8,128)S(1)}, ...), condition=%wide.region_21.22_spmd.clone.clone, body=%wide.region_2.21_spmd.clone.clone.sunk | while | flops 828592128 | bytes 3468911 | solution.py:74
  63.8 4.3 %fusion.91 = (f32[256]{0:T(256)S(1)}, f32[256]{0:T(256)S(1)}, f32[256]{0:T(256)S(1)}, f32[256]{0:T(256)S(1)}, f32[256]{0:T(256)S(1)}, /*index=5*/f32[256]{0:T(25...) fusion(f32[1024]{0:T(1024)S(1)} %get-tuple-element.397, ...), kind=kOutput, calls=%fused_computation.37.clone.1 | convolution fusion | flops 413134848 | bytes 1995264 | tf_op jit(solution)/shard_map/while/body/eval_jaxpr/dot_general | solution.py:45
  69.4 3.9 %fusion.94 = f32[256,64]{0,1:T(8,128)} fusion(f32[1024,64]{1,0:T(8,128)} %get-tuple-element.398, f32[256]{0:T(256)S(1)} %bitcast.168, f32[256]{0:T(256)S(1)} %bitcast.170, f32[256]{0:T(256)S(1)} %bitcast.172, f32[256]{0:T(256)S(1)} %bitcast.174, f32[256]{0:T(256)S(1)} %bitcast.176, f32[256]{0:T(256)S(1)} %bitcast.178, f32[256]{0:T(256)S(1)} %bitcast.180, ...), kind=kOutput, calls=%fused_computation.60.clone.1 | convolution fusion | flops 207355904 | bytes 344064 | tf_op jit(solution)/shard_map/while/body/eval_jaxpr/dot_general | solution.py:62
  73.3 2.9 %convolution_add_fusion.2 = f32[1024,64]{0,1:T(8,128)S(1)} fusion(f32[256,64]{0,1:T(8,128)} %fusion.94, f32[256]{0:T(256)S(1)} %bitcast.169, f32[256]{0:T(256)S(1)} %bitcast.171, f32[256]{0:T(256)S(1)} %bitcast.173, f32[256]{0:T(256)S(1)} %bitcast.175, f32[256]{0:T(256)S(1)} %bitcast.177, f32[256]{0:T(256)S(1)} %bitcast.179, f32[256]{0:T(256)S(1)} %bitcast.181, ...), kind=kOutput, calls=%fused_computation.35.clone.1 | convolution fusion | flops 207486976 | bytes 606209 | tf_op jit(solution)/shard_map/while/body/eval_jaxpr/dot_general | solution.py:65
  76.9 4.3 %fusion.91 = (f32[256]{0:T(256)S(1)}, f32[256]{0:T(256)S(1)}, f32[256]{0:T(256)S(1)}, f32[256]{0:T(256)S(1)}, f32[256]{0:T(256)S(1)}, /*index=5*/f32[256]{0:T(25...) fusion(f32[1024]{0:T(1024)S(1)} %get-tuple-element.397, ...), kind=kOutput, calls=%fused_computation.37.clone.1 | convolution fusion | flops 413134848 | bytes 1995264 | tf_op jit(solution)/shard_map/while/body/eval_jaxpr/dot_general | solution.py:45
  82.5 3.9 %fusion.94 = f32[256,64]{0,1:T(8,128)} fusion(f32[1024,64]{1,0:T(8,128)} %get-tuple-element.398, f32[256]{0:T(256)S(1)} %bitcast.168, f32[256]{0:T(256)S(1)} %bitcast.170, f32[256]{0:T(256)S(1)} %bitcast.172, f32[256]{0:T(256)S(1)} %bitcast.174, f32[256]{0:T(256)S(1)} %bitcast.176, f32[256]{0:T(256)S(1)} %bitcast.178, f32[256]{0:T(256)S(1)} %bitcast.180, ...), kind=kOutput, calls=%fused_computation.60.clone.1 | convolution fusion | flops 207355904 | bytes 344064 | tf_op jit(solution)/shard_map/while/body/eval_jaxpr/dot_general | solution.py:62
  86.4 2.9 %convolution_add_fusion.2 = f32[1024,64]{0,1:T(8,128)S(1)} fusion(f32[256,64]{0,1:T(8,128)} %fusion.94, f32[256]{0:T(256)S(1)} %bitcast.169, f32[256]{0:T(256)S(1)} %bitcast.171, f32[256]{0:T(256)S(1)} %bitcast.173, f32[256]{0:T(256)S(1)} %bitcast.175, f32[256]{0:T(256)S(1)} %bitcast.177, f32[256]{0:T(256)S(1)} %bitcast.179, f32[256]{0:T(256)S(1)} %bitcast.181, ...), kind=kOutput, calls=%fused_computation.35.clone.1 | convolution fusion | flops 207486976 | bytes 606209 | tf_op jit(solution)/shard_map/while/body/eval_jaxpr/dot_general | solution.py:65
  90.1 4.3 %fusion.91 = (f32[256]{0:T(256)S(1)}, f32[256]{0:T(256)S(1)}, f32[256]{0:T(256)S(1)}, f32[256]{0:T(256)S(1)}, f32[256]{0:T(256)S(1)}, /*index=5*/f32[256]{0:T(25...) fusion(f32[1024]{0:T(1024)S(1)} %get-tuple-element.397, ...), kind=kOutput, calls=%fused_computation.37.clone.1 | convolution fusion | flops 413134848 | bytes 1995264 | tf_op jit(solution)/shard_map/while/body/eval_jaxpr/dot_general | solution.py:45
  95.7 3.9 %fusion.94 = f32[256,64]{0,1:T(8,128)} fusion(f32[1024,64]{1,0:T(8,128)} %get-tuple-element.398, f32[256]{0:T(256)S(1)} %bitcast.168, f32[256]{0:T(256)S(1)} %bitcast.170, f32[256]{0:T(256)S(1)} %bitcast.172, f32[256]{0:T(256)S(1)} %bitcast.174, f32[256]{0:T(256)S(1)} %bitcast.176, f32[256]{0:T(256)S(1)} %bitcast.178, f32[256]{0:T(256)S(1)} %bitcast.180, ...), kind=kOutput, calls=%fused_computation.60.clone.1 | convolution fusion | flops 207355904 | bytes 344064 | tf_op jit(solution)/shard_map/while/body/eval_jaxpr/dot_general | solution.py:62
  99.6 2.9 %convolution_add_fusion.2 = f32[1024,64]{0,1:T(8,128)S(1)} fusion(f32[256,64]{0,1:T(8,128)} %fusion.94, f32[256]{0:T(256)S(1)} %bitcast.169, f32[256]{0:T(256)S(1)} %bitcast.171, f32[256]{0:T(256)S(1)} %bitcast.173, f32[256]{0:T(256)S(1)} %bitcast.175, f32[256]{0:T(256)S(1)} %bitcast.177, f32[256]{0:T(256)S(1)} %bitcast.179, f32[256]{0:T(256)S(1)} %bitcast.181, ...), kind=kOutput, calls=%fused_computation.35.clone.1 | convolution fusion | flops 207486976 | bytes 606209 | tf_op jit(solution)/shard_map/while/body/eval_jaxpr/dot_general | solution.py:65
  103.2 4.3 %fusion.91 = (f32[256]{0:T(256)S(1)}, f32[256]{0:T(256)S(1)}, f32[256]{0:T(256)S(1)}, f32[256]{0:T(256)S(1)}, f32[256]{0:T(256)S(1)}, /*index=5*/f32[256]{0:T(25...) fusion(f32[1024]{0:T(1024)S(1)} %get-tuple-element.397, ...), kind=kOutput, calls=%fused_computation.37.clone.1 | convolution fusion | flops 413134848 | bytes 1995264 | tf_op jit(solution)/shard_map/while/body/eval_jaxpr/dot_general | solution.py:45
  108.8 3.9 %fusion.94 = f32[256,64]{0,1:T(8,128)} fusion(f32[1024,64]{1,0:T(8,128)} %get-tuple-element.398, f32[256]{0:T(256)S(1)} %bitcast.168, f32[256]{0:T(256)S(1)} %bitcast.170, f32[256]{0:T(256)S(1)} %bitcast.172, f32[256]{0:T(256)S(1)} %bitcast.174, f32[256]{0:T(256)S(1)} %bitcast.176, f32[256]{0:T(256)S(1)} %bitcast.178, f32[256]{0:T(256)S(1)} %bitcast.180, ...), kind=kOutput, calls=%fused_computation.60.clone.1 | convolution fusion | flops 207355904 | bytes 344064 | tf_op jit(solution)/shard_map/while/body/eval_jaxpr/dot_general | solution.py:62
  112.7 2.9 %convolution_add_fusion.2 = f32[1024,64]{0,1:T(8,128)S(1)} fusion(f32[256,64]{0,1:T(8,128)} %fusion.94, f32[256]{0:T(256)S(1)} %bitcast.169, f32[256]{0:T(256)S(1)} %bitcast.171, f32[256]{0:T(256)S(1)} %bitcast.173, f32[256]{0:T(256)S(1)} %bitcast.175, f32[256]{0:T(256)S(1)} %bitcast.177, f32[256]{0:T(256)S(1)} %bitcast.179, f32[256]{0:T(256)S(1)} %bitcast.181, ...), kind=kOutput, calls=%fused_computation.35.clone.1 | convolution fusion | flops 207486976 | bytes 606209 | tf_op jit(solution)/shard_map/while/body/eval_jaxpr/dot_general | solution.py:65
  116.4 4.3 %fusion.91 = (f32[256]{0:T(256)S(1)}, f32[256]{0:T(256)S(1)}, f32[256]{0:T(256)S(1)}, f32[256]{0:T(256)S(1)}, f32[256]{0:T(256)S(1)}, /*index=5*/f32[256]{0:T(25...) fusion(f32[1024]{0:T(1024)S(1)} %get-tuple-element.397, ...), kind=kOutput, calls=%fused_computation.37.clone.1 | convolution fusion | flops 413134848 | bytes 1995264 | tf_op jit(solution)/shard_map/while/body/eval_jaxpr/dot_general | solution.py:45
  122.0 3.9 %fusion.94 = f32[256,64]{0,1:T(8,128)} fusion(f32[1024,64]{1,0:T(8,128)} %get-tuple-element.398, f32[256]{0:T(256)S(1)} %bitcast.168, f32[256]{0:T(256)S(1)} %bitcast.170, f32[256]{0:T(256)S(1)} %bitcast.172, f32[256]{0:T(256)S(1)} %bitcast.174, f32[256]{0:T(256)S(1)} %bitcast.176, f32[256]{0:T(256)S(1)} %bitcast.178, f32[256]{0:T(256)S(1)} %bitcast.180, ...), kind=kOutput, calls=%fused_computation.60.clone.1 | convolution fusion | flops 207355904 | bytes 344064 | tf_op jit(solution)/shard_map/while/body/eval_jaxpr/dot_general | solution.py:62
  125.9 2.9 %convolution_add_fusion.2 = f32[1024,64]{0,1:T(8,128)S(1)} fusion(f32[256,64]{0,1:T(8,128)} %fusion.94, f32[256]{0:T(256)S(1)} %bitcast.169, f32[256]{0:T(256)S(1)} %bitcast.171, f32[256]{0:T(256)S(1)} %bitcast.173, f32[256]{0:T(256)S(1)} %bitcast.175, f32[256]{0:T(256)S(1)} %bitcast.177, f32[256]{0:T(256)S(1)} %bitcast.179, f32[256]{0:T(256)S(1)} %bitcast.181, ...), kind=kOutput, calls=%fused_computation.35.clone.1 | convolution fusion | flops 207486976 | bytes 606209 | tf_op jit(solution)/shard_map/while/body/eval_jaxpr/dot_general | solution.py:65
  129.5 4.3 %fusion.91 = (f32[256]{0:T(256)S(1)}, f32[256]{0:T(256)S(1)}, f32[256]{0:T(256)S(1)}, f32[256]{0:T(256)S(1)}, f32[256]{0:T(256)S(1)}, /*index=5*/f32[256]{0:T(25...) fusion(f32[1024]{0:T(1024)S(1)} %get-tuple-element.397, ...), kind=kOutput, calls=%fused_computation.37.clone.1 | convolution fusion | flops 413134848 | bytes 1995264 | tf_op jit(solution)/shard_map/while/body/eval_jaxpr/dot_general | solution.py:45
  135.1 3.9 %fusion.94 = f32[256,64]{0,1:T(8,128)} fusion(f32[1024,64]{1,0:T(8,128)} %get-tuple-element.398, f32[256]{0:T(256)S(1)} %bitcast.168, f32[256]{0:T(256)S(1)} %bitcast.170, f32[256]{0:T(256)S(1)} %bitcast.172, f32[256]{0:T(256)S(1)} %bitcast.174, f32[256]{0:T(256)S(1)} %bitcast.176, f32[256]{0:T(256)S(1)} %bitcast.178, f32[256]{0:T(256)S(1)} %bitcast.180, ...), kind=kOutput, calls=%fused_computation.60.clone.1 | convolution fusion | flops 207355904 | bytes 344064 | tf_op jit(solution)/shard_map/while/body/eval_jaxpr/dot_general | solution.py:62
  139.0 2.9 %convolution_add_fusion.2 = f32[1024,64]{0,1:T(8,128)S(1)} fusion(f32[256,64]{0,1:T(8,128)} %fusion.94, f32[256]{0:T(256)S(1)} %bitcast.169, f32[256]{0:T(256)S(1)} %bitcast.171, f32[256]{0:T(256)S(1)} %bitcast.173, f32[256]{0:T(256)S(1)} %bitcast.175, f32[256]{0:T(256)S(1)} %bitcast.177, f32[256]{0:T(256)S(1)} %bitcast.179, f32[256]{0:T(256)S(1)} %bitcast.181, ...), kind=kOutput, calls=%fused_computation.35.clone.1 | convolution fusion | flops 207486976 | bytes 606209 | tf_op jit(solution)/shard_map/while/body/eval_jaxpr/dot_general | solution.py:65
  142.0 9.3 %all_to_all.15 = f32[8,128,64]{1,2,0:T(8,128)S(1)} all-to-all(f32[8,128,64]{1,2,0:T(8,128)S(1)} %copy_bitcast_fusion), channel_id=1, replica_groups=mesh['samp'=4,'arow'=4,'acol'=2] {'arow','acol'}, dimensions={0} | all-to-all | bytes 524288 | tf_op jit(solution)/shard_map/all_to_all | solution.py:82
  154.7 2.5 %reshape.53 = f32[2048,64]{1,0:T(8,128)} reshape(f32[16,8192]{1,0:T(8,128)} %fusion.64) | data formatting | bytes 1048576 | tf_op jit(solution)/shard_map/reshape | solution.py:98
  157.2 51.4 %all-reduce.4.cloned.1.call-done = f32[2048,64]{1,0:T(8,128)} async-done(((f32[2048,64]{1,0:T(8,128)}), f32[2048,64]{1,0:T(8,128)}) %all-reduce.4.cloned.1.call-update) | async-done | bytes 524304 | tf_op jit(solution)/shard_map/psum | solution.py:98
  208.6 2.3 %copy.39 = f32[2048,64]{0,1:T(8,128)} copy(f32[2048,64]{1,0:T(8,128)} %all-reduce.4.cloned.1.call-done) | data formatting | bytes 1048576 | tf_op jit(solution)/shard_map/psum | solution.py:98
  (79 shorter events, 23.6 us)
Async XLA Ops:
  6.5 23.9 %copy-start = (bf16[2048,768]{1,0:T(8,128)(2,1)S(1)}, bf16[2048,768]{1,0:T(8,128)(2,1)}, u32[]{:S(2)}) copy-start(bf16[2048,768]{1,0:T(8,128)(2,1)} %param.7) | copy-start | bytes 9437188
  8.2 5.4 %copy-start.1 = (u32[32]{0:T(128)S(1)}, u32[32]{0:T(128)}, u32[]{:S(2)}) copy-start(u32[32]{0:T(128)} %constant.129) | copy-start | bytes 388
  27.1 8.8 %all-to-all-start.1 = ((bf16[8,128,64]{1,2,0:T(8,128)(2,1)}), bf16[8,128,64]{1,2,0:T(8,128)(2,1)S(1)}, u32[]{:S(2)}, u32[]{:S(2)}) async-start(bf16[8,128,64]{1,2,0:T(8,128)(2,1)} %gather_fusion.1), calls=%async_computation.1 | async-start | bytes 262144 | tf_op jit(solution)/shard_map/all_to_all | solution.py:30
  35.9 25.3 %all-to-all-start = ((bf16[8,128,768]{2,1,0:T(8,128)(2,1)}), bf16[8,128,768]{2,1,0:T(8,128)(2,1)}, u32[]{:S(2)}, u32[]{:S(2)}) async-start(bf16[8,128,768]{2,1,0:T(8,128)(2,1)} %gather_fusion), calls=%async_computation | async-start | bytes 3145728 | tf_op jit(solution)/shard_map/all_to_all | solution.py:29
  40.2 168.4 %all-reduce.4.cloned.1.call-start = ((), (), s32[]{:S(2)}) async-start(), calls=%async_computation.3 | async-start | bytes 2097152 | tf_op jit(solution)/shard_map/psum | solution.py:98
Sparse Core Ops, SparseCore 0:
  157.3 51.2 all-reduce.3
where the time goes:
time: 220 us; the launch traced here: 218 us
  waiting for transfers between devices  75.1 us (34%)
  matrix products  67.8 us (31%)
  local copies, waits for them, and re-layouts  22.8 us (10%)
  blocking collectives  18.8 us (9%)
  between operations  14.1 us (6%)
  other arithmetic  11.1 us (5%)
  starting transfers between devices  7.7 us (4%)
    psum x1, waiting for transfers between devices, per_device(): return lax.psum(mine.reshape(shard_size, COLS), 'samp')  51.4 us
    dot_general x6, matrix products, one_block(): lax.dot_general(group_rows, flat_anchor, (((1,), (1,)), ((), ())), prefer...  25.7 us
    dot_general x6, matrix products, one_block(): jnp.dot(zmatrix, flat_panel, precision=lax.Precision.HIGHEST, preferred_e...  23.4 us
    all_to_all x1, waiting for transfers between devices, per_device(): lax.all_to_all(anchor_out, ('arow', 'acol'), split_axis=0, concat_axis=0,...  20 us
    dot_general x6, matrix products, one_block(): lax.dot_general(zmatrix, projected, (((0,), (0,)), ((), ())), precision=l...  17.5 us
    unnamed x1, blocking collectives  9.47 us
    all_to_all x1, blocking collectives, per_device(): lax.all_to_all(outgoing.reshape(owners, BA, COLS), ('arow', 'acol'), spli...  9.35 us
    reduce_sum x6, other arithmetic, one_block(): row_scale = lax.rsqrt(jnp.mean(rows_float * rows_float, axis=1) + 1e-06)  6.93 us
  transfers between devices with their start and end apart: 3, of which 3 were waited for; matrix products, arithmetic and copies ran while one was open for 1% of the time, Pallas kernels for 0%

commit v1 on v0

v1 whole, which is shorter than its diff:
```python
import functools
import math

import jax
import jax.numpy as jnp
from jax import lax
from jax.experimental import pallas as pl
from jax.experimental.pallas import tpu as pltpu
from jax.sharding import PartitionSpec as P

BA = 128
EPS = 1e-6
TEMPERATURE = 0.05
LANES = 128
GROUP = 2
HEADER = 8
FULL = 32704.0
STEPS_PER_OCTAVE = 256.0
MIB = 1024 * 1024

VMEM = pl.BlockSpec(memory_space=pltpu.VMEM)
SMEM = pl.BlockSpec(memory_space=pltpu.SMEM)
ANY = pl.BlockSpec(memory_space=pl.ANY)


def divide(x, by):
    if by & (by - 1) == 0:
        return lax.shift_right_logical(x, by.bit_length() - 1), x & (by - 1)
    quotient = lax.div(x, jnp.int32(by))
    return quotient, x - quotient * by


def params(limit_mib, **more):
    return pltpu.CompilerParams(vmem_limit_bytes=limit_mib * MIB, **more)


class Plan:
    def __init__(self, rows, cols):
        self.rows, self.cols = rows, cols
        self.owners = rows * cols
        self.xor = self.owners & (self.owners - 1) == 0

    def me(self):
        return lax.axis_index("arow") * self.cols + lax.axis_index("acol")

    def owner_at(self, me, step):
        return me ^ step if self.xor else lax.rem(me + step, self.owners)

    def asker_at(self, me, step):
        return me ^ step if self.xor else lax.rem(me + self.owners - step, self.owners)

    def step_of(self, me, owner):
        return me ^ owner if self.xor else lax.rem(owner - me + self.owners, self.owners)

    def pairs(self, step):
        n = self.owners
        return [(i, i ^ step if self.xor else (i - step) % n) for i in range(n)]


def prepare_kernel(plan, shard, near_ref, slot_ref, wanted_ref):
    me = plan.me()
    owner, within = divide(near_ref[...], shard)
    block, place = divide(within, BA)
    slot_ref[...] = plan.step_of(me, owner) * BA + place
    for o in range(plan.owners):
        picked = jnp.where(owner == o, block, 0)
        wanted_ref[o : o + 1, :] = jnp.full((1, LANES), jnp.max(picked), jnp.int32)


def gather_kernel(plan, depth_tiles, cols, asked_ref, anchors_ref, panel_ref, *refs):
    out, sem = refs[:-1], refs[-1]
    me = plan.me()
    copies = []
    for step in range(plan.owners):
        block = asked_ref[plan.asker_at(me, step), 0]
        start = pl.multiple_of(block * BA, BA)
        for j in range(depth_tiles):
            copies.append((
                anchors_ref.at[pl.ds(start, BA), pl.ds(j * LANES, LANES)],
                out[step].at[pl.ds(j * BA, BA), :],
            ))
        copies.append((
            panel_ref.at[:, pl.ds(start, BA)],
            out[step].at[pl.ds(depth_tiles * BA, cols), :],
        ))
    copies = [pltpu.make_async_copy(a, b, sem.at[i]) for i, (a, b) in enumerate(copies)]
    for c in copies:
        c.start()
    for c in copies:
        c.wait()


def row_scale_row(rows, depth):
    wide = rows.astype(jnp.float32)
    square = wide * wide
    high = square.astype(jnp.bfloat16)
    low = (square - high.astype(jnp.float32)).astype(jnp.bfloat16)
    ones = jnp.ones((8, depth), jnp.bfloat16)
    dims = (((1,), (1,)), ((), ()))
    total = lax.dot_general(ones, high, dims, preferred_element_type=jnp.float32)
    total += lax.dot_general(ones, low, dims, preferred_element_type=jnp.float32)
    return lax.rsqrt(total / depth + EPS)


def split(x):
    high = x.astype(jnp.bfloat16)
    return high, (x - high.astype(jnp.float32)).astype(jnp.bfloat16)


def group_body(base, depth, cols, cand, tile, messages, rows_ref, slot_ref, scale_ref, first, total_ref, high_ref, low_ref):
    depth_tiles = depth // LANES
    count = len(messages) * BA
    blocks, panels, scales = [], [], []
    for m in messages:
        block = jnp.concatenate([m[j * BA : (j + 1) * BA, :] for j in range(depth_tiles)], axis=1)
        wide = block.astype(jnp.float32)
        mean = jnp.sum(wide * wide, axis=1, keepdims=True) / depth
        scales.append(lax.rsqrt(mean + EPS) * (math.log2(math.e) / TEMPERATURE / depth))
        blocks.append(block)
        panels.append(m[depth_tiles * BA : depth_tiles * BA + cols, :])
    block = jnp.concatenate(blocks, axis=0)
    anchor_scale = jnp.concatenate(scales, axis=0)
    panel = jnp.concatenate(panels, axis=1)
    panel = jnp.concatenate([panel, jnp.ones((cols, count), jnp.bfloat16)], axis=0)
    iota = lax.broadcasted_iota(jnp.int32, (count, tile), 0) + base
    for t in range(rows_ref.shape[0] // tile):
        span = slice(t * tile, (t + 1) * tile)
        rows = rows_ref[span, :]
        if first:
            scale_ref[:, span] = row_scale_row(rows, depth)
        dots = lax.dot_general(
            block, rows, (((1,), (1,)), ((), ())), preferred_element_type=jnp.float32
        )
        hit = iota == slot_ref[0:1, span]
        for k in range(1, cand):
            hit = hit | (iota == slot_ref[k : k + 1, span])
        power = jnp.exp2(dots * anchor_scale * scale_ref[0:1, span])
        high, low = split(jnp.where(hit, power, 0.0))
        high_ref[:, span] = high
        low_ref[:, span] = low
        part = jnp.dot(panel, high, preferred_element_type=jnp.float32)
        part += jnp.dot(panel, low, preferred_element_type=jnp.float32)
        total_ref[:, span] = part if first else total_ref[:, span] + part


def first_kernel(sizes, *refs):
    n = len(refs) - 6
    messages, (rows_ref, slot_ref, scale_ref, total_ref, high_ref, low_ref) = refs[:n], refs[n:]
    group_body(0, *sizes, messages, rows_ref, slot_ref, scale_ref, True, total_ref, high_ref, low_ref)


def next_kernel(base, sizes, *refs):
    n = len(refs) - 7
    messages, (rows_ref, slot_ref, scale_ref, before_ref, total_ref, high_ref, low_ref) = refs[:n], refs[n:]
    total_ref[...] = before_ref[...]
    group_body(base, *sizes, messages, rows_ref, slot_ref, scale_ref, False, total_ref, high_ref, low_ref)


def last_kernel(plan, copies, base, sizes, n_messages, n_before, *refs):
    messages, refs = refs[:n_messages], refs[n_messages:]
    rows_ref, slot_ref, scale_ref, before_ref, wanted_ref = refs[:5]
    parts = refs[5 : 5 + 2 * n_before]
    out_ref, total, high_ref, low_ref = refs[5 + 2 * n_before :]
    cols = sizes[1]
    total[...] = before_ref[...]
    group_body(base, *sizes, messages, rows_ref, slot_ref, scale_ref, False, total, high_ref, low_ref)
    me = plan.me()
    inverse = 1.0 / total[cols : cols + 1, :]
    high, low = split(total[0:cols, :] * inverse * inverse)
    both = jnp.concatenate([high, low], axis=0)
    dims = (((1,), (1,)), ((), ()))
    step = 0
    for weights_high, weights_low in [*zip(parts[0::2], parts[1::2]), (high_ref, low_ref)]:
        main = lax.dot_general(both, weights_high[...], dims, preferred_element_type=jnp.float32)
        rest = lax.dot_general(high, weights_low[...], dims, preferred_element_type=jnp.float32)
        terms = main[:cols, :] + main[cols:, :] + rest
        for b in range(terms.shape[1] // BA):
            block = terms[:, b * BA : (b + 1) * BA]
            owner = plan.owner_at(me, step)
            top = jnp.maximum(jnp.max(jnp.abs(block), axis=0, keepdims=True), 1e-30)
            code = jnp.ceil(jnp.log2(top) * STEPS_PER_OCTAVE)
            value = jnp.round(block * (jnp.exp2(code * (-1.0 / STEPS_PER_OCTAVE)) * FULL))
            index = wanted_ref[pl.ds(owner, 1), :]
            line = lax.broadcasted_iota(jnp.int32, (HEADER, BA), 0)
            header = jnp.where(line == 0, code.astype(jnp.int32), jnp.where(line == 1, index, 0))
            message = jnp.concatenate([value.astype(jnp.int32), header], axis=0).astype(jnp.int16)
            for c in range(copies):
                out_ref[pl.ds(c * plan.owners + owner, 1)] = message[None]
            step += 1


def sum_kernel(cols, messages_ref, out_ref):
    out_ref[...] = jnp.zeros_like(out_ref)

    def add(d, carry):
        message = messages_ref[pl.ds(d, 1)][0].astype(jnp.int32)
        code = message[cols : cols + 1, :].astype(jnp.float32)
        index = jnp.max(message[cols + 1 : cols + 2, :])
        scale = jnp.exp2(code * (1.0 / STEPS_PER_OCTAVE)) * (1.0 / FULL)
        place = pl.ds(pl.multiple_of(index * BA, BA), BA)
        out_ref[:, place] += message[:cols, :].astype(jnp.float32) * scale
        return carry

    lax.fori_loop(0, messages_ref.shape[0], add, 0)


def per_device(embeddings, anchors, subspace, nearest):
    plan = Plan(lax.axis_size("arow"), lax.axis_size("acol"))
    copies = lax.axis_size("samp")
    owners = plan.owners
    shard, depth = anchors.shape
    cols = subspace.shape[1]
    rows, cand = nearest.shape
    depth_tiles = depth // LANES
    f32, bf16, i32 = jnp.float32, jnp.bfloat16, jnp.int32
    struct = jax.ShapeDtypeStruct

    slot, wanted = pl.pallas_call(
        functools.partial(prepare_kernel, plan, shard),
        out_shape=(struct((cand, rows), i32), struct((owners, LANES), i32)),
        in_specs=[VMEM],
        out_specs=(VMEM, VMEM),
        compiler_params=params(4),
        name="prepare",
    )(nearest.T)
    asked = lax.all_to_all(wanted, ("arow", "acol"), 0, 0, tiled=True)

    message = struct((depth_tiles * BA + cols, LANES), bf16)
    sent = pl.pallas_call(
        functools.partial(gather_kernel, plan, depth_tiles, cols),
        out_shape=(message,) * owners,
        in_specs=[SMEM, ANY, ANY],
        out_specs=(ANY,) * owners,
        scratch_shapes=[pltpu.SemaphoreType.DMA((owners * (depth_tiles + 1),))],
        compiler_params=params(4),
        name="gather",
    )(asked, anchors, subspace.T)
    held = [sent[0]] + [
        lax.ppermute(sent[s], ("arow", "acol"), plan.pairs(s)) for s in range(1, owners)
    ]

    tile = math.gcd(rows, 256)
    sizes = (depth, cols, cand, tile)
    size = min(GROUP, owners)
    groups = [list(range(s, min(s + size, owners))) for s in range(0, owners, size)]
    state, parts = None, []
    for g in groups[:-1]:
        n = len(g) * BA
        outs = (struct((2 * cols, rows), f32), struct((n, rows), bf16), struct((n, rows), bf16))
        cost = pl.CostEstimate(flops=2 * n * rows * (depth + 4 * cols), bytes_accessed=rows * depth * 2, transcendentals=n * rows)
        if state is None:
            scale, state, high, low = pl.pallas_call(
                functools.partial(first_kernel, sizes),
                out_shape=(struct((8, rows), f32), *outs),
                in_specs=[VMEM] * (len(g) + 2),
                out_specs=(VMEM,) * 4,
                cost_estimate=cost,
                compiler_params=params(24),
                name="first_group",
            )(*[held[s] for s in g], embeddings, slot)
        else:
            state, high, low = pl.pallas_call(
                functools.partial(next_kernel, g[0] * BA, sizes),
                out_shape=outs,
                in_specs=[VMEM] * (len(g) + 4),
                out_specs=(VMEM,) * 3,
                cost_estimate=cost,
                compiler_params=params(24),
                name="next_group",
            )(*[held[s] for s in g], embeddings, slot, scale, state)
        parts += [high, low]
    g = groups[-1]
    n = len(g) * BA
    terms = pl.pallas_call(
        functools.partial(last_kernel, plan, copies, g[0] * BA, sizes, len(g), len(parts) // 2),
        out_shape=struct((copies * owners, cols + HEADER, BA), jnp.int16),
        in_specs=[VMEM] * (len(g) + 5 + len(parts)),
        out_specs=VMEM,
        scratch_shapes=[pltpu.VMEM((2 * cols, rows), f32), pltpu.VMEM((n, rows), bf16), pltpu.VMEM((n, rows), bf16)],
        compiler_params=params(56),
        name="last_group",
    )(*[held[s] for s in g], embeddings, slot, scale, state, wanted, *parts)
    returned = lax.all_to_all(terms, ("samp", "arow", "acol"), 0, 0, tiled=True)
    result = pl.pallas_call(
        functools.partial(sum_kernel, cols),
        out_shape=struct((cols, shard), f32),
        in_specs=[VMEM],
        out_specs=VMEM,
        compiler_params=params(16),
        name="sum_terms",
    )(returned)
    return result.T


def solution(mesh):
    in_specs = (
        P(("samp", "arow", "acol"), None),
        P(("arow", "acol"), None),
        P(("arow", "acol"), None),
        P(("samp", "arow", "acol"), None),
    )
    return jax.shard_map(
        per_device, mesh=mesh, in_specs=in_specs, out_specs=P(("arow", "acol"), None), check_vma=False
    )
```

time: 220 us -> 82 us (0.37)
  matrix products: 67.8 us -> 0 us
  waiting for transfers between devices: 75.1 us -> 8.21 us
  Pallas kernels: 0 us -> 29.8 us
  between operations: 14.1 us -> 0.14 us
  local copies, waits for them, and re-layouts: 22.8 us -> 9 us
  blocking collectives: 18.8 us -> 30.4 us
  other arithmetic: 11.1 us -> 0 us
  starting transfers between devices: 7.7 us -> 4.19 us
    dot_general x19 -> x0, matrix products: 67.8 us -> none  [the longest x6 25.7 us: one_block(): lax.dot_general(group_rows, flat_anchor, (((1,), (1,)), ((), ())), prefer...]
    psum x1 -> x0, waiting for transfers between devices: 51.4 us -> none  [per_device(): return lax.psum(mine.reshape(shard_size, COLS), 'samp')]
    pallas_call x0 -> x7, Pallas kernels: none -> 29.8 us  [the longest x1 9.15 us: per_device(): pl.pallas_call(functools.partial(last_kernel, plan, copies, g[0] * BA, si...]
    all_to_all x2 -> x0, waiting for transfers between devices: 23.7 us -> none  [the longest x1 20 us: per_device(): lax.all_to_all(anchor_out, ('arow', 'acol'), split_axis=0, concat_axis=0,...]
    all_to_all x1 -> x2, blocking collectives: 9.35 us -> 30.4 us  [the longest x1 20.7 us: per_device(): returned = lax.all_to_all(terms, ('samp', 'arow', 'acol'), 0, 0, tiled=True)]
    unnamed x1 -> x0, blocking collectives: 9.47 us -> none
    reduce_sum x13 -> x0, other arithmetic: 8.88 us -> none  [the longest x6 6.93 us: one_block(): row_scale = lax.rsqrt(jnp.mean(rows_float * rows_float, axis=1) + 1e-06)]
    ppermute x0 -> x7, waiting for transfers between devices: none -> 8.21 us  [per_device(): lax.ppermute(sent[s], ('arow', 'acol'), plan.pairs(s))]
  transfers between devices with their start and end apart: 3 -> 7, of which waited for: 3 -> 2; matrix products, arithmetic and copies ran while one was open for 1% -> 0% of each run, Pallas kernels for 0% -> 14%
where the time goes in v1:
time: 82 us; the launch traced here: 81.7 us
  blocking collectives  30.4 us (37%)
  Pallas kernels  29.8 us (36%)
  local copies, waits for them, and re-layouts  9 us (11%)
  waiting for transfers between devices  8.21 us (10%)
  starting transfers between devices  4.19 us (5%)
    all_to_all x1, blocking collectives, per_device(): returned = lax.all_to_all(terms, ('samp', 'arow', 'acol'), 0, 0, tiled=True)  20.7 us
    all_to_all x1, blocking collectives, per_device(): asked = lax.all_to_all(wanted, ('arow', 'acol'), 0, 0, tiled=True)  9.63 us
    pallas_call x1, Pallas kernels, per_device(): pl.pallas_call(functools.partial(last_kernel, plan, copies, g[0] * BA, si...  9.15 us
    unnamed x32, local copies, waits for them, and re-layouts  9 us
    ppermute x7, waiting for transfers between devices, per_device(): lax.ppermute(sent[s], ('arow', 'acol'), plan.pairs(s))  8.21 us
    pallas_call x1, Pallas kernels, per_device(): pl.pallas_call(functools.partial(sum_kernel, cols), out_shape=struct((col...  7.43 us
    pallas_call x2, Pallas kernels, per_device(): pl.pallas_call(functools.partial(next_kernel, g[0] * BA, sizes), out_shap...  6.08 us
    pallas_call x1, Pallas kernels, per_device(): pl.pallas_call(functools.partial(first_kernel, sizes), out_shape=(struct(...  5.28 us
  transfers between devices with their start and end apart: 7, of which 2 were waited for; matrix products, arithmetic and copies ran while one was open for 0% of the time, Pallas kernels for 14%

profile of v1, /device:TPU:0, one launch (start us, length us, event | category | flops | bytes accessed | tf_op | source)
XLA Modules:
  0.0 81.7 jit_solution(9190994369785139171)
XLA Ops:
  0.0 0.9 %copy-done.12 = s32[1536,8]{0,1:T(8,128)S(1)} copy-done((s32[1536,8]{0,1:T(8,128)S(1)}, s32[1536,8]{0,1:T(8,128)}, u32[]{:S(2)}) %copy-start.12) | copy-done | bytes 49176
  1.0 0.3 prepare.1
  1.2 9.6 %all_to_all.16 = s32[8,1,128]{2,1,0:T(1,128)S(1)} all-to-all(s32[8,1,128]{2,1,0:T(1,128)S(1)} %bitcast.9), channel_id=1, replica_groups=mesh['samp'=4,'arow'=4,'acol'=2] {'arow','acol'}, dimensions={0} | all-to-all | bytes 8192 | tf_op jit(solution)/shard_map/all_to_all | solution.py:226
  10.9 1.9 %copy-done.1 = bf16[2048,768]{1,0:T(8,128)(2,1)S(1)} copy-done((bf16[2048,768]{1,0:T(8,128)(2,1)S(1)}, bf16[2048,768]{1,0:T(8,128)(2,1)}, u32[]{:S(2)}) %copy-start.1) | copy-done | bytes 3145752
  12.8 0.9 %copy-done.11 = bf16[2048,64]{0,1:T(8,128)(2,1)S(1)} copy-done((bf16[2048,64]{0,1:T(8,128)(2,1)S(1)}, bf16[2048,64]{0,1:T(8,128)(2,1)}, u32[]{:S(2)}) %copy-start.11) | copy-done | bytes 262168
  13.7 1.6 %gather.1 = (bf16[832,128]{1,0:T(8,128)(2,1)S(1)}, bf16[832,128]{1,0:T(8,128)(2,1)S(1)}, bf16[832,128]{1,0:T(8,128)(2,1)S(1)}, bf16[832,128]{1,0:T(8,128)(2,1)S(...) custom-call(s32[8,128]{1,0:T(8,128)S(1)} %bitcast.10, ...), custom_call_target="tpu_custom_call" | custom-call | tf_op jit(solution)/shard_map/gather/pallas_call | solution.py:229
  15.3 0.1 collective-permute-start.2
  15.4 0.6 collective-permute-start.5
  16.0 1.2 %collective-permute-start.6 = (bf16[832,128]{1,0:T(8,128)(2,1)S(1)}, bf16[832,128]{1,0:T(8,128)(2,1)S(1)}, u32[]{:S(2)}, u32[]{:S(2)}) collective-permute-start(bf16[832,128]{1,0:T(8,128)(2,1)S(1)} %get-tuple-element.35), channel_id=1, source_target_pairs={{0,3},{1,2},{2,1},{3,0},{4,7},{5,6},{6,5},{7,4},{8,11},{9,10},{10,... | collective-permute-start | bytes 638984 | tf_op jit(solution)/shard_map/ppermute | solution.py:239
  17.2 0.6 collective-permute-start.3
  17.8 1.1 %collective-permute-start.4 = (bf16[832,128]{1,0:T(8,128)(2,1)S(1)}, bf16[832,128]{1,0:T(8,128)(2,1)S(1)}, u32[]{:S(2)}, u32[]{:S(2)}) collective-permute-start(bf16[832,128]{1,0:T(8,128)(2,1)S(1)} %get-tuple-element.33), channel_id=1, source_target_pairs={{0,5},{1,4},{2,7},{3,6},{4,1},{5,0},{6,3},{7,2},{8,13},{9,12},{10,... | collective-permute-start | bytes 638984 | tf_op jit(solution)/shard_map/ppermute | solution.py:239
  18.9 0.0 collective-permute-done.2.refs_1_
  18.9 0.6 collective-permute-start
  19.5 4.0 %collective-permute-done.5.refs_0_ = bf16[832,128]{1,0:T(8,128)(2,1)S(1)} collective-permute-done((bf16[832,128]{1,0:T(8,128)(2,1)S(1)}, bf16[832,128]{1,0:T(8,128)(2,1)S(1)}, u32[]{:S(2)}, u32[]{:S(2)}) %collective-permute-start.5) | collective-permute-done | bytes 213024 | tf_op jit(solution)/shard_map/ppermute | solution.py:239
  23.5 0.0 collective-permute-start.1
  23.5 5.3 %first_group.1 = (f32[8,1536]{1,0:T(8,128)S(1)}, f32[128,1536]{1,0:T(8,128)S(1)}, bf16[256,1536]{1,0:T(8,128)(2,1)S(1)}, bf16[256,1536]{1,0:T(8,128)(2,1)S(1)}) custom-call(bf16[832,128]{1,0:T(8,128)(2,1)S(1)} %get-tuple-element.29.refs_0_, bf16[832,128]{1,0:T(8,128)(2,1)S(1)} %collective-permute-done.2.refs_1_, bf16[1536,768]{1,0:T(8,128)(2,1)S(1)} %copy-done, ...), custom_call_target="tpu_custom_call" | custom-call | flops 805306368 | bytes 2359296 | tf_op jit(solution)/shard_map/first_group/pallas_call | solution.py:252
  28.8 0.9 %copy-done.3 = bf16[256,1536]{1,0:T(8,128)(2,1)} copy-done((bf16[256,1536]{1,0:T(8,128)(2,1)}, bf16[256,1536]{1,0:T(8,128)(2,1)S(1)}, u32[]{:S(2)}) %copy-start.3) | copy-done | bytes 786456
  29.7 0.0 collective-permute-done.6.refs_1_
  29.7 3.0 %next_group.2 = (f32[128,1536]{1,0:T(8,128)S(1)}, bf16[256,1536]{1,0:T(8,128)(2,1)S(1)}, bf16[256,1536]{1,0:T(8,128)(2,1)S(1)}) custom-call(bf16[832,128]{1,0:T(8,128)(2,1)S(1)} %collective-permute-done.5.refs_0_, bf16[832,128]{1,0:T(8,128)(2,1)S(1)} %collective-permute-done.6.refs_1_, bf16[1536,768]{1,0:T(8,128)(2,1)S(1)} %copy-done, ...), custom_call_target="tpu_custom_call" | custom-call | flops 805306368 | bytes 2359296 | tf_op jit(solution)/shard_map/next_group/pallas_call | solution.py:262
  32.8 0.9 %copy-done.5 = bf16[256,1536]{1,0:T(8,128)(2,1)} copy-done((bf16[256,1536]{1,0:T(8,128)(2,1)}, bf16[256,1536]{1,0:T(8,128)(2,1)S(1)}, u32[]{:S(2)}) %copy-start.5) | copy-done | bytes 786456
  33.7 0.0 collective-permute-done.3.refs_0_
  33.7 4.2 %collective-permute-done.4.refs_1_ = bf16[832,128]{1,0:T(8,128)(2,1)S(1)} collective-permute-done((bf16[832,128]{1,0:T(8,128)(2,1)S(1)}, bf16[832,128]{1,0:T(8,128)(2,1)S(1)}, u32[]{:S(2)}, u32[]{:S(2)}) %collective-permute-start.4) | collective-permute-done | bytes 213024 | tf_op jit(solution)/shard_map/ppermute | solution.py:239
  37.9 3.0 %next_group.3 = (f32[128,1536]{1,0:T(8,128)S(1)}, bf16[256,1536]{1,0:T(8,128)(2,1)S(1)}, bf16[256,1536]{1,0:T(8,128)(2,1)S(1)}) custom-call(bf16[832,128]{1,0:T(8,128)(2,1)S(1)} %collective-permute-done.3.refs_0_, bf16[832,128]{1,0:T(8,128)(2,1)S(1)} %collective-permute-done.4.refs_1_, bf16[1536,768]{1,0:T(8,128)(2,1)S(1)} %copy-done, ...), custom_call_target="tpu_custom_call" | custom-call | flops 805306368 | bytes 2359296 | tf_op jit(solution)/shard_map/next_group/pallas_call | solution.py:262
  40.9 0.9 %copy-done.6 = f32[128,1536]{1,0:T(8,128)} copy-done((f32[128,1536]{1,0:T(8,128)}, f32[128,1536]{1,0:T(8,128)S(1)}, u32[]{:S(2)}) %copy-start.6) | copy-done | bytes 786456
  41.8 0.9 %copy-done.7 = bf16[256,1536]{1,0:T(8,128)(2,1)} copy-done((bf16[256,1536]{1,0:T(8,128)(2,1)}, bf16[256,1536]{1,0:T(8,128)(2,1)S(1)}, u32[]{:S(2)}) %copy-start.7) | copy-done | bytes 786456
  42.7 0.9 %copy-done.8 = bf16[256,1536]{1,0:T(8,128)(2,1)} copy-done((bf16[256,1536]{1,0:T(8,128)(2,1)}, bf16[256,1536]{1,0:T(8,128)(2,1)S(1)}, u32[]{:S(2)}) %copy-start.8) | copy-done | bytes 786456
  43.6 0.0 collective-permute-done.refs_0_
  43.6 0.7 copy-done.14
  44.3 0.1 copy-done.15
  44.4 9.2 %last_group.1 = s16[32,72,128]{2,1,0:T(8,128)(2,1)} custom-call(bf16[832,128]{1,0:T(8,128)(2,1)} %copy-done.14, bf16[832,128]{1,0:T(8,128)(2,1)} %copy-done.15, bf16[1536,768]{1,0:T(8,128)(2,1)} %refs_2_.7, s32[8,1536]{1,0:T(8,128)} %copy-done.9, f32[8,1536]{1,0:T(8,128)} %copy-done.10, f32[128,1536]{1,0:T(8,128)} %copy-done.6, s32[8,128]{1,0:T(8,128)} %copy-done.13, ...), custom_call_target="tpu_custom_call" | custom-call | tf_op jit(solution)/shard_map/last_group/pallas_call | solution.py:274
  53.5 20.7 %all_to_all.17.messages_ref = s16[32,72,128]{2,1,0:T(8,128)(2,1)S(1)} all-to-all(s16[32,72,128]{2,1,0:T(8,128)(2,1)} %last_group.1), channel_id=1, replica_groups=mesh['samp'=4,'arow'=4,'acol'=2] {'samp','arow','acol'}, dimensions={0} | all-to-all | bytes 1179648 | tf_op jit(solution)/shard_map/all_to_all | solution.py:283
  74.3 7.4 %sum_terms.1 = f32[64,2048]{1,0:T(8,128)} custom-call(s16[32,72,128]{2,1,0:T(8,128)(2,1)S(1)} %all_to_all.17.messages_ref), custom_call_target="tpu_custom_call" | custom-call | tf_op jit(solution)/shard_map/sum_terms/pallas_call | solution.py:284
  (23 shorter events, 0.0 us)
Async XLA Ops:
  0.0 23.5 %copy-start = (bf16[1536,768]{1,0:T(8,128)(2,1)S(1)}, bf16[1536,768]{1,0:T(8,128)(2,1)}, u32[]{:S(2)}) copy-start(bf16[1536,768]{1,0:T(8,128)(2,1)} %refs_2_.7) | copy-start | bytes 7077892
  0.0 0.9 %copy-start.12 = (s32[1536,8]{0,1:T(8,128)S(1)}, s32[1536,8]{0,1:T(8,128)}, u32[]{:S(2)}) copy-start(s32[1536,8]{0,1:T(8,128)} %param.7) | copy-start | bytes 147460
  1.2 27.6 %copy-start.13 = (s32[8,128]{1,0:T(8,128)}, s32[8,128]{1,0:T(8,128)S(1)}, u32[]{:S(2)}) copy-start(s32[8,128]{1,0:T(8,128)S(1)} %get-tuple-element.25.refs_6_) | copy-start | bytes 12292
  1.2 36.6 %copy-start.9 = (s32[8,1536]{1,0:T(8,128)}, s32[8,1536]{1,0:T(8,128)S(1)}, u32[]{:S(2)}) copy-start(s32[8,1536]{1,0:T(8,128)S(1)} %get-tuple-element.28.refs_3_) | copy-start | bytes 147460
  10.9 1.9 %copy-start.1 = (bf16[2048,768]{1,0:T(8,128)(2,1)S(1)}, bf16[2048,768]{1,0:T(8,128)(2,1)}, u32[]{:S(2)}) copy-start(bf16[2048,768]{1,0:T(8,128)(2,1)} %anchors_ref.1) | copy-start | bytes 9437188
  12.8 0.9 %copy-start.11 = (bf16[2048,64]{0,1:T(8,128)(2,1)S(1)}, bf16[2048,64]{0,1:T(8,128)(2,1)}, u32[]{:S(2)}) copy-start(bf16[2048,64]{0,1:T(8,128)(2,1)} %param.6) | copy-start | bytes 786436
  15.3 3.6 %collective-permute-start.2 = (bf16[832,128]{1,0:T(8,128)(2,1)S(1)}, bf16[832,128]{1,0:T(8,128)(2,1)S(1)}, u32[]{:S(2)}, u32[]{:S(2)}) collective-permute-start(bf16[832,128]{1,0:T(8,128)(2,1)S(1)} %get-tuple-element.30), channel_id=1, source_target_pairs={{0,1},{1,0},{2,3},{3,2},{4,5},{5,4},{6,7},{7,6},{8,9},{9,8},{10,11... | collective-permute-start | bytes 638984 | tf_op jit(solution)/shard_map/ppermute | solution.py:239
  15.4 8.1 %collective-permute-start.5 = (bf16[832,128]{1,0:T(8,128)(2,1)S(1)}, bf16[832,128]{1,0:T(8,128)(2,1)S(1)}, u32[]{:S(2)}, u32[]{:S(2)}) collective-permute-start(bf16[832,128]{1,0:T(8,128)(2,1)S(1)} %get-tuple-element.34), channel_id=1, source_target_pairs={{0,2},{1,3},{2,0},{3,1},{4,6},{5,7},{6,4},{7,5},{8,10},{9,11},{10,... | collective-permute-start | bytes 638984 | tf_op jit(solution)/shard_map/ppermute | solution.py:239
  16.0 13.7 %collective-permute-start.6 = (bf16[832,128]{1,0:T(8,128)(2,1)S(1)}, bf16[832,128]{1,0:T(8,128)(2,1)S(1)}, u32[]{:S(2)}, u32[]{:S(2)}) collective-permute-start(bf16[832,128]{1,0:T(8,128)(2,1)S(1)} %get-tuple-element.35), channel_id=1, source_target_pairs={{0,3},{1,2},{2,1},{3,0},{4,7},{5,6},{6,5},{7,4},{8,11},{9,10},{10,... | collective-permute-start | bytes 638984 | tf_op jit(solution)/shard_map/ppermute | solution.py:239
  17.2 16.4 %collective-permute-start.3 = (bf16[832,128]{1,0:T(8,128)(2,1)S(1)}, bf16[832,128]{1,0:T(8,128)(2,1)S(1)}, u32[]{:S(2)}, u32[]{:S(2)}) collective-permute-start(bf16[832,128]{1,0:T(8,128)(2,1)S(1)} %get-tuple-element.32), channel_id=1, source_target_pairs={{0,4},{1,5},{2,6},{3,7},{4,0},{5,1},{6,2},{7,3},{8,12},{9,13},{10,... | collective-permute-start | bytes 638984 | tf_op jit(solution)/shard_map/ppermute | solution.py:239
  17.8 20.1 %collective-permute-start.4 = (bf16[832,128]{1,0:T(8,128)(2,1)S(1)}, bf16[832,128]{1,0:T(8,128)(2,1)S(1)}, u32[]{:S(2)}, u32[]{:S(2)}) collective-permute-start(bf16[832,128]{1,0:T(8,128)(2,1)S(1)} %get-tuple-element.33), channel_id=1, source_target_pairs={{0,5},{1,4},{2,7},{3,6},{4,1},{5,0},{6,3},{7,2},{8,13},{9,12},{10,... | collective-permute-start | bytes 638984 | tf_op jit(solution)/shard_map/ppermute | solution.py:239
  18.9 24.7 %collective-permute-start = (bf16[832,128]{1,0:T(8,128)(2,1)S(1)}, bf16[832,128]{1,0:T(8,128)(2,1)S(1)}, u32[]{:S(2)}, u32[]{:S(2)}) collective-permute-start(bf16[832,128]{1,0:T(8,128)(2,1)S(1)} %get-tuple-element.26), channel_id=1, source_target_pairs={{0,6},{1,7},{2,4},{3,5},{4,2},{5,3},{6,0},{7,1},{8,14},{9,15},{10,... | collective-permute-start | bytes 638984 | tf_op jit(solution)/shard_map/ppermute | solution.py:239
  23.5 20.1 %collective-permute-start.1 = (bf16[832,128]{1,0:T(8,128)(2,1)S(1)}, bf16[832,128]{1,0:T(8,128)(2,1)S(1)}, u32[]{:S(2)}, u32[]{:S(2)}) collective-permute-start(bf16[832,128]{1,0:T(8,128)(2,1)S(1)} %get-tuple-element.27), channel_id=1, source_target_pairs={{0,7},{1,6},{2,5},{3,4},{4,3},{5,2},{6,1},{7,0},{8,15},{9,14},{10,... | collective-permute-start | bytes 638984 | tf_op jit(solution)/shard_map/ppermute | solution.py:239
  28.8 0.9 %copy-start.3 = (bf16[256,1536]{1,0:T(8,128)(2,1)}, bf16[256,1536]{1,0:T(8,128)(2,1)S(1)}, u32[]{:S(2)}) copy-start(bf16[256,1536]{1,0:T(8,128)(2,1)S(1)} %get-tuple-element.40.refs_8_) | copy-start | bytes 2359300
  29.7 11.2 %copy-start.2 = (bf16[256,1536]{1,0:T(8,128)(2,1)}, bf16[256,1536]{1,0:T(8,128)(2,1)S(1)}, u32[]{:S(2)}) copy-start(bf16[256,1536]{1,0:T(8,128)(2,1)S(1)} %get-tuple-element.39.refs_7_) | copy-start | bytes 2359300
  29.7 11.2 %copy-start.10 = (f32[8,1536]{1,0:T(8,128)}, f32[8,1536]{1,0:T(8,128)S(1)}, u32[]{:S(2)}) copy-start(f32[8,1536]{1,0:T(8,128)S(1)} %get-tuple-element.31.refs_4_) | copy-start | bytes 147460
  32.8 0.9 %copy-start.5 = (bf16[256,1536]{1,0:T(8,128)(2,1)}, bf16[256,1536]{1,0:T(8,128)(2,1)S(1)}, u32[]{:S(2)}) copy-start(bf16[256,1536]{1,0:T(8,128)(2,1)S(1)} %get-tuple-element.42.refs_10_) | copy-start | bytes 2359300
  33.7 10.0 %copy-start.4 = (bf16[256,1536]{1,0:T(8,128)(2,1)}, bf16[256,1536]{1,0:T(8,128)(2,1)S(1)}, u32[]{:S(2)}) copy-start(bf16[256,1536]{1,0:T(8,128)(2,1)S(1)} %get-tuple-element.41.refs_9_) | copy-start | bytes 2359300
  40.9 0.9 %copy-start.6 = (f32[128,1536]{1,0:T(8,128)}, f32[128,1536]{1,0:T(8,128)S(1)}, u32[]{:S(2)}) copy-start(f32[128,1536]{1,0:T(8,128)S(1)} %get-tuple-element.38.refs_5_) | copy-start | bytes 2359300
  41.8 0.9 %copy-start.7 = (bf16[256,1536]{1,0:T(8,128)(2,1)}, bf16[256,1536]{1,0:T(8,128)(2,1)S(1)}, u32[]{:S(2)}) copy-start(bf16[256,1536]{1,0:T(8,128)(2,1)S(1)} %get-tuple-element.43.refs_11_) | copy-start | bytes 2359300
  42.7 0.9 %copy-start.8 = (bf16[256,1536]{1,0:T(8,128)(2,1)}, bf16[256,1536]{1,0:T(8,128)(2,1)S(1)}, u32[]{:S(2)}) copy-start(bf16[256,1536]{1,0:T(8,128)(2,1)S(1)} %get-tuple-element.44.refs_12_) | copy-start | bytes 2359300
  43.6 0.7 copy-start.14
  43.6 0.7 copy-start.15

commit v2 on v1

v2 whole, which is shorter than its diff:
```python
import functools
import math

import jax
import jax.numpy as jnp
from jax import lax
from jax.experimental import pallas as pl
from jax.experimental.pallas import tpu as pltpu
from jax.sharding import PartitionSpec as P

BA = 128
EPS = 1e-6
TEMPERATURE = 0.05
LANES = 128
MISS = -1e30
IN_FLIGHT = 5
HEADER = 8
FULL = 32704.0
STEPS_PER_OCTAVE = 256.0
MIB = 1024 * 1024

VMEM = pl.BlockSpec(memory_space=pltpu.VMEM)
SMEM = pl.BlockSpec(memory_space=pltpu.SMEM)
ANY = pl.BlockSpec(memory_space=pl.ANY)
HBM = pl.BlockSpec(memory_space=pltpu.HBM)
QUICK = pl.CostEstimate(flops=1, bytes_accessed=1, transcendentals=0)


def divide(x, by):
    if by & (by - 1) == 0:
        return lax.shift_right_logical(x, by.bit_length() - 1), x & (by - 1)
    quotient = lax.div(x, jnp.int32(by))
    return quotient, x - quotient * by


def params(limit_mib, **more):
    return pltpu.CompilerParams(vmem_limit_bytes=int(limit_mib * MIB), **more)


class Plan:
    def __init__(self, rows, cols):
        self.rows, self.cols = rows, cols
        self.owners = rows * cols
        self.xor = self.owners & (self.owners - 1) == 0

    def me(self):
        return lax.axis_index("arow") * self.cols + lax.axis_index("acol")

    def owner_at(self, me, step):
        return me ^ step if self.xor else lax.rem(me + step, self.owners)

    def asker_at(self, me, step):
        return me ^ step if self.xor else lax.rem(me + self.owners - step, self.owners)

    def step_of(self, me, owner):
        return me ^ owner if self.xor else lax.rem(owner - me + self.owners, self.owners)

    def order(self):
        if self.owners == 8 and self.xor:
            return [(2, 0), (4, 0), (3, 0), (5, 0), (6, 0), (7, 2), (1, 4)]
        return [(s, max(s - IN_FLIGHT, 0)) for s in range(1, self.owners)]

    def sent(self):
        return [*(s for s, _ in self.order()), 0]

    def groups(self):
        if self.owners == 8 and self.xor:
            return [[0, 2], [3, 4], [1, 5], [6], [7]]
        order = list(range(1, self.owners))
        return [[0], *(order[i : min(i + 2, len(order) - 1)] for i in range(0, len(order) - 1, 2)), order[-1:]]

    def pairs(self, step):
        n = self.owners
        return [(i, i ^ step if self.xor else (i - step) % n) for i in range(n)]


def prepare_kernel(plan, shard, near_ref, slot_ref, wanted_ref):
    me = plan.me()
    owner, within = divide(near_ref[...], shard)
    block, place = divide(within, BA)
    slot_ref[...] = plan.step_of(me, owner) * BA + place
    for o in range(plan.owners):
        picked = jnp.where(owner == o, block, 0)
        wanted_ref[o : o + 1, :] = jnp.full((1, LANES), jnp.max(picked), jnp.int32)


def gather_kernel(plan, depth_tiles, cols, asked_ref, anchors_ref, panel_ref, *refs):
    out, blocks, sem = refs[:-2], refs[-2], refs[-1]
    me = plan.me()
    starts, copies, panels = {}, {}, {}
    for step in plan.sent():
        block = jnp.max(asked_ref[pl.ds(plan.asker_at(me, step), 1), :])
        starts[step] = pl.multiple_of(block * BA, BA)
        copies[step] = pltpu.make_async_copy(
            anchors_ref.at[pl.ds(starts[step], BA), :], blocks.at[step], sem.at[step]
        )
        copies[step].start()
    for step in plan.sent():
        panels[step] = pltpu.make_async_copy(
            panel_ref.at[:, pl.ds(starts[step], BA)],
            out[step].at[pl.ds(depth_tiles * BA, cols), :],
            sem.at[plan.owners + step],
        )
        panels[step].start()
    for step in plan.sent():
        copies[step].wait()
        for j in range(depth_tiles):
            out[step][j * BA : (j + 1) * BA, :] = blocks[step, :, j * LANES : (j + 1) * LANES]
    for step in plan.sent():
        panels[step].wait()


def split(x):
    high = x.astype(jnp.bfloat16)
    return high, (x - high.astype(jnp.float32)).astype(jnp.bfloat16)


def rows_kernel(rows_ref, slot_ref, turned_ref, scale_ref, bias_ref):
    rows, depth = rows_ref.shape
    tile = math.gcd(rows, 256)
    for t in range(rows // tile):
        span = slice(t * tile, (t + 1) * tile)
        turned = jnp.transpose(rows_ref[span, :])
        turned_ref[:, span] = turned
        wide = turned.astype(jnp.float32)
        mean = jnp.sum(wide * wide, axis=0, keepdims=True) / depth
        scale_ref[:, span] = jnp.broadcast_to(lax.rsqrt(mean + EPS), (8, tile))
    step, place = divide(slot_ref[...], BA)
    iota = lax.broadcasted_iota(jnp.int32, (BA, rows), 0).astype(jnp.bfloat16)
    for s in range(bias_ref.shape[0] // BA):
        key = jnp.where(step == s, place, -1).astype(jnp.bfloat16)
        bias = jnp.full(iota.shape, MISS, jnp.bfloat16)
        for k in range(slot_ref.shape[0]):
            bias = jnp.where(iota == key[k : k + 1, :], jnp.bfloat16(0), bias)
        bias_ref[s * BA : (s + 1) * BA, :] = bias


def group_body(steps, depth, cols, tile, messages, rows_ref, bias_ref, scale_ref, before, total_ref, high_ref, low_ref):
    depth_tiles = depth // LANES
    count = len(messages) * BA
    blocks, panels, scales = [], [], []
    for m in messages:
        block = jnp.concatenate([m[j * BA : (j + 1) * BA, :] for j in range(depth_tiles)], axis=1)
        wide = block.astype(jnp.float32)
        mean = jnp.sum(wide * wide, axis=1, keepdims=True) / depth
        scales.append(lax.rsqrt(mean + EPS) * (math.log2(math.e) / TEMPERATURE / depth))
        blocks.append(block)
        panels.append(m[depth_tiles * BA : depth_tiles * BA + cols, :])
    block = jnp.concatenate(blocks, axis=0)
    anchor_scale = jnp.concatenate(scales, axis=0)
    panel = jnp.concatenate(panels, axis=1)
    panel = jnp.concatenate([panel, jnp.ones((cols, count), jnp.bfloat16)], axis=0)
    for t in range(rows_ref.shape[1] // tile):
        span = slice(t * tile, (t + 1) * tile)
        dots = jnp.dot(block, rows_ref[:, span], preferred_element_type=jnp.float32)
        bias = jnp.concatenate([bias_ref[s * BA : (s + 1) * BA, span] for s in steps], axis=0)
        high, low = split(jnp.exp2(dots * anchor_scale * scale_ref[0:1, span] + bias.astype(jnp.float32)))
        high_ref[:, span] = high
        low_ref[:, span] = low
    for t in range(rows_ref.shape[1] // tile):
        span = slice(t * tile, (t + 1) * tile)
        part = jnp.dot(panel, high_ref[:, span], preferred_element_type=jnp.float32)
        part += jnp.dot(panel, low_ref[:, span], preferred_element_type=jnp.float32)
        total_ref[:, span] = part if before is None else before[:, span] + part


def group_kernel(steps, sizes, *refs):
    messages, refs = refs[: len(steps)], refs[len(steps) :]
    rows_ref, bias_ref, scale_ref = refs[:3]
    before = refs[3] if len(refs) == 7 else None
    group_body(steps, *sizes, messages, rows_ref, bias_ref, scale_ref, before, *refs[-3:])


def last_kernel(plan, copies, groups, sizes, *refs):
    steps = groups[-1]
    messages, refs = refs[: len(steps)], refs[len(steps) :]
    rows_ref, bias_ref, scale_ref, before, wanted_ref = refs[:5]
    parts = [*refs[5:-5], *refs[-3:-1]]
    out_ref, total, high_ref, low_ref, terms = refs[-5:]
    cols = sizes[1]
    group_body(steps, *sizes, messages, rows_ref, bias_ref, scale_ref, before, total, high_ref, low_ref)
    me = plan.me()
    inverse = 1.0 / total[cols : cols + 1, :]
    high, low = split(total[0:cols, :] * inverse * inverse)
    both = jnp.concatenate([high, low], axis=0)
    dims = (((1,), (1,)), ((), ()))
    at = 0
    for g, weights_high, weights_low in zip(groups, parts[0::2], parts[1::2], strict=True):
        span = slice(at, at + len(g) * BA)
        main = lax.dot_general(both, weights_high[...], dims, preferred_element_type=jnp.float32)
        rest = lax.dot_general(high, weights_low[...], dims, preferred_element_type=jnp.float32)
        terms[0 : 2 * cols, span] = main
        terms[2 * cols :, span] = rest
        at += len(g) * BA
    at = 0
    for g in groups:
        for step in g:
            span = slice(at, at + BA)
            at += BA
            block = terms[0:cols, span] + terms[cols : 2 * cols, span] + terms[2 * cols :, span]
            owner = plan.owner_at(me, step)
            top = jnp.maximum(jnp.max(jnp.abs(block), axis=0, keepdims=True), 1e-30)
            code = jnp.ceil(jnp.log2(top) * STEPS_PER_OCTAVE)
            value = jnp.round(block * (jnp.exp2(code * (-1.0 / STEPS_PER_OCTAVE)) * FULL))
            index = wanted_ref[pl.ds(owner, 1), :]
            line = lax.broadcasted_iota(jnp.int32, (HEADER, BA), 0)
            header = jnp.where(line == 0, code.astype(jnp.int32), jnp.where(line == 1, index, 0))
            message = jnp.concatenate([value.astype(jnp.int32), header], axis=0).astype(jnp.int16)
            for c in range(copies):
                out_ref[pl.ds(c * plan.owners + owner, 1)] = message[None]


def sum_kernel(cols, messages_ref, out_ref):
    out_ref[...] = jnp.zeros_like(out_ref)
    count = messages_ref.shape[0]
    batch = math.gcd(count, 32)

    def add(i, carry):
        headers = [messages_ref[i * batch + d, cols : cols + HEADER, :].astype(jnp.int32) for d in range(batch)]
        places = [pl.multiple_of(jnp.max(h[1:2, :]) * BA, BA) for h in headers]
        for d in range(batch):
            code = headers[d][0:1, :].astype(jnp.float32)
            scale = jnp.exp2(code * (1.0 / STEPS_PER_OCTAVE)) * (1.0 / FULL)
            values = messages_ref[i * batch + d, 0:cols, :].astype(jnp.int32).astype(jnp.float32)
            out_ref[:, pl.ds(places[d], BA)] += values * scale
        return carry

    lax.fori_loop(0, count // batch, add, 0, unroll=count == batch)


def per_device(embeddings, anchors, subspace, nearest):
    plan = Plan(lax.axis_size("arow"), lax.axis_size("acol"))
    copies = lax.axis_size("samp")
    owners = plan.owners
    shard, depth = anchors.shape
    cols = subspace.shape[1]
    rows, cand = nearest.shape
    depth_tiles = depth // LANES
    f32, bf16, i32 = jnp.float32, jnp.bfloat16, jnp.int32
    struct = jax.ShapeDtypeStruct

    panel = subspace.T
    slot, wanted = pl.pallas_call(
        functools.partial(prepare_kernel, plan, shard),
        out_shape=(struct((cand, rows), i32), struct((owners, LANES), i32)),
        in_specs=[VMEM],
        out_specs=(VMEM, VMEM),
        compiler_params=params(4),
        name="prepare",
    )(nearest.T)
    asked = lax.all_to_all(wanted, ("arow", "acol"), 0, 0, tiled=True)

    tile = math.gcd(rows, 256)
    message = struct((depth_tiles * BA + cols, LANES), bf16)
    sent = pl.pallas_call(
        functools.partial(gather_kernel, plan, depth_tiles, cols),
        out_shape=(message,) * owners,
        in_specs=[VMEM, HBM, HBM],
        out_specs=(VMEM,) * owners,
        scratch_shapes=[pltpu.VMEM((owners, BA, depth), bf16), pltpu.SemaphoreType.DMA((2 * owners,))],
        compiler_params=params(52.125),
        name="gather",
    )(asked, anchors, panel)
    slot, *sent = lax.optimization_barrier((slot, *sent))
    turned, scale, bias = pl.pallas_call(
        rows_kernel,
        out_shape=(struct((depth, rows), bf16), struct((8, rows), f32), struct((owners * BA, rows), bf16)),
        in_specs=[VMEM, VMEM],
        out_specs=(VMEM,) * 3,
        cost_estimate=QUICK,
        compiler_params=params(16),
        name="rows",
        )(embeddings, slot)

    sizes = (depth, cols, tile)

    def weigh(g, state):
        n = len(g) * BA
        return pl.pallas_call(
            functools.partial(group_kernel, g, sizes),
            out_shape=(struct((2 * cols, rows), f32), struct((n, rows), bf16), struct((n, rows), bf16)),
            in_specs=[VMEM] * (len(g) + 3 + len(state)),
            out_specs=(VMEM,) * 3,
            cost_estimate=QUICK,
            compiler_params=params(10),
            name="weights",
        )(*[held[s] for s in g], turned, bias, scale, *state)

    groups = plan.groups()
    held, total, parts = {0: sent[0]}, None, []
    for s, after in plan.order():
        block = sent[s]
        if after:
            block, *_ = lax.optimization_barrier((block, held[after]))
        held[s] = lax.ppermute(block, ("arow", "acol"), plan.pairs(s))
    for g in groups[:-1]:
        total, high, low = weigh(g, [] if total is None else [total])
        parts += [high, low]
    g = groups[-1]
    n = len(g) * BA
    small = owners * BA * rows * 4 <= 8 * MIB
    terms = pl.pallas_call(
        functools.partial(last_kernel, plan, copies, groups, sizes),
        out_shape=struct((copies * owners, cols + HEADER, BA), jnp.int16),
        in_specs=[VMEM] * (len(g) + 5 + len(parts)),
        out_specs=VMEM,
        cost_estimate=QUICK,
        scratch_shapes=[pltpu.VMEM((2 * cols, rows), f32), pltpu.VMEM((n, rows), bf16), pltpu.VMEM((n, rows), bf16), pltpu.VMEM((3 * cols, owners * BA), f32)],
        compiler_params=params(14 if small else 60),
        name="terms",
    )(*[held[s] for s in g], turned, bias, scale, total, wanted, *parts)
    returned = lax.all_to_all(terms, ("samp", "arow", "acol"), 0, 0, tiled=True)
    result = pl.pallas_call(
        functools.partial(sum_kernel, cols),
        out_shape=struct((cols, shard), f32),
        in_specs=[VMEM],
        out_specs=VMEM,
        compiler_params=params(16),
        name="sum_terms",
    )(returned)
    return result.T


def solution(mesh):
    in_specs = (
        P(("samp", "arow", "acol"), None),
        P(("arow", "acol"), None),
        P(("arow", "acol"), None),
        P(("samp", "arow", "acol"), None),
    )
    return jax.shard_map(
        per_device, mesh=mesh, in_specs=in_specs, out_specs=P(("arow", "acol"), None), check_vma=False
    )
```

time: 82 us -> 59.4 us (0.72)
  Pallas kernels: 29.8 us -> 13.3 us
  local copies, waits for them, and re-layouts: 9 us -> 0.95 us
  blocking collectives: 30.4 us -> 31.7 us
    pallas_call x4 -> x6, Pallas kernels: 20.5 us -> 9.94 us  [the longest x4 4.52 us: weigh(): pl.pallas_call(functools.partial(group_kernel, g, sizes), out_shape=(stru...]
    unnamed x32 -> x4, local copies, waits for them, and re-layouts: 9 us -> 0.95 us
    pallas_call x1, Pallas kernels: 7.43 us -> 1.25 us  [per_device(): pl.pallas_call(functools.partial(sum_kernel, cols), out_shape=struct((col...]
    all_to_all x1, blocking collectives: 20.7 us -> 22 us  [per_device(): returned = lax.all_to_all(terms, ('samp', 'arow', 'acol'), 0, 0, tiled=True)]
  transfers between devices with their start and end apart: 7 -> 7, of which waited for: 2 -> 4; matrix products, arithmetic and copies ran while one was open for 0% -> 0% of each run, Pallas kernels for 14% -> 12%
where the time goes in v2:
time: 59.4 us; the launch traced here: 59.2 us
  blocking collectives  31.7 us (53%)
  Pallas kernels  13.3 us (22%)
  waiting for transfers between devices  8.73 us (15%)
  starting transfers between devices  4.43 us (7%)
  local copies, waits for them, and re-layouts  0.95 us (2%)
    all_to_all x1, blocking collectives, per_device(): returned = lax.all_to_all(terms, ('samp', 'arow', 'acol'), 0, 0, tiled=True)  22 us
    all_to_all x1, blocking collectives, per_device(): asked = lax.all_to_all(wanted, ('arow', 'acol'), 0, 0, tiled=True)  9.63 us
    ppermute x7, waiting for transfers between devices, per_device(): held[s] = lax.ppermute(block, ('arow', 'acol'), plan.pairs(s))  8.73 us
    pallas_call x4, Pallas kernels, weigh(): pl.pallas_call(functools.partial(group_kernel, g, sizes), out_shape=(stru...  4.52 us
    ppermute x7, starting transfers between devices, per_device(): held[s] = lax.ppermute(block, ('arow', 'acol'), plan.pairs(s))  4.43 us
    pallas_call x1, Pallas kernels, per_device(): pl.pallas_call(functools.partial(last_kernel, plan, copies, groups, sizes...  2.71 us
    pallas_call x1, Pallas kernels, per_device(): pl.pallas_call(rows_kernel, out_shape=(struct((depth, rows), bf16), struc...  2.71 us
    pallas_call x1, Pallas kernels, per_device(): pl.pallas_call(functools.partial(gather_kernel, plan, depth_tiles, cols),...  1.85 us
  transfers between devices with their start and end apart: 7, of which 4 were waited for; matrix products, arithmetic and copies ran while one was open for 0% of the time, Pallas kernels for 12%

profile of v2, /device:TPU:0, one launch (start us, length us, event | category | flops | bytes accessed | tf_op | source)
XLA Modules:
  0.0 59.2 jit_solution(16574307294566036366)
XLA Ops:
  0.0 0.0 copy-start
  0.0 0.0 copy-start.1
  0.0 0.9 %copy-done.1 = s32[1536,8]{0,1:T(8,128)S(1)} copy-done((s32[1536,8]{0,1:T(8,128)S(1)}, s32[1536,8]{0,1:T(8,128)}, u32[]{:S(2)}) %copy-start.1) | copy-done | bytes 49176
  1.0 0.3 prepare.1
  1.2 9.6 %all_to_all.16 = s32[8,1,128]{2,1,0:T(1,128)S(1)} all-to-all(s32[8,1,128]{2,1,0:T(1,128)S(1)} %bitcast.8), channel_id=1, replica_groups=mesh['samp'=4,'arow'=4,'acol'=2] {'arow','acol'}, dimensions={0} | all-to-all | bytes 8192 | tf_op jit(solution)/shard_map/all_to_all | solution.py:251
  10.9 1.8 %gather.1 = (bf16[832,128]{1,0:T(8,128)(2,1)S(1)}, bf16[832,128]{1,0:T(8,128)(2,1)S(1)}, bf16[832,128]{1,0:T(8,128)(2,1)S(1)}, bf16[832,128]{1,0:T(8,128)(2,1)S(...) custom-call(s32[8,128]{1,0:T(8,128)S(1)} %bitcast.9, ...), custom_call_target="tpu_custom_call" | custom-call | tf_op jit(solution)/shard_map/gather/pallas_call | solution.py:255
  12.7 0.7 %collective-permute-start.3 = (bf16[832,128]{1,0:T(8,128)(2,1)S(1)}, bf16[832,128]{1,0:T(8,128)(2,1)S(1)}, u32[]{:S(2)}, u32[]{:S(2)}) collective-permute-start(bf16[832,128]{1,0:T(8,128)(2,1)S(1)} %get-tuple-element.60), channel_id=1, source_target_pairs={{0,4},{1,5},{2,6},{3,7},{4,0},{5,1},{6,2},{7,3},{8,12},{9,13},{10,... | collective-permute-start | bytes 638984 | tf_op jit(solution)/shard_map/ppermute | solution.py:295
  13.4 0.5 collective-permute-start
  13.9 2.4 %collective-permute-start.2 = (bf16[832,128]{1,0:T(8,128)(2,1)S(1)}, bf16[832,128]{1,0:T(8,128)(2,1)S(1)}, u32[]{:S(2)}, u32[]{:S(2)}) collective-permute-start(bf16[832,128]{1,0:T(8,128)(2,1)S(1)} %get-tuple-element.58), channel_id=1, source_target_pairs={{0,6},{1,7},{2,4},{3,5},{4,2},{5,3},{6,0},{7,1},{8,14},{9,15},{10,... | collective-permute-start | bytes 638984 | tf_op jit(solution)/shard_map/ppermute | solution.py:295
  16.3 0.0 collective-permute-start.5
  16.3 0.8 %collective-permute-start.6 = (bf16[832,128]{1,0:T(8,128)(2,1)S(1)}, bf16[832,128]{1,0:T(8,128)(2,1)S(1)}, u32[]{:S(2)}, u32[]{:S(2)}) collective-permute-start(bf16[832,128]{1,0:T(8,128)(2,1)S(1)} %get-tuple-element.63), channel_id=1, source_target_pairs={{0,3},{1,2},{2,1},{3,0},{4,7},{5,6},{6,5},{7,4},{8,11},{9,10},{10,... | collective-permute-start | bytes 638984 | tf_op jit(solution)/shard_map/ppermute | solution.py:295
  17.1 3.8 %collective-permute-done.3.refs_1_ = bf16[832,128]{1,0:T(8,128)(2,1)S(1)} collective-permute-done((bf16[832,128]{1,0:T(8,128)(2,1)S(1)}, bf16[832,128]{1,0:T(8,128)(2,1)S(1)}, u32[]{:S(2)}, u32[]{:S(2)}) %collective-permute-start.3) | collective-permute-done | bytes 213024 | tf_op jit(solution)/shard_map/ppermute | solution.py:295
  20.9 0.0 collective-permute-start.4
  20.9 0.6 %collective-permute-done.refs_1_ = bf16[832,128]{1,0:T(8,128)(2,1)S(1)} collective-permute-done((bf16[832,128]{1,0:T(8,128)(2,1)S(1)}, bf16[832,128]{1,0:T(8,128)(2,1)S(1)}, u32[]{:S(2)}, u32[]{:S(2)}) %collective-permute-start) | collective-permute-done | bytes 213024 | tf_op jit(solution)/shard_map/ppermute | solution.py:295
  21.6 0.0 collective-permute-start.1
  21.6 0.0 copy-done
  21.6 2.7 %rows.1 = (bf16[768,1536]{1,0:T(8,128)(2,1)S(1)}, f32[8,1536]{1,0:T(8,128)S(1)}, bf16[1024,1536]{1,0:T(8,128)(2,1)S(1)}) custom-call(bf16[1536,768]{1,0:T(8,128)(2,1)S(1)} %copy-done, s32[8,1536]{1,0:T(8,128)S(1)} %get-tuple-element.54.slot_ref), custom_call_target="tpu_custom_call" | custom-call | flops 1 | bytes 1 | tf_op jit(solution)/shard_map/rows/pallas_call | solution.py:265
  24.3 1.2 %weights.4 = (f32[128,1536]{1,0:T(8,128)S(1)}, bf16[256,1536]{1,0:T(8,128)(2,1)S(1)}, bf16[256,1536]{1,0:T(8,128)(2,1)S(1)}) custom-call(bf16[832,128]{1,0:T(8,128)(2,1)S(1)} %get-tuple-element.64.refs_0_, bf16[832,128]{1,0:T(8,128)(2,1)S(1)} %collective-permute-done.refs_1_, bf16[768,1536]{1,0:T(8,128)(2,1)S(1)} %get-tuple-element.55.refs_2_.refs_1_, ...), custom_call_target="tpu_custom_call" | custom-call | flops 1 | bytes 1 | tf_op jit(solution)/shard_map/weights/pallas_call | solution.py:279
  25.5 3.2 %collective-permute-done.6.refs_0_ = bf16[832,128]{1,0:T(8,128)(2,1)S(1)} collective-permute-done((bf16[832,128]{1,0:T(8,128)(2,1)S(1)}, bf16[832,128]{1,0:T(8,128)(2,1)S(1)}, u32[]{:S(2)}, u32[]{:S(2)}) %collective-permute-start.6) | collective-permute-done | bytes 213024 | tf_op jit(solution)/shard_map/ppermute | solution.py:295
  28.8 1.2 %weights.5 = (f32[128,1536]{1,0:T(8,128)S(1)}, bf16[256,1536]{1,0:T(8,128)(2,1)S(1)}, bf16[256,1536]{1,0:T(8,128)(2,1)S(1)}) custom-call(bf16[832,128]{1,0:T(8,128)(2,1)S(1)} %collective-permute-done.6.refs_0_, bf16[832,128]{1,0:T(8,128)(2,1)S(1)} %collective-permute-done.3.refs_1_, bf16[768,1536]{1,0:T(8,128)(2,1)S(1)} %get-tuple-element.55.refs_2_.refs_1_, ...), custom_call_target="tpu_custom_call" | custom-call | flops 1 | bytes 1 | tf_op jit(solution)/shard_map/weights/pallas_call | solution.py:279
  30.0 0.0 collective-permute-done.5.refs_1_
  30.0 0.0 collective-permute-done.4.refs_0_
  30.1 1.2 %weights.6 = (f32[128,1536]{1,0:T(8,128)S(1)}, bf16[256,1536]{1,0:T(8,128)(2,1)S(1)}, bf16[256,1536]{1,0:T(8,128)(2,1)S(1)}) custom-call(bf16[832,128]{1,0:T(8,128)(2,1)S(1)} %collective-permute-done.4.refs_0_, bf16[832,128]{1,0:T(8,128)(2,1)S(1)} %collective-permute-done.5.refs_1_, bf16[768,1536]{1,0:T(8,128)(2,1)S(1)} %get-tuple-element.55.refs_2_.refs_1_, ...), custom_call_target="tpu_custom_call" | custom-call | flops 1 | bytes 1 | tf_op jit(solution)/shard_map/weights/pallas_call | solution.py:279
  31.3 0.0 collective-permute-done.2.refs_0_
  31.3 0.8 %weights.7 = (f32[128,1536]{1,0:T(8,128)S(1)}, bf16[128,1536]{1,0:T(8,128)(2,1)S(1)}, bf16[128,1536]{1,0:T(8,128)(2,1)S(1)}) custom-call(bf16[832,128]{1,0:T(8,128)(2,1)S(1)} %collective-permute-done.2.refs_0_, bf16[768,1536]{1,0:T(8,128)(2,1)S(1)} %get-tuple-element.55.refs_2_.refs_1_, bf16[1024,1536]{1,0:T(8,128)(2,1)S(1)} %get-tuple-element.56.refs_3_.refs_2_, ...), custom_call_target="tpu_custom_call" | custom-call | flops 1 | bytes 1 | tf_op jit(solution)/shard_map/weights/pallas_call | solution.py:279
  32.1 1.0 %collective-permute-done.1.refs_0_ = bf16[832,128]{1,0:T(8,128)(2,1)S(1)} collective-permute-done((bf16[832,128]{1,0:T(8,128)(2,1)S(1)}, bf16[832,128]{1,0:T(8,128)(2,1)S(1)}, u32[]{:S(2)}, u32[]{:S(2)}) %collective-permute-start.1) | collective-permute-done | bytes 213024 | tf_op jit(solution)/shard_map/ppermute | solution.py:295
  33.2 2.7 %terms.1 = s16[32,72,128]{2,1,0:T(8,128)(2,1)S(1)} custom-call(bf16[832,128]{1,0:T(8,128)(2,1)S(1)} %collective-permute-done.1.refs_0_, bf16[768,1536]{1,0:T(8,128)(2,1)S(1)} %get-tuple-element.55.refs_2_.refs_1_, bf16[1024,1536]{1,0:T(8,128)(2,1)S(1)} %get-tuple-element.56.refs_3_.refs_2_, f32[8,1536]{1,0:T(8,128)S(1)} %get-tuple-element.57.refs_4_.refs_3_, ...), custom_call_target="tpu_custom_call" | custom-call | flops 1 | bytes 1 | tf_op jit(solution)/shard_map/terms/pallas_call | solution.py:302
  35.9 22.0 %all_to_all.17.messages_ref = s16[32,72,128]{2,1,0:T(8,128)(2,1)S(1)} all-to-all(s16[32,72,128]{2,1,0:T(8,128)(2,1)S(1)} %terms.1), channel_id=1, replica_groups=mesh['samp'=4,'arow'=4,'acol'=2] {'samp','arow','acol'}, dimensions={0} | all-to-all | bytes 1179648 | tf_op jit(solution)/shard_map/all_to_all | solution.py:312
  57.9 1.2 %sum_terms.1 = f32[64,2048]{1,0:T(8,128)} custom-call(s16[32,72,128]{2,1,0:T(8,128)(2,1)S(1)} %all_to_all.17.messages_ref), custom_call_target="tpu_custom_call" | custom-call | tf_op jit(solution)/shard_map/sum_terms/pallas_call | solution.py:313
Async XLA Ops:
  0.0 21.6 %copy-start = (bf16[1536,768]{1,0:T(8,128)(2,1)S(1)}, bf16[1536,768]{1,0:T(8,128)(2,1)}, u32[]{:S(2)}) copy-start(bf16[1536,768]{1,0:T(8,128)(2,1)} %rows_ref.1) | copy-start | bytes 7077892
  0.0 0.9 %copy-start.1 = (s32[1536,8]{0,1:T(8,128)S(1)}, s32[1536,8]{0,1:T(8,128)}, u32[]{:S(2)}) copy-start(s32[1536,8]{0,1:T(8,128)} %param.7) | copy-start | bytes 147460
  12.7 8.2 %collective-permute-start.3 = (bf16[832,128]{1,0:T(8,128)(2,1)S(1)}, bf16[832,128]{1,0:T(8,128)(2,1)S(1)}, u32[]{:S(2)}, u32[]{:S(2)}) collective-permute-start(bf16[832,128]{1,0:T(8,128)(2,1)S(1)} %get-tuple-element.60), channel_id=1, source_target_pairs={{0,4},{1,5},{2,6},{3,7},{4,0},{5,1},{6,2},{7,3},{8,12},{9,13},{10,... | collective-permute-start | bytes 638984 | tf_op jit(solution)/shard_map/ppermute | solution.py:295
  13.4 8.2 %collective-permute-start = (bf16[832,128]{1,0:T(8,128)(2,1)S(1)}, bf16[832,128]{1,0:T(8,128)(2,1)S(1)}, u32[]{:S(2)}, u32[]{:S(2)}) collective-permute-start(bf16[832,128]{1,0:T(8,128)(2,1)S(1)} %get-tuple-element.52), channel_id=1, source_target_pairs={{0,2},{1,3},{2,0},{3,1},{4,6},{5,7},{6,4},{7,5},{8,10},{9,11},{10,... | collective-permute-start | bytes 638984 | tf_op jit(solution)/shard_map/ppermute | solution.py:295
  13.9 17.4 %collective-permute-start.2 = (bf16[832,128]{1,0:T(8,128)(2,1)S(1)}, bf16[832,128]{1,0:T(8,128)(2,1)S(1)}, u32[]{:S(2)}, u32[]{:S(2)}) collective-permute-start(bf16[832,128]{1,0:T(8,128)(2,1)S(1)} %get-tuple-element.58), channel_id=1, source_target_pairs={{0,6},{1,7},{2,4},{3,5},{4,2},{5,3},{6,0},{7,1},{8,14},{9,15},{10,... | collective-permute-start | bytes 638984 | tf_op jit(solution)/shard_map/ppermute | solution.py:295
  16.3 13.8 %collective-permute-start.5 = (bf16[832,128]{1,0:T(8,128)(2,1)S(1)}, bf16[832,128]{1,0:T(8,128)(2,1)S(1)}, u32[]{:S(2)}, u32[]{:S(2)}) collective-permute-start(bf16[832,128]{1,0:T(8,128)(2,1)S(1)} %get-tuple-element.62), channel_id=1, source_target_pairs={{0,5},{1,4},{2,7},{3,6},{4,1},{5,0},{6,3},{7,2},{8,13},{9,12},{10,... | collective-permute-start | bytes 638984 | tf_op jit(solution)/shard_map/ppermute | solution.py:295
  16.3 12.5 %collective-permute-start.6 = (bf16[832,128]{1,0:T(8,128)(2,1)S(1)}, bf16[832,128]{1,0:T(8,128)(2,1)S(1)}, u32[]{:S(2)}, u32[]{:S(2)}) collective-permute-start(bf16[832,128]{1,0:T(8,128)(2,1)S(1)} %get-tuple-element.63), channel_id=1, source_target_pairs={{0,3},{1,2},{2,1},{3,0},{4,7},{5,6},{6,5},{7,4},{8,11},{9,10},{10,... | collective-permute-start | bytes 638984 | tf_op jit(solution)/shard_map/ppermute | solution.py:295
  20.9 9.1 %collective-permute-start.4 = (bf16[832,128]{1,0:T(8,128)(2,1)S(1)}, bf16[832,128]{1,0:T(8,128)(2,1)S(1)}, u32[]{:S(2)}, u32[]{:S(2)}) collective-permute-start(bf16[832,128]{1,0:T(8,128)(2,1)S(1)} %get-tuple-element.61), channel_id=1, source_target_pairs={{0,1},{1,0},{2,3},{3,2},{4,5},{5,4},{6,7},{7,6},{8,9},{9,8},{10,11... | collective-permute-start | bytes 638984 | tf_op jit(solution)/shard_map/ppermute | solution.py:295
  21.6 11.6 %collective-permute-start.1 = (bf16[832,128]{1,0:T(8,128)(2,1)S(1)}, bf16[832,128]{1,0:T(8,128)(2,1)S(1)}, u32[]{:S(2)}, u32[]{:S(2)}) collective-permute-start(bf16[832,128]{1,0:T(8,128)(2,1)S(1)} %get-tuple-element.53), channel_id=1, source_target_pairs={{0,7},{1,6},{2,5},{3,4},{4,3},{5,2},{6,1},{7,0},{8,15},{9,14},{10,... | collective-permute-start | bytes 638984 | tf_op jit(solution)/shard_map/ppermute | solution.py:295

commit v3 on v2

--- a/solution.py
+++ b/solution.py
@@ -13,8 +13,10 @@
 TEMPERATURE = 0.05
 LANES = 128
 MISS = -1e30
+ORDER = [(2, 0), (4, 0), (6, 0), (3, 0), (5, 0), (7, 2), (1, 4)]
+GROUPS = [[0, 2], [1, 4], [5], [3, 6], [7]]
+LIMIT_EVEN, LIMIT_ODD = 52.9, 52.1
 IN_FLIGHT = 5
-HEADER = 8
 FULL = 32704.0
 STEPS_PER_OCTAVE = 256.0
 MIB = 1024 * 1024
@@ -39,75 +41,83 @@
 
 class Plan:
     def __init__(self, rows, cols):
-        self.rows, self.cols = rows, cols
+        self.cols = cols
         self.owners = rows * cols
-        self.xor = self.owners & (self.owners - 1) == 0
+        assert self.owners & (self.owners - 1) == 0 and cols % 2 == 0
 
     def me(self):
         return lax.axis_index("arow") * self.cols + lax.axis_index("acol")
 
-    def owner_at(self, me, step):
-        return me ^ step if self.xor else lax.rem(me + step, self.owners)
-
-    def asker_at(self, me, step):
-        return me ^ step if self.xor else lax.rem(me + self.owners - step, self.owners)
-
-    def step_of(self, me, owner):
-        return me ^ owner if self.xor else lax.rem(owner - me + self.owners, self.owners)
+    def even(self):
+        return list(range(0, self.owners, 2))
+
+    def odd(self):
+        return list(range(1, self.owners, 2))
 
     def order(self):
-        if self.owners == 8 and self.xor:
-            return [(2, 0), (4, 0), (3, 0), (5, 0), (6, 0), (7, 2), (1, 4)]
-        return [(s, max(s - IN_FLIGHT, 0)) for s in range(1, self.owners)]
-
-    def sent(self):
-        return [*(s for s, _ in self.order()), 0]
+        if self.owners == 8:
+            return ORDER
+        steps = [*self.even()[1:], *self.odd()]
+        return [(s, steps[i - IN_FLIGHT] if i >= IN_FLIGHT else 0) for i, s in enumerate(steps)]
 
     def groups(self):
-        if self.owners == 8 and self.xor:
-            return [[0, 2], [3, 4], [1, 5], [6], [7]]
-        order = list(range(1, self.owners))
+        if self.owners == 8:
+            return GROUPS
+        order = [s for s, _ in self.order()]
         return [[0], *(order[i : min(i + 2, len(order) - 1)] for i in range(0, len(order) - 1, 2)), order[-1:]]
 
     def pairs(self, step):
-        n = self.owners
-        return [(i, i ^ step if self.xor else (i - step) % n) for i in range(n)]
+        return [(i, i ^ step) for i in range(self.owners)]
 
 
 def prepare_kernel(plan, shard, near_ref, slot_ref, wanted_ref):
     me = plan.me()
     owner, within = divide(near_ref[...], shard)
     block, place = divide(within, BA)
-    slot_ref[...] = plan.step_of(me, owner) * BA + place
+    slot_ref[...] = (me ^ owner) * BA + place
     for o in range(plan.owners):
         picked = jnp.where(owner == o, block, 0)
         wanted_ref[o : o + 1, :] = jnp.full((1, LANES), jnp.max(picked), jnp.int32)
 
 
-def gather_kernel(plan, depth_tiles, cols, asked_ref, anchors_ref, panel_ref, *refs):
-    out, blocks, sem = refs[:-2], refs[-2], refs[-1]
+def cut(starts, depth_tiles, cols, anchors_ref, panel_ref, out, blocks, sem):
+    copies, panels = [], []
+    for i, start in enumerate(starts):
+        copies.append(pltpu.make_async_copy(anchors_ref.at[pl.ds(start, BA), :], blocks.at[i], sem.at[i]))
+        copies[i].start()
+    for i, start in enumerate(starts):
+        panels.append(pltpu.make_async_copy(
+            panel_ref.at[:, pl.ds(start, BA)], out[i].at[pl.ds(depth_tiles * BA, cols), :], sem.at[len(starts) + i]
+        ))
+        panels[i].start()
+    for i, copy in enumerate(copies):
+        copy.wait()
+        for j in range(depth_tiles):
+            out[i][j * BA : (j + 1) * BA, :] = blocks[i, :, j * LANES : (j + 1) * LANES]
+    for panel in panels:
+        panel.wait()
+
+
+def block_start(line):
+    return pl.multiple_of(jnp.max(line) * BA, BA)
+
+
+def even_kernel(plan, depth_tiles, cols, *refs):
+    n = len(plan.even())
+    asked, (anchors_ref, panel_ref), out = refs[:n], refs[n : n + 2], refs[n + 2 : 2 * n + 2]
+    passed_ref, blocks, sem = refs[2 * n + 2 :]
     me = plan.me()
-    starts, copies, panels = {}, {}, {}
-    for step in plan.sent():
-        block = jnp.max(asked_ref[pl.ds(plan.asker_at(me, step), 1), :])
-        starts[step] = pl.multiple_of(block * BA, BA)
-        copies[step] = pltpu.make_async_copy(
-            anchors_ref.at[pl.ds(starts[step], BA), :], blocks.at[step], sem.at[step]
-        )
-        copies[step].start()
-    for step in plan.sent():
-        panels[step] = pltpu.make_async_copy(
-            panel_ref.at[:, pl.ds(starts[step], BA)],
-            out[step].at[pl.ds(depth_tiles * BA, cols), :],
-            sem.at[plan.owners + step],
-        )
-        panels[step].start()
-    for step in plan.sent():
-        copies[step].wait()
-        for j in range(depth_tiles):
-            out[step][j * BA : (j + 1) * BA, :] = blocks[step, :, j * LANES : (j + 1) * LANES]
-    for step in plan.sent():
-        panels[step].wait()
+    starts = [block_start(a[pl.ds(me, 1), :]) for a in asked]
+    passed_ref[...] = jnp.zeros_like(passed_ref)
+    for i, a in enumerate(asked):
+        passed_ref[i : i + 1, :] = a[pl.ds(me ^ 1, 1), :]
+    cut(starts, depth_tiles, cols, anchors_ref, panel_ref, out, blocks, sem)
+
+
+def odd_kernel(plan, depth_tiles, cols, passed_ref, anchors_ref, panel_ref, *refs):
+    n = len(plan.odd())
+    starts = [block_start(passed_ref[i : i + 1, :]) for i in range(n)]
+    cut(starts, depth_tiles, cols, anchors_ref, panel_ref, refs[:n], *refs[n:])
 
 
 def split(x):
@@ -184,45 +194,45 @@
     high, low = split(total[0:cols, :] * inverse * inverse)
     both = jnp.concatenate([high, low], axis=0)
     dims = (((1,), (1,)), ((), ()))
-    at = 0
     for g, weights_high, weights_low in zip(groups, parts[0::2], parts[1::2], strict=True):
-        span = slice(at, at + len(g) * BA)
         main = lax.dot_general(both, weights_high[...], dims, preferred_element_type=jnp.float32)
         rest = lax.dot_general(high, weights_low[...], dims, preferred_element_type=jnp.float32)
-        terms[0 : 2 * cols, span] = main
-        terms[2 * cols :, span] = rest
-        at += len(g) * BA
-    at = 0
-    for g in groups:
-        for step in g:
-            span = slice(at, at + BA)
-            at += BA
-            block = terms[0:cols, span] + terms[cols : 2 * cols, span] + terms[2 * cols :, span]
-            owner = plan.owner_at(me, step)
-            top = jnp.maximum(jnp.max(jnp.abs(block), axis=0, keepdims=True), 1e-30)
-            code = jnp.ceil(jnp.log2(top) * STEPS_PER_OCTAVE)
-            value = jnp.round(block * (jnp.exp2(code * (-1.0 / STEPS_PER_OCTAVE)) * FULL))
-            index = wanted_ref[pl.ds(owner, 1), :]
-            line = lax.broadcasted_iota(jnp.int32, (HEADER, BA), 0)
-            header = jnp.where(line == 0, code.astype(jnp.int32), jnp.where(line == 1, index, 0))
-            message = jnp.concatenate([value.astype(jnp.int32), header], axis=0).astype(jnp.int16)
-            for c in range(copies):
-                out_ref[pl.ds(c * plan.owners + owner, 1)] = message[None]
+        for b, step in enumerate(g):
+            span, to = slice(b * BA, (b + 1) * BA), slice(step * BA, (step + 1) * BA)
+            terms[:, to] = main[:cols, span] + main[cols:, span] + rest[:, span]
+    size = cols // 2 + 1
+    for owner in range(plan.owners):
+        block = terms[:, pl.ds(pl.multiple_of((me ^ owner) * BA, BA), BA)]
+        top = jnp.maximum(jnp.max(jnp.abs(block), axis=0, keepdims=True), 1e-30)
+        code = jnp.ceil(jnp.log2(top) * STEPS_PER_OCTAVE)
+        value = jnp.round(block * (jnp.exp2(code * (-1.0 / STEPS_PER_OCTAVE)) * FULL)).astype(jnp.int32)
+        pairs = jnp.left_shift(value[: cols // 2, :], 16) | (value[cols // 2 :, :] & 0xFFFF)
+        header = jnp.left_shift(code.astype(jnp.int32), 16) | wanted_ref[owner : owner + 1, :]
+        message = jnp.concatenate([pairs, header], axis=0)
+        for c in range(copies):
+            at = (c * plan.owners + owner) * size
+            out_ref[at : at + size, :] = message
 
 
 def sum_kernel(cols, messages_ref, out_ref):
     out_ref[...] = jnp.zeros_like(out_ref)
-    count = messages_ref.shape[0]
+    half = cols // 2
+    size = half + 1
+    count = messages_ref.shape[0] // size
     batch = math.gcd(count, 32)
 
     def add(i, carry):
-        headers = [messages_ref[i * batch + d, cols : cols + HEADER, :].astype(jnp.int32) for d in range(batch)]
-        places = [pl.multiple_of(jnp.max(h[1:2, :]) * BA, BA) for h in headers]
+        part = messages_ref.at[pl.ds(pl.multiple_of(i * batch * size, 8), batch * size), :]
+        headers = [part[d * size + half : (d + 1) * size, :] for d in range(batch)]
+        places = [pl.multiple_of(jnp.max(h & 0xFFFF) * BA, BA) for h in headers]
         for d in range(batch):
-            code = headers[d][0:1, :].astype(jnp.float32)
+            code = jnp.right_shift(headers[d], 16).astype(jnp.float32)
             scale = jnp.exp2(code * (1.0 / STEPS_PER_OCTAVE)) * (1.0 / FULL)
-            values = messages_ref[i * batch + d, 0:cols, :].astype(jnp.int32).astype(jnp.float32)
-            out_ref[:, pl.ds(places[d], BA)] += values * scale
+            pairs = part[d * size : d * size + half, :]
+            first = jnp.right_shift(pairs, 16).astype(jnp.float32)
+            second = jnp.right_shift(jnp.left_shift(pairs, 16), 16).astype(jnp.float32)
+            out_ref[:half, pl.ds(places[d], BA)] += first * scale
+            out_ref[half:, pl.ds(places[d], BA)] += second * scale
         return carry
 
     lax.fori_loop(0, count // batch, add, 0, unroll=count == batch)
@@ -248,20 +258,38 @@
         compiler_params=params(4),
         name="prepare",
     )(nearest.T)
-    asked = lax.all_to_all(wanted, ("arow", "acol"), 0, 0, tiled=True)
-
+    here = ("arow", "acol")
     tile = math.gcd(rows, 256)
+
     message = struct((depth_tiles * BA + cols, LANES), bf16)
-    sent = pl.pallas_call(
-        functools.partial(gather_kernel, plan, depth_tiles, cols),
-        out_shape=(message,) * owners,
+    even, odd = plan.even(), plan.odd()
+    half = len(even)
+    scratch = [pltpu.VMEM((half, BA, depth), bf16), pltpu.SemaphoreType.DMA((2 * half,))]
+    passed = struct((-(-half // 8) * 8, LANES), i32)
+    asked = [wanted, *(lax.ppermute(wanted, here, plan.pairs(s)) for s in even[1:])]
+    *sent_even, passed = pl.pallas_call(
+        functools.partial(even_kernel, plan, depth_tiles, cols),
+        out_shape=(*(message,) * half, passed),
+        in_specs=[*[VMEM] * half, HBM, HBM],
+        out_specs=(VMEM,) * (half + 1),
+        scratch_shapes=scratch,
+        cost_estimate=QUICK,
+        compiler_params=params(LIMIT_EVEN),
+        name="cut_even",
+    )(*asked, anchors, panel)
+    passed = lax.ppermute(passed, here, plan.pairs(1))
+    sent_odd = pl.pallas_call(
+        functools.partial(odd_kernel, plan, depth_tiles, cols),
+        out_shape=(message,) * half,
         in_specs=[VMEM, HBM, HBM],
-        out_specs=(VMEM,) * owners,
-        scratch_shapes=[pltpu.VMEM((owners, BA, depth), bf16), pltpu.SemaphoreType.DMA((2 * owners,))],
-        compiler_params=params(52.125),
-        name="gather",
-    )(asked, anchors, panel)
-    slot, *sent = lax.optimization_barrier((slot, *sent))
+        out_specs=(VMEM,) * half,
+        scratch_shapes=scratch,
+        cost_estimate=QUICK,
+        compiler_params=params(LIMIT_ODD),
+        name="cut_odd",
+    )(passed, anchors, panel)
+    slot, *sent_odd = lax.optimization_barrier((slot, *sent_odd))
+    sent = {**dict(zip(even, sent_even)), **dict(zip(odd, sent_odd))}
     turned, scale, bias = pl.pallas_call(
         rows_kernel,
         out_shape=(struct((depth, rows), bf16), struct((8, rows), f32), struct((owners * BA, rows), bf16)),
@@ -292,7 +320,7 @@
         block = sent[s]
         if after:
             block, *_ = lax.optimization_barrier((block, held[after]))
-        held[s] = lax.ppermute(block, ("arow", "acol"), plan.pairs(s))
+        held[s] = lax.ppermute(block, here, plan.pairs(s))
     for g in groups[:-1]:
         total, high, low = weigh(g, [] if total is None else [total])
         parts += [high, low]
@@ -301,15 +329,15 @@
     small = owners * BA * rows * 4 <= 8 * MIB
     terms = pl.pallas_call(
         functools.partial(last_kernel, plan, copies, groups, sizes),
-        out_shape=struct((copies * owners, cols + HEADER, BA), jnp.int16),
+        out_shape=struct((copies * owners * (cols // 2 + 1), BA), i32),
         in_specs=[VMEM] * (len(g) + 5 + len(parts)),
         out_specs=VMEM,
         cost_estimate=QUICK,
-        scratch_shapes=[pltpu.VMEM((2 * cols, rows), f32), pltpu.VMEM((n, rows), bf16), pltpu.VMEM((n, rows), bf16), pltpu.VMEM((3 * cols, owners * BA), f32)],
+        scratch_shapes=[pltpu.VMEM((2 * cols, rows), f32), pltpu.VMEM((n, rows), bf16), pltpu.VMEM((n, rows), bf16), pltpu.VMEM((cols, owners * BA), f32)],
         compiler_params=params(14 if small else 60),
         name="terms",
     )(*[held[s] for s in g], turned, bias, scale, total, wanted, *parts)
-    returned = lax.all_to_all(terms, ("samp", "arow", "acol"), 0, 0, tiled=True)
+    returned = lax.all_to_all(terms[:, None, :], ("samp", "arow", "acol"), 0, 0, tiled=True)[:, 0, :]
     result = pl.pallas_call(
         functools.partial(sum_kernel, cols),
         out_shape=struct((cols, shard), f32),

time: 59.4 us -> 56.1 us (0.944)
  blocking collectives: 31.7 us -> 20.9 us
  starting transfers between devices: 4.43 us -> 11.2 us
  Pallas kernels: 13.3 us -> 14.7 us
    all_to_all x2 -> x1, blocking collectives: 31.7 us -> 20.9 us  [per_device(): lax.all_to_all(terms[:, None, :], ('samp', 'arow', 'acol'), 0, 0, tiled=T...]
    ppermute x7 -> x11, starting transfers between devices: 4.43 us -> 11.2 us  [the longest x7 6.55 us: per_device(): held[s] = lax.ppermute(block, here, plan.pairs(s))]
    pallas_call x1 -> x2, Pallas kernels: 1.85 us -> 3.18 us  [the longest x1 1.65 us: per_device(): pl.pallas_call(functools.partial(even_kernel, plan, depth_tiles, cols), o...]
    ppermute x7 -> x11, waiting for transfers between devices: 8.73 us -> 8.31 us  [the longest x7 4.84 us: per_device(): held[s] = lax.ppermute(block, here, plan.pairs(s))]
  transfers between devices with their start and end apart: 7 -> 11, of which waited for: 4 -> 7; matrix products, arithmetic and copies ran while one was open for 0% -> 0% of each run, Pallas kernels for 12% -> 16%
where the time goes in v3:
time: 56.1 us; the launch traced here: 56 us
  blocking collectives  20.9 us (37%)
  Pallas kernels  14.7 us (26%)
  starting transfers between devices  11.2 us (20%)
  waiting for transfers between devices  8.31 us (15%)
  local copies, waits for them, and re-layouts  0.85 us (2%)
    all_to_all x1, blocking collectives, per_device(): lax.all_to_all(terms[:, None, :], ('samp', 'arow', 'acol'), 0, 0, tiled=T...  20.9 us
    ppermute x7, starting transfers between devices, per_device(): held[s] = lax.ppermute(block, here, plan.pairs(s))  6.55 us
    ppermute x7, waiting for transfers between devices, per_device(): held[s] = lax.ppermute(block, here, plan.pairs(s))  4.84 us
    ppermute x3, starting transfers between devices, per_device(): lax.ppermute(wanted, here, plan.pairs(s))  4.6 us
    pallas_call x4, Pallas kernels, weigh(): pl.pallas_call(functools.partial(group_kernel, g, sizes), out_shape=(stru...  4.51 us
    ppermute x3, waiting for transfers between devices, per_device(): lax.ppermute(wanted, here, plan.pairs(s))  3.47 us
    pallas_call x1, Pallas kernels, per_device(): pl.pallas_call(functools.partial(last_kernel, plan, copies, groups, sizes...  2.72 us
    pallas_call x1, Pallas kernels, per_device(): pl.pallas_call(rows_kernel, out_shape=(struct((depth, rows), bf16), struc...  2.71 us
  transfers between devices with their start and end apart: 11, of which 7 were waited for; matrix products, arithmetic and copies ran while one was open for 0% of the time, Pallas kernels for 16%

profile of v3, /device:TPU:0, one launch (start us, length us, event | category | flops | bytes accessed | tf_op | source)
XLA Modules:
  0.0 56.0 jit_solution(2492107088181978013)
XLA Ops:
  0.0 0.8 %copy-done.2 = s32[1536,8]{0,1:T(8,128)S(1)} copy-done((s32[1536,8]{0,1:T(8,128)S(1)}, s32[1536,8]{0,1:T(8,128)}, u32[]{:S(2)}) %copy-start.2) | copy-done | bytes 49176
  0.8 0.3 prepare.1
  1.1 4.0 %collective-permute-start.2 = (s32[8,128]{1,0:T(8,128)S(1)}, s32[8,128]{1,0:T(8,128)S(1)}, u32[]{:S(2)}, u32[]{:S(2)}) collective-permute-start(s32[8,128]{1,0:T(8,128)S(1)} %get-tuple-element.39.refs_0_.refs_5_), channel_id=1, source_target_pairs={{0,6},{1,7},{2,4},{3,5},{4,2},{5,3},{6,0},{7,1},{8,14},{9,15},{10,... | collective-permute-start | bytes 12296 | tf_op jit(solution)/shard_map/ppermute | solution.py:269
  5.1 0.5 collective-permute-start.1
  5.6 0.1 collective-permute-start
  5.7 0.9 %collective-permute-done.2.refs_3_ = s32[8,128]{1,0:T(8,128)S(1)} collective-permute-done((s32[8,128]{1,0:T(8,128)S(1)}, s32[8,128]{1,0:T(8,128)S(1)}, u32[]{:S(2)}, u32[]{:S(2)}) %collective-permute-start.2) | collective-permute-done | bytes 4128 | tf_op jit(solution)/shard_map/ppermute | solution.py:269
  6.7 2.0 %collective-permute-done.1.refs_2_ = s32[8,128]{1,0:T(8,128)S(1)} collective-permute-done((s32[8,128]{1,0:T(8,128)S(1)}, s32[8,128]{1,0:T(8,128)S(1)}, u32[]{:S(2)}, u32[]{:S(2)}) %collective-permute-start.1) | collective-permute-done | bytes 4128 | tf_op jit(solution)/shard_map/ppermute | solution.py:269
  8.7 0.5 collective-permute-done.refs_1_
  9.2 1.6 %cut_even.1 = (bf16[832,128]{1,0:T(8,128)(2,1)S(1)}, bf16[832,128]{1,0:T(8,128)(2,1)S(1)}, bf16[832,128]{1,0:T(8,128)(2,1)S(1)}, bf16[832,128]{1,0:T(8,128)(2,1)S(1)}, s32[8,128]{1,0:T(8,128)S(1)}) custom-call(s32[8,128]{1,0:T(8,128)S(1)} %get-tuple-element.39.refs_0_.refs_5_, s32[8,128]{1,0:T(8,128)S(1)} %collective-permute-done.refs_1_, ...), custom_call_target="tpu_custom_call" | custom-call | flops 1 | bytes 1 | tf_op jit(solution)/shard_map/cut_even/pallas_call | solution.py:270
  10.9 1.6 %collective-permute-start.9 = (bf16[832,128]{1,0:T(8,128)(2,1)S(1)}, bf16[832,128]{1,0:T(8,128)(2,1)S(1)}, u32[]{:S(2)}, u32[]{:S(2)}) collective-permute-start(bf16[832,128]{1,0:T(8,128)(2,1)S(1)} %get-tuple-element.56), channel_id=1, source_target_pairs={{0,4},{1,5},{2,6},{3,7},{4,0},{5,1},{6,2},{7,3},{8,12},{9,13},{10,... | collective-permute-start | bytes 638984 | tf_op jit(solution)/shard_map/ppermute | solution.py:323
  12.4 0.5 collective-permute-start.4
  13.0 0.0 collective-permute-start.3
  13.0 1.4 %collective-permute-start.7 = (bf16[832,128]{1,0:T(8,128)(2,1)S(1)}, bf16[832,128]{1,0:T(8,128)(2,1)S(1)}, u32[]{:S(2)}, u32[]{:S(2)}) collective-permute-start(bf16[832,128]{1,0:T(8,128)(2,1)S(1)} %get-tuple-element.53), channel_id=1, source_target_pairs={{0,6},{1,7},{2,4},{3,5},{4,2},{5,3},{6,0},{7,1},{8,14},{9,15},{10,... | collective-permute-start | bytes 638984 | tf_op jit(solution)/shard_map/ppermute | solution.py:323
  14.4 1.5 %cut_odd.1 = (bf16[832,128]{1,0:T(8,128)(2,1)S(1)}, bf16[832,128]{1,0:T(8,128)(2,1)S(1)}, bf16[832,128]{1,0:T(8,128)(2,1)S(1)}, bf16[832,128]{1,0:T(8,128)(2,1)S(1)}) custom-call(s32[8,128]{1,0:T(8,128)S(1)} %collective-permute-done.3.passed_ref, bf16[2048,768]{1,0:T(8,128)(2,1)} %anchors_ref.1, bf16[64,2048]{1,0:T(8,128)(2,1)S(1)} %bitcast.10), custom_call_target="tpu_custom_call" | custom-call | flops 1 | bytes 1 | tf_op jit(solution)/shard_map/cut_odd/pallas_call | solution.py:281
  16.0 0.9 %collective-permute-done.9.refs_1_ = bf16[832,128]{1,0:T(8,128)(2,1)S(1)} collective-permute-done((bf16[832,128]{1,0:T(8,128)(2,1)S(1)}, bf16[832,128]{1,0:T(8,128)(2,1)S(1)}, u32[]{:S(2)}, u32[]{:S(2)}) %collective-permute-start.9) | collective-permute-done | bytes 213024 | tf_op jit(solution)/shard_map/ppermute | solution.py:323
  16.8 0.0 collective-permute-start.10
  16.8 2.7 %collective-permute-start.8 = (bf16[832,128]{1,0:T(8,128)(2,1)S(1)}, bf16[832,128]{1,0:T(8,128)(2,1)S(1)}, u32[]{:S(2)}, u32[]{:S(2)}) collective-permute-start(bf16[832,128]{1,0:T(8,128)(2,1)S(1)} %get-tuple-element.54), channel_id=1, source_target_pairs={{0,5},{1,4},{2,7},{3,6},{4,1},{5,0},{6,3},{7,2},{8,13},{9,12},{10,... | collective-permute-start | bytes 638984 | tf_op jit(solution)/shard_map/ppermute | solution.py:323
  19.6 0.0 collective-permute-start.6
  19.6 0.8 %collective-permute-done.4.refs_1_ = bf16[832,128]{1,0:T(8,128)(2,1)S(1)} collective-permute-done((bf16[832,128]{1,0:T(8,128)(2,1)S(1)}, bf16[832,128]{1,0:T(8,128)(2,1)S(1)}, u32[]{:S(2)}, u32[]{:S(2)}) %collective-permute-start.4) | collective-permute-done | bytes 213024 | tf_op jit(solution)/shard_map/ppermute | solution.py:323
  20.4 0.3 collective-permute-start.5
  20.6 2.7 %rows.1 = (bf16[768,1536]{1,0:T(8,128)(2,1)S(1)}, f32[8,1536]{1,0:T(8,128)S(1)}, bf16[1024,1536]{1,0:T(8,128)(2,1)S(1)}) custom-call(bf16[1536,768]{1,0:T(8,128)(2,1)S(1)} %copy-done, s32[8,1536]{1,0:T(8,128)S(1)} %get-tuple-element.48.slot_ref), custom_call_target="tpu_custom_call" | custom-call | flops 1 | bytes 1 | tf_op jit(solution)/shard_map/rows/pallas_call | solution.py:293
  23.4 1.2 %weights.4 = (f32[128,1536]{1,0:T(8,128)S(1)}, bf16[256,1536]{1,0:T(8,128)(2,1)S(1)}, bf16[256,1536]{1,0:T(8,128)(2,1)S(1)}) custom-call(bf16[832,128]{1,0:T(8,128)(2,1)S(1)} %get-tuple-element.58.refs_0_, bf16[832,128]{1,0:T(8,128)(2,1)S(1)} %collective-permute-done.4.refs_1_, bf16[768,1536]{1,0:T(8,128)(2,1)S(1)} %get-tuple-element.49.refs_2_.refs_1_, ...), custom_call_target="tpu_custom_call" | custom-call | flops 1 | bytes 1 | tf_op jit(solution)/shard_map/weights/pallas_call | solution.py:307
  24.6 0.0 collective-permute-done.10.refs_0_
  24.6 1.2 %weights.5 = (f32[128,1536]{1,0:T(8,128)S(1)}, bf16[256,1536]{1,0:T(8,128)(2,1)S(1)}, bf16[256,1536]{1,0:T(8,128)(2,1)S(1)}) custom-call(bf16[832,128]{1,0:T(8,128)(2,1)S(1)} %collective-permute-done.10.refs_0_, bf16[832,128]{1,0:T(8,128)(2,1)S(1)} %collective-permute-done.9.refs_1_, bf16[768,1536]{1,0:T(8,128)(2,1)S(1)} %get-tuple-element.49.refs_2_.refs_1_, ...), custom_call_target="tpu_custom_call" | custom-call | flops 1 | bytes 1 | tf_op jit(solution)/shard_map/weights/pallas_call | solution.py:307
  25.9 2.3 %collective-permute-done.8.refs_0_ = bf16[832,128]{1,0:T(8,128)(2,1)S(1)} collective-permute-done((bf16[832,128]{1,0:T(8,128)(2,1)S(1)}, bf16[832,128]{1,0:T(8,128)(2,1)S(1)}, u32[]{:S(2)}, u32[]{:S(2)}) %collective-permute-start.8) | collective-permute-done | bytes 213024 | tf_op jit(solution)/shard_map/ppermute | solution.py:323
  28.2 0.8 %weights.6 = (f32[128,1536]{1,0:T(8,128)S(1)}, bf16[128,1536]{1,0:T(8,128)(2,1)S(1)}, bf16[128,1536]{1,0:T(8,128)(2,1)S(1)}) custom-call(bf16[832,128]{1,0:T(8,128)(2,1)S(1)} %collective-permute-done.8.refs_0_, bf16[768,1536]{1,0:T(8,128)(2,1)S(1)} %get-tuple-element.49.refs_2_.refs_1_, bf16[1024,1536]{1,0:T(8,128)(2,1)S(1)} %get-tuple-element.50.refs_3_.refs_2_, ...), custom_call_target="tpu_custom_call" | custom-call | flops 1 | bytes 1 | tf_op jit(solution)/shard_map/weights/pallas_call | solution.py:307
  29.0 0.0 collective-permute-done.7.refs_1_
  29.0 1.2 %weights.7 = (f32[128,1536]{1,0:T(8,128)S(1)}, bf16[256,1536]{1,0:T(8,128)(2,1)S(1)}, bf16[256,1536]{1,0:T(8,128)(2,1)S(1)}) custom-call(bf16[832,128]{1,0:T(8,128)(2,1)S(1)} %collective-permute-done.6.refs_0_, bf16[832,128]{1,0:T(8,128)(2,1)S(1)} %collective-permute-done.7.refs_1_, bf16[768,1536]{1,0:T(8,128)(2,1)S(1)} %get-tuple-element.49.refs_2_.refs_1_, ...), custom_call_target="tpu_custom_call" | custom-call | flops 1 | bytes 1 | tf_op jit(solution)/shard_map/weights/pallas_call | solution.py:307
  30.2 0.8 %collective-permute-done.5.refs_0_ = bf16[832,128]{1,0:T(8,128)(2,1)S(1)} collective-permute-done((bf16[832,128]{1,0:T(8,128)(2,1)S(1)}, bf16[832,128]{1,0:T(8,128)(2,1)S(1)}, u32[]{:S(2)}, u32[]{:S(2)}) %collective-permute-start.5) | collective-permute-done | bytes 213024 | tf_op jit(solution)/shard_map/ppermute | solution.py:323
  31.1 2.7 %terms.1 = s32[1056,128]{1,0:T(8,128)S(1)} custom-call(bf16[832,128]{1,0:T(8,128)(2,1)S(1)} %collective-permute-done.5.refs_0_, bf16[768,1536]{1,0:T(8,128)(2,1)S(1)} %get-tuple-element.49.refs_2_.refs_1_, bf16[1024,1536]{1,0:T(8,128)(2,1)S(1)} %get-tuple-element.50.refs_3_.refs_2_, f32[8,1536]{1,0:T(8,128)S(1)} %get-tuple-element.51.refs_4_.refs_3_, ...), custom_call_target="tpu_custom_call" | custom-call | flops 1 | bytes 1 | tf_op jit(solution)/shard_map/terms/pallas_call | solution.py:330
  33.8 20.9 %all_to_all.5 = s32[1056,1,128]{2,1,0:T(1,128)S(1)} all-to-all(s32[1056,1,128]{2,1,0:T(1,128)S(1)} %bitcast.7), channel_id=1, replica_groups=mesh['samp'=4,'arow'=4,'acol'=2] {'samp','arow','acol'}, dimensions={0} | all-to-all | bytes 1081344 | tf_op jit(solution)/shard_map/all_to_all | solution.py:340
  54.7 1.3 %sum_terms.1 = f32[64,2048]{1,0:T(8,128)} custom-call(s32[1056,128]{1,0:T(8,128)S(1)} %bitcast.8), custom_call_target="tpu_custom_call" | custom-call | tf_op jit(solution)/shard_map/sum_terms/pallas_call | solution.py:341
  (7 shorter events, 0.0 us)
Async XLA Ops:
  0.0 14.4 %copy-start.1 = (bf16[2048,64]{0,1:T(8,128)(2,1)S(1)}, bf16[2048,64]{0,1:T(8,128)(2,1)}, u32[]{:S(2)}) copy-start(bf16[2048,64]{0,1:T(8,128)(2,1)} %param.6) | copy-start | bytes 786436
  0.0 0.8 %copy-start.2 = (s32[1536,8]{0,1:T(8,128)S(1)}, s32[1536,8]{0,1:T(8,128)}, u32[]{:S(2)}) copy-start(s32[1536,8]{0,1:T(8,128)} %param.7) | copy-start | bytes 147460
  1.1 5.5 %collective-permute-start.2 = (s32[8,128]{1,0:T(8,128)S(1)}, s32[8,128]{1,0:T(8,128)S(1)}, u32[]{:S(2)}, u32[]{:S(2)}) collective-permute-start(s32[8,128]{1,0:T(8,128)S(1)} %get-tuple-element.39.refs_0_.refs_5_), channel_id=1, source_target_pairs={{0,6},{1,7},{2,4},{3,5},{4,2},{5,3},{6,0},{7,1},{8,14},{9,15},{10,... | collective-permute-start | bytes 12296 | tf_op jit(solution)/shard_map/ppermute | solution.py:269
  5.1 3.6 %collective-permute-start.1 = (s32[8,128]{1,0:T(8,128)S(1)}, s32[8,128]{1,0:T(8,128)S(1)}, u32[]{:S(2)}, u32[]{:S(2)}) collective-permute-start(s32[8,128]{1,0:T(8,128)S(1)} %get-tuple-element.39.refs_0_.refs_5_), channel_id=1, source_target_pairs={{0,4},{1,5},{2,6},{3,7},{4,0},{5,1},{6,2},{7,3},{8,12},{9,13},{10,... | collective-permute-start | bytes 12296 | tf_op jit(solution)/shard_map/ppermute | solution.py:269
  5.6 3.6 %collective-permute-start = (s32[8,128]{1,0:T(8,128)S(1)}, s32[8,128]{1,0:T(8,128)S(1)}, u32[]{:S(2)}, u32[]{:S(2)}) collective-permute-start(s32[8,128]{1,0:T(8,128)S(1)} %get-tuple-element.39.refs_0_.refs_5_), channel_id=1, source_target_pairs={{0,2},{1,3},{2,0},{3,1},{4,6},{5,7},{6,4},{7,5},{8,10},{9,11},{10,... | collective-permute-start | bytes 12296 | tf_op jit(solution)/shard_map/ppermute | solution.py:269
  9.2 11.5 %copy-start = (bf16[1536,768]{1,0:T(8,128)(2,1)S(1)}, bf16[1536,768]{1,0:T(8,128)(2,1)}, u32[]{:S(2)}) copy-start(bf16[1536,768]{1,0:T(8,128)(2,1)} %rows_ref.1) | copy-start | bytes 7077892
  10.9 6.0 %collective-permute-start.9 = (bf16[832,128]{1,0:T(8,128)(2,1)S(1)}, bf16[832,128]{1,0:T(8,128)(2,1)S(1)}, u32[]{:S(2)}, u32[]{:S(2)}) collective-permute-start(bf16[832,128]{1,0:T(8,128)(2,1)S(1)} %get-tuple-element.56), channel_id=1, source_target_pairs={{0,4},{1,5},{2,6},{3,7},{4,0},{5,1},{6,2},{7,3},{8,12},{9,13},{10,... | collective-permute-start | bytes 638984 | tf_op jit(solution)/shard_map/ppermute | solution.py:323
  12.4 8.0 %collective-permute-start.4 = (bf16[832,128]{1,0:T(8,128)(2,1)S(1)}, bf16[832,128]{1,0:T(8,128)(2,1)S(1)}, u32[]{:S(2)}, u32[]{:S(2)}) collective-permute-start(bf16[832,128]{1,0:T(8,128)(2,1)S(1)} %get-tuple-element.46), channel_id=1, source_target_pairs={{0,2},{1,3},{2,0},{3,1},{4,6},{5,7},{6,4},{7,5},{8,10},{9,11},{10,... | collective-permute-start | bytes 638984 | tf_op jit(solution)/shard_map/ppermute | solution.py:323
  13.0 1.4 %collective-permute-start.3 = (s32[8,128]{1,0:T(8,128)S(1)}, s32[8,128]{1,0:T(8,128)S(1)}, u32[]{:S(2)}, u32[]{:S(2)}) collective-permute-start(s32[8,128]{1,0:T(8,128)S(1)} %get-tuple-element.40), channel_id=1, source_target_pairs={{0,1},{1,0},{2,3},{3,2},{4,5},{5,4},{6,7},{7,6},{8,9},{9,8},{10,11... | collective-permute-start | bytes 12296 | tf_op jit(solution)/shard_map/ppermute | solution.py:280
  13.0 16.0 %collective-permute-start.7 = (bf16[832,128]{1,0:T(8,128)(2,1)S(1)}, bf16[832,128]{1,0:T(8,128)(2,1)S(1)}, u32[]{:S(2)}, u32[]{:S(2)}) collective-permute-start(bf16[832,128]{1,0:T(8,128)(2,1)S(1)} %get-tuple-element.53), channel_id=1, source_target_pairs={{0,6},{1,7},{2,4},{3,5},{4,2},{5,3},{6,0},{7,1},{8,14},{9,15},{10,... | collective-permute-start | bytes 638984 | tf_op jit(solution)/shard_map/ppermute | solution.py:323
  16.8 7.8 %collective-permute-start.10 = (bf16[832,128]{1,0:T(8,128)(2,1)S(1)}, bf16[832,128]{1,0:T(8,128)(2,1)S(1)}, u32[]{:S(2)}, u32[]{:S(2)}) collective-permute-start(bf16[832,128]{1,0:T(8,128)(2,1)S(1)} %get-tuple-element.57), channel_id=1, source_target_pairs={{0,1},{1,0},{2,3},{3,2},{4,5},{5,4},{6,7},{7,6},{8,9},{9,8},{10,11... | collective-permute-start | bytes 638984 | tf_op jit(solution)/shard_map/ppermute | solution.py:323
  16.8 11.3 %collective-permute-start.8 = (bf16[832,128]{1,0:T(8,128)(2,1)S(1)}, bf16[832,128]{1,0:T(8,128)(2,1)S(1)}, u32[]{:S(2)}, u32[]{:S(2)}) collective-permute-start(bf16[832,128]{1,0:T(8,128)(2,1)S(1)} %get-tuple-element.54), channel_id=1, source_target_pairs={{0,5},{1,4},{2,7},{3,6},{4,1},{5,0},{6,3},{7,2},{8,13},{9,12},{10,... | collective-permute-start | bytes 638984 | tf_op jit(solution)/shard_map/ppermute | solution.py:323
  19.6 9.4 %collective-permute-start.6 = (bf16[832,128]{1,0:T(8,128)(2,1)S(1)}, bf16[832,128]{1,0:T(8,128)(2,1)S(1)}, u32[]{:S(2)}, u32[]{:S(2)}) collective-permute-start(bf16[832,128]{1,0:T(8,128)(2,1)S(1)} %get-tuple-element.52), channel_id=1, source_target_pairs={{0,3},{1,2},{2,1},{3,0},{4,7},{5,6},{6,5},{7,4},{8,11},{9,10},{10,... | collective-permute-start | bytes 638984 | tf_op jit(solution)/shard_map/ppermute | solution.py:323
  20.4 10.7 %collective-permute-start.5 = (bf16[832,128]{1,0:T(8,128)(2,1)S(1)}, bf16[832,128]{1,0:T(8,128)(2,1)S(1)}, u32[]{:S(2)}, u32[]{:S(2)}) collective-permute-start(bf16[832,128]{1,0:T(8,128)(2,1)S(1)} %get-tuple-element.47), channel_id=1, source_target_pairs={{0,7},{1,6},{2,5},{3,4},{4,3},{5,2},{6,1},{7,0},{8,15},{9,14},{10,... | collective-permute-start | bytes 638984 | tf_op jit(solution)/shard_map/ppermute | solution.py:323

commit v4 on v3

--- a/solution.py
+++ b/solution.py
@@ -15,7 +15,7 @@
 MISS = -1e30
 ORDER = [(2, 0), (4, 0), (6, 0), (3, 0), (5, 0), (7, 2), (1, 4)]
 GROUPS = [[0, 2], [1, 4], [5], [3, 6], [7]]
-LIMIT_EVEN, LIMIT_ODD = 52.9, 52.1
+LIMIT_STAGE = 49
 IN_FLIGHT = 5
 FULL = 32704.0
 STEPS_PER_OCTAVE = 256.0
@@ -49,7 +49,7 @@
         return lax.axis_index("arow") * self.cols + lax.axis_index("acol")
 
     def even(self):
-        return list(range(0, self.owners, 2))
+        return [0, *range(self.owners - 2, 0, -2)]
 
     def odd(self):
         return list(range(1, self.owners, 2))
@@ -57,7 +57,7 @@
     def order(self):
         if self.owners == 8:
             return ORDER
-        steps = [*self.even()[1:], *self.odd()]
+        steps = [*self.even()[:0:-1], *self.odd()]
         return [(s, steps[i - IN_FLIGHT] if i >= IN_FLIGHT else 0) for i, s in enumerate(steps)]
 
     def groups(self):
@@ -80,22 +80,22 @@
         wanted_ref[o : o + 1, :] = jnp.full((1, LANES), jnp.max(picked), jnp.int32)
 
 
-def cut(starts, depth_tiles, cols, anchors_ref, panel_ref, out, blocks, sem):
-    copies, panels = [], []
+def stage_kernel(_, anchors_ref, panel_ref, anchors_out, panel_out, sem):
+    copies = [
+        pltpu.make_async_copy(anchors_ref, anchors_out, sem.at[0]),
+        pltpu.make_async_copy(panel_ref, panel_out, sem.at[1]),
+    ]
+    for copy in copies:
+        copy.start()
+    for copy in copies:
+        copy.wait()
+
+
+def cut(starts, depth_tiles, cols, anchors_ref, panel_ref, out):
     for i, start in enumerate(starts):
-        copies.append(pltpu.make_async_copy(anchors_ref.at[pl.ds(start, BA), :], blocks.at[i], sem.at[i]))
-        copies[i].start()
-    for i, start in enumerate(starts):
-        panels.append(pltpu.make_async_copy(
-            panel_ref.at[:, pl.ds(start, BA)], out[i].at[pl.ds(depth_tiles * BA, cols), :], sem.at[len(starts) + i]
-        ))
-        panels[i].start()
-    for i, copy in enumerate(copies):
-        copy.wait()
         for j in range(depth_tiles):
-            out[i][j * BA : (j + 1) * BA, :] = blocks[i, :, j * LANES : (j + 1) * LANES]
-    for panel in panels:
-        panel.wait()
+            out[i][j * BA : (j + 1) * BA, :] = anchors_ref[pl.ds(start, BA), j * LANES : (j + 1) * LANES]
+        out[i][depth_tiles * BA :, :] = panel_ref[:, pl.ds(start, BA)]
 
 
 def block_start(line):
@@ -105,19 +105,19 @@
 def even_kernel(plan, depth_tiles, cols, *refs):
     n = len(plan.even())
     asked, (anchors_ref, panel_ref), out = refs[:n], refs[n : n + 2], refs[n + 2 : 2 * n + 2]
-    passed_ref, blocks, sem = refs[2 * n + 2 :]
+    passed_ref = refs[2 * n + 2]
     me = plan.me()
     starts = [block_start(a[pl.ds(me, 1), :]) for a in asked]
     passed_ref[...] = jnp.zeros_like(passed_ref)
-    for i, a in enumerate(asked):
-        passed_ref[i : i + 1, :] = a[pl.ds(me ^ 1, 1), :]
-    cut(starts, depth_tiles, cols, anchors_ref, panel_ref, out, blocks, sem)
+    for s, a in zip(plan.even(), asked):
+        passed_ref[s // 2 : s // 2 + 1, :] = a[pl.ds(me ^ 1, 1), :]
+    cut(starts, depth_tiles, cols, anchors_ref, panel_ref, out)
 
 
 def odd_kernel(plan, depth_tiles, cols, passed_ref, anchors_ref, panel_ref, *refs):
     n = len(plan.odd())
     starts = [block_start(passed_ref[i : i + 1, :]) for i in range(n)]
-    cut(starts, depth_tiles, cols, anchors_ref, panel_ref, refs[:n], *refs[n:])
+    cut(starts, depth_tiles, cols, anchors_ref, panel_ref, refs)
 
 
 def split(x):
@@ -264,30 +264,37 @@
     message = struct((depth_tiles * BA + cols, LANES), bf16)
     even, odd = plan.even(), plan.odd()
     half = len(even)
-    scratch = [pltpu.VMEM((half, BA, depth), bf16), pltpu.SemaphoreType.DMA((2 * half,))]
+    staged = pl.pallas_call(
+        stage_kernel,
+        out_shape=(struct(anchors.shape, bf16), struct(panel.shape, bf16)),
+        in_specs=[VMEM, HBM, HBM],
+        out_specs=(VMEM, VMEM),
+        scratch_shapes=[pltpu.SemaphoreType.DMA((2,))],
+        cost_estimate=QUICK,
+        compiler_params=params(LIMIT_STAGE),
+        name="stage",
+    )(wanted, anchors, panel)
     passed = struct((-(-half // 8) * 8, LANES), i32)
     asked = [wanted, *(lax.ppermute(wanted, here, plan.pairs(s)) for s in even[1:])]
     *sent_even, passed = pl.pallas_call(
         functools.partial(even_kernel, plan, depth_tiles, cols),
         out_shape=(*(message,) * half, passed),
-        in_specs=[*[VMEM] * half, HBM, HBM],
+        in_specs=[VMEM] * (half + 2),
         out_specs=(VMEM,) * (half + 1),
-        scratch_shapes=scratch,
-        cost_estimate=QUICK,
-        compiler_params=params(LIMIT_EVEN),
+        cost_estimate=QUICK,
+        compiler_params=params(4),
         name="cut_even",
-    )(*asked, anchors, panel)
+    )(*asked, *staged)
     passed = lax.ppermute(passed, here, plan.pairs(1))
     sent_odd = pl.pallas_call(
         functools.partial(odd_kernel, plan, depth_tiles, cols),
         out_shape=(message,) * half,
-        in_specs=[VMEM, HBM, HBM],
+        in_specs=[VMEM] * 3,
         out_specs=(VMEM,) * half,
-        scratch_shapes=scratch,
-        cost_estimate=QUICK,
-        compiler_params=params(LIMIT_ODD),
+        cost_estimate=QUICK,
+        compiler_params=params(4),
         name="cut_odd",
-    )(passed, anchors, panel)
+    )(passed, *staged)
     slot, *sent_odd = lax.optimization_barrier((slot, *sent_odd))
     sent = {**dict(zip(even, sent_even)), **dict(zip(odd, sent_odd))}
     turned, scale, bias = pl.pallas_call(

time: 56.1 us -> 55.7 us (level)
  waiting for transfers between devices: 8.31 us -> 6.89 us
  local copies, waits for them, and re-layouts: 0.85 us -> 1.75 us
    pallas_call x0 -> x1, Pallas kernels: none -> 1.91 us  [per_device(): pl.pallas_call(stage_kernel, out_shape=(struct(anchors.shape, bf16), stru...]
    ppermute x3, waiting for transfers between devices: 3.47 us -> 1.6 us  [per_device(): lax.ppermute(wanted, here, plan.pairs(s))]
    pallas_call x1, Pallas kernels: 1.65 us -> 0.35 us  [per_device(): pl.pallas_call(functools.partial(even_kernel, plan, depth_tiles, cols), o...]
    pallas_call x1, Pallas kernels: 1.53 us -> 0.35 us  [per_device(): pl.pallas_call(functools.partial(odd_kernel, plan, depth_tiles, cols), ou...]
    unnamed x6, local copies, waits for them, and re-layouts: 0.85 us -> 1.75 us
  transfers between devices with their start and end apart: 11 -> 11, of which waited for: 7 -> 3; matrix products, arithmetic and copies ran while one was open for 0% -> 0% of each run, Pallas kernels for 16% -> 17%
where the time goes in v4:
time: 55.7 us; the launch traced here: 55.4 us
  blocking collectives  21 us (38%)
  Pallas kernels  14.2 us (25%)
  starting transfers between devices  11.4 us (20%)
  waiting for transfers between devices  6.89 us (12%)
  local copies, waits for them, and re-layouts  1.75 us (3%)
    all_to_all x1, blocking collectives, per_device(): lax.all_to_all(terms[:, None, :], ('samp', 'arow', 'acol'), 0, 0, tiled=T...  21 us
    ppermute x7, starting transfers between devices, per_device(): held[s] = lax.ppermute(block, here, plan.pairs(s))  6.89 us
    ppermute x7, waiting for transfers between devices, per_device(): held[s] = lax.ppermute(block, here, plan.pairs(s))  5.28 us
    pallas_call x4, Pallas kernels, weigh(): pl.pallas_call(functools.partial(group_kernel, g, sizes), out_shape=(stru...  4.55 us
    ppermute x3, starting transfers between devices, per_device(): lax.ppermute(wanted, here, plan.pairs(s))  4.54 us
    pallas_call x1, Pallas kernels, per_device(): pl.pallas_call(functools.partial(last_kernel, plan, copies, groups, sizes...  2.73 us
    pallas_call x1, Pallas kernels, per_device(): pl.pallas_call(rows_kernel, out_shape=(struct((depth, rows), bf16), struc...  2.71 us
    pallas_call x1, Pallas kernels, per_device(): pl.pallas_call(stage_kernel, out_shape=(struct(anchors.shape, bf16), stru...  1.91 us
  transfers between devices with their start and end apart: 11, of which 3 were waited for; matrix products, arithmetic and copies ran while one was open for 0% of the time, Pallas kernels for 17%

profile of v4, /device:TPU:0, one launch (start us, length us, event | category | flops | bytes accessed | tf_op | source)
XLA Modules:
  0.0 55.4 jit_solution(15765737965126948345)
XLA Ops:
  0.0 0.8 %copy-done.2 = s32[1536,8]{0,1:T(8,128)S(1)} copy-done((s32[1536,8]{0,1:T(8,128)S(1)}, s32[1536,8]{0,1:T(8,128)}, u32[]{:S(2)}) %copy-start.2) | copy-done | bytes 49176
  0.8 0.3 prepare.1
  1.1 3.0 %collective-permute-start.2 = (s32[8,128]{1,0:T(8,128)S(1)}, s32[8,128]{1,0:T(8,128)S(1)}, u32[]{:S(2)}, u32[]{:S(2)}) collective-permute-start(s32[8,128]{1,0:T(8,128)S(1)} %get-tuple-element.41._.refs_0_.refs_5_), channel_id=1, source_target_pairs={{0,2},{1,3},{2,0},{3,1},{4,6},{5,7},{6,4},{7,5},{8,10},{9,11},{10,... | collective-permute-start | bytes 12296 | tf_op jit(solution)/shard_map/ppermute | solution.py:278
  4.1 1.5 %collective-permute-start.1 = (s32[8,128]{1,0:T(8,128)S(1)}, s32[8,128]{1,0:T(8,128)S(1)}, u32[]{:S(2)}, u32[]{:S(2)}) collective-permute-start(s32[8,128]{1,0:T(8,128)S(1)} %get-tuple-element.41._.refs_0_.refs_5_), channel_id=1, source_target_pairs={{0,4},{1,5},{2,6},{3,7},{4,0},{5,1},{6,2},{7,3},{8,12},{9,13},{10,... | collective-permute-start | bytes 12296 | tf_op jit(solution)/shard_map/ppermute | solution.py:278
  5.6 0.0 collective-permute-start
  5.6 0.9 %copy-done.1 = bf16[2048,64]{0,1:T(8,128)(2,1)S(1)} copy-done((bf16[2048,64]{0,1:T(8,128)(2,1)S(1)}, bf16[2048,64]{0,1:T(8,128)(2,1)}, u32[]{:S(2)}) %copy-start.1) | copy-done | bytes 262168
  6.6 1.9 %stage.1 = (bf16[2048,768]{1,0:T(8,128)(2,1)S(1)}, bf16[64,2048]{1,0:T(8,128)(2,1)S(1)}) custom-call(s32[8,128]{1,0:T(8,128)S(1)} %get-tuple-element.41._.refs_0_.refs_5_, bf16[2048,768]{1,0:T(8,128)(2,1)} %anchors_ref.1, bf16[64,2048]{1,0:T(8,128)(2,1)S(1)} %bitcast.9), custom_call_target="tpu_custom_call" | custom-call | flops 1 | bytes 1 | tf_op jit(solution)/shard_map/stage/pallas_call | solution.py:267
  8.5 0.0 collective-permute-done.2.refs_3_
  8.5 0.0 collective-permute-done.1.refs_2_
  8.5 1.6 %collective-permute-done.refs_1_ = s32[8,128]{1,0:T(8,128)S(1)} collective-permute-done((s32[8,128]{1,0:T(8,128)S(1)}, s32[8,128]{1,0:T(8,128)S(1)}, u32[]{:S(2)}, u32[]{:S(2)}) %collective-permute-start) | collective-permute-done | bytes 4128 | tf_op jit(solution)/shard_map/ppermute | solution.py:278
  10.1 0.3 cut_even.1
  10.5 0.6 %collective-permute-start.9 = (bf16[832,128]{1,0:T(8,128)(2,1)S(1)}, bf16[832,128]{1,0:T(8,128)(2,1)S(1)}, u32[]{:S(2)}, u32[]{:S(2)}) collective-permute-start(bf16[832,128]{1,0:T(8,128)(2,1)S(1)} %get-tuple-element.60), channel_id=1, source_target_pairs={{0,4},{1,5},{2,6},{3,7},{4,0},{5,1},{6,2},{7,3},{8,12},{9,13},{10,... | collective-permute-start | bytes 638984 | tf_op jit(solution)/shard_map/ppermute | solution.py:330
  11.0 1.4 %collective-permute-start.4 = (bf16[832,128]{1,0:T(8,128)(2,1)S(1)}, bf16[832,128]{1,0:T(8,128)(2,1)S(1)}, u32[]{:S(2)}, u32[]{:S(2)}) collective-permute-start(bf16[832,128]{1,0:T(8,128)(2,1)S(1)} %get-tuple-element.50), channel_id=1, source_target_pairs={{0,2},{1,3},{2,0},{3,1},{4,6},{5,7},{6,4},{7,5},{8,10},{9,11},{10,... | collective-permute-start | bytes 638984 | tf_op jit(solution)/shard_map/ppermute | solution.py:330
  12.4 0.0 collective-permute-start.3
  12.4 1.6 %collective-permute-start.7 = (bf16[832,128]{1,0:T(8,128)(2,1)S(1)}, bf16[832,128]{1,0:T(8,128)(2,1)S(1)}, u32[]{:S(2)}, u32[]{:S(2)}) collective-permute-start(bf16[832,128]{1,0:T(8,128)(2,1)S(1)} %get-tuple-element.57), channel_id=1, source_target_pairs={{0,6},{1,7},{2,4},{3,5},{4,2},{5,3},{6,0},{7,1},{8,14},{9,15},{10,... | collective-permute-start | bytes 638984 | tf_op jit(solution)/shard_map/ppermute | solution.py:330
  14.0 0.3 cut_odd.1
  14.4 2.0 %collective-permute-done.9.refs_1_ = bf16[832,128]{1,0:T(8,128)(2,1)S(1)} collective-permute-done((bf16[832,128]{1,0:T(8,128)(2,1)S(1)}, bf16[832,128]{1,0:T(8,128)(2,1)S(1)}, u32[]{:S(2)}, u32[]{:S(2)}) %collective-permute-start.9) | collective-permute-done | bytes 213024 | tf_op jit(solution)/shard_map/ppermute | solution.py:330
  16.4 0.8 %collective-permute-start.8 = (bf16[832,128]{1,0:T(8,128)(2,1)S(1)}, bf16[832,128]{1,0:T(8,128)(2,1)S(1)}, u32[]{:S(2)}, u32[]{:S(2)}) collective-permute-start(bf16[832,128]{1,0:T(8,128)(2,1)S(1)} %get-tuple-element.58), channel_id=1, source_target_pairs={{0,5},{1,4},{2,7},{3,6},{4,1},{5,0},{6,3},{7,2},{8,13},{9,12},{10,... | collective-permute-start | bytes 638984 | tf_op jit(solution)/shard_map/ppermute | solution.py:330
  17.2 1.1 %collective-permute-start.6 = (bf16[832,128]{1,0:T(8,128)(2,1)S(1)}, bf16[832,128]{1,0:T(8,128)(2,1)S(1)}, u32[]{:S(2)}, u32[]{:S(2)}) collective-permute-start(bf16[832,128]{1,0:T(8,128)(2,1)S(1)} %get-tuple-element.56), channel_id=1, source_target_pairs={{0,3},{1,2},{2,1},{3,0},{4,7},{5,6},{6,5},{7,4},{8,11},{9,10},{10,... | collective-permute-start | bytes 638984 | tf_op jit(solution)/shard_map/ppermute | solution.py:330
  18.3 0.0 collective-permute-done.4.refs_1_
  18.3 1.4 %collective-permute-start.5 = (bf16[832,128]{1,0:T(8,128)(2,1)S(1)}, bf16[832,128]{1,0:T(8,128)(2,1)S(1)}, u32[]{:S(2)}, u32[]{:S(2)}) collective-permute-start(bf16[832,128]{1,0:T(8,128)(2,1)S(1)} %get-tuple-element.51), channel_id=1, source_target_pairs={{0,7},{1,6},{2,5},{3,4},{4,3},{5,2},{6,1},{7,0},{8,15},{9,14},{10,... | collective-permute-start | bytes 638984 | tf_op jit(solution)/shard_map/ppermute | solution.py:330
  19.7 2.7 %rows.1 = (bf16[768,1536]{1,0:T(8,128)(2,1)S(1)}, f32[8,1536]{1,0:T(8,128)S(1)}, bf16[1024,1536]{1,0:T(8,128)(2,1)S(1)}) custom-call(bf16[1536,768]{1,0:T(8,128)(2,1)S(1)} %copy-done, s32[8,1536]{1,0:T(8,128)S(1)} %get-tuple-element.52.slot_ref), custom_call_target="tpu_custom_call" | custom-call | flops 1 | bytes 1 | tf_op jit(solution)/shard_map/rows/pallas_call | solution.py:300
  22.4 1.3 %weights.4 = (f32[128,1536]{1,0:T(8,128)S(1)}, bf16[256,1536]{1,0:T(8,128)(2,1)S(1)}, bf16[256,1536]{1,0:T(8,128)(2,1)S(1)}) custom-call(bf16[832,128]{1,0:T(8,128)(2,1)S(1)} %get-tuple-element.62.refs_0_, bf16[832,128]{1,0:T(8,128)(2,1)S(1)} %collective-permute-done.4.refs_1_, bf16[768,1536]{1,0:T(8,128)(2,1)S(1)} %get-tuple-element.53.refs_2_.refs_1_, ...), custom_call_target="tpu_custom_call" | custom-call | flops 1 | bytes 1 | tf_op jit(solution)/shard_map/weights/pallas_call | solution.py:314
  23.7 0.0 collective-permute-done.10.refs_0_
  23.7 1.2 %weights.5 = (f32[128,1536]{1,0:T(8,128)S(1)}, bf16[256,1536]{1,0:T(8,128)(2,1)S(1)}, bf16[256,1536]{1,0:T(8,128)(2,1)S(1)}) custom-call(bf16[832,128]{1,0:T(8,128)(2,1)S(1)} %collective-permute-done.10.refs_0_, bf16[832,128]{1,0:T(8,128)(2,1)S(1)} %collective-permute-done.9.refs_1_, bf16[768,1536]{1,0:T(8,128)(2,1)S(1)} %get-tuple-element.53.refs_2_.refs_1_, ...), custom_call_target="tpu_custom_call" | custom-call | flops 1 | bytes 1 | tf_op jit(solution)/shard_map/weights/pallas_call | solution.py:314
  25.0 3.3 %collective-permute-done.8.refs_0_ = bf16[832,128]{1,0:T(8,128)(2,1)S(1)} collective-permute-done((bf16[832,128]{1,0:T(8,128)(2,1)S(1)}, bf16[832,128]{1,0:T(8,128)(2,1)S(1)}, u32[]{:S(2)}, u32[]{:S(2)}) %collective-permute-start.8) | collective-permute-done | bytes 213024 | tf_op jit(solution)/shard_map/ppermute | solution.py:330
  28.2 0.8 %weights.6 = (f32[128,1536]{1,0:T(8,128)S(1)}, bf16[128,1536]{1,0:T(8,128)(2,1)S(1)}, bf16[128,1536]{1,0:T(8,128)(2,1)S(1)}) custom-call(bf16[832,128]{1,0:T(8,128)(2,1)S(1)} %collective-permute-done.8.refs_0_, bf16[768,1536]{1,0:T(8,128)(2,1)S(1)} %get-tuple-element.53.refs_2_.refs_1_, bf16[1024,1536]{1,0:T(8,128)(2,1)S(1)} %get-tuple-element.54.refs_3_.refs_2_, ...), custom_call_target="tpu_custom_call" | custom-call | flops 1 | bytes 1 | tf_op jit(solution)/shard_map/weights/pallas_call | solution.py:314
  29.0 0.0 collective-permute-done.7.refs_1_
  29.1 1.2 %weights.7 = (f32[128,1536]{1,0:T(8,128)S(1)}, bf16[256,1536]{1,0:T(8,128)(2,1)S(1)}, bf16[256,1536]{1,0:T(8,128)(2,1)S(1)}) custom-call(bf16[832,128]{1,0:T(8,128)(2,1)S(1)} %collective-permute-done.6.refs_0_, bf16[832,128]{1,0:T(8,128)(2,1)S(1)} %collective-permute-done.7.refs_1_, bf16[768,1536]{1,0:T(8,128)(2,1)S(1)} %get-tuple-element.53.refs_2_.refs_1_, ...), custom_call_target="tpu_custom_call" | custom-call | flops 1 | bytes 1 | tf_op jit(solution)/shard_map/weights/pallas_call | solution.py:314
  30.3 2.7 %terms.1 = s32[1056,128]{1,0:T(8,128)S(1)} custom-call(bf16[832,128]{1,0:T(8,128)(2,1)S(1)} %collective-permute-done.5.refs_0_, bf16[768,1536]{1,0:T(8,128)(2,1)S(1)} %get-tuple-element.53.refs_2_.refs_1_, bf16[1024,1536]{1,0:T(8,128)(2,1)S(1)} %get-tuple-element.54.refs_3_.refs_2_, f32[8,1536]{1,0:T(8,128)S(1)} %get-tuple-element.55.refs_4_.refs_3_, ...), custom_call_target="tpu_custom_call" | custom-call | flops 1 | bytes 1 | tf_op jit(solution)/shard_map/terms/pallas_call | solution.py:337
  33.1 21.0 %all_to_all.5 = s32[1056,1,128]{2,1,0:T(1,128)S(1)} all-to-all(s32[1056,1,128]{2,1,0:T(1,128)S(1)} %bitcast.7), channel_id=1, replica_groups=mesh['samp'=4,'arow'=4,'acol'=2] {'samp','arow','acol'}, dimensions={0} | all-to-all | bytes 1081344 | tf_op jit(solution)/shard_map/all_to_all | solution.py:347
  54.1 1.3 %sum_terms.1 = f32[64,2048]{1,0:T(8,128)} custom-call(s32[1056,128]{1,0:T(8,128)S(1)} %bitcast.8), custom_call_target="tpu_custom_call" | custom-call | tf_op jit(solution)/shard_map/sum_terms/pallas_call | solution.py:348
  (8 shorter events, 0.0 us)
Async XLA Ops:
  0.0 0.8 %copy-start.2 = (s32[1536,8]{0,1:T(8,128)S(1)}, s32[1536,8]{0,1:T(8,128)}, u32[]{:S(2)}) copy-start(s32[1536,8]{0,1:T(8,128)} %param.7) | copy-start | bytes 147460
  1.1 7.4 %collective-permute-start.2 = (s32[8,128]{1,0:T(8,128)S(1)}, s32[8,128]{1,0:T(8,128)S(1)}, u32[]{:S(2)}, u32[]{:S(2)}) collective-permute-start(s32[8,128]{1,0:T(8,128)S(1)} %get-tuple-element.41._.refs_0_.refs_5_), channel_id=1, source_target_pairs={{0,2},{1,3},{2,0},{3,1},{4,6},{5,7},{6,4},{7,5},{8,10},{9,11},{10,... | collective-permute-start | bytes 12296 | tf_op jit(solution)/shard_map/ppermute | solution.py:278
  4.1 4.4 %collective-permute-start.1 = (s32[8,128]{1,0:T(8,128)S(1)}, s32[8,128]{1,0:T(8,128)S(1)}, u32[]{:S(2)}, u32[]{:S(2)}) collective-permute-start(s32[8,128]{1,0:T(8,128)S(1)} %get-tuple-element.41._.refs_0_.refs_5_), channel_id=1, source_target_pairs={{0,4},{1,5},{2,6},{3,7},{4,0},{5,1},{6,2},{7,3},{8,12},{9,13},{10,... | collective-permute-start | bytes 12296 | tf_op jit(solution)/shard_map/ppermute | solution.py:278
  5.6 4.5 %collective-permute-start = (s32[8,128]{1,0:T(8,128)S(1)}, s32[8,128]{1,0:T(8,128)S(1)}, u32[]{:S(2)}, u32[]{:S(2)}) collective-permute-start(s32[8,128]{1,0:T(8,128)S(1)} %get-tuple-element.41._.refs_0_.refs_5_), channel_id=1, source_target_pairs={{0,6},{1,7},{2,4},{3,5},{4,2},{5,3},{6,0},{7,1},{8,14},{9,15},{10,... | collective-permute-start | bytes 12296 | tf_op jit(solution)/shard_map/ppermute | solution.py:278
  5.6 0.9 %copy-start.1 = (bf16[2048,64]{0,1:T(8,128)(2,1)S(1)}, bf16[2048,64]{0,1:T(8,128)(2,1)}, u32[]{:S(2)}) copy-start(bf16[2048,64]{0,1:T(8,128)(2,1)} %param.6) | copy-start | bytes 786436
  10.1 9.6 %copy-start = (bf16[1536,768]{1,0:T(8,128)(2,1)S(1)}, bf16[1536,768]{1,0:T(8,128)(2,1)}, u32[]{:S(2)}) copy-start(bf16[1536,768]{1,0:T(8,128)(2,1)} %rows_ref.1) | copy-start | bytes 7077892
  10.5 5.9 %collective-permute-start.9 = (bf16[832,128]{1,0:T(8,128)(2,1)S(1)}, bf16[832,128]{1,0:T(8,128)(2,1)S(1)}, u32[]{:S(2)}, u32[]{:S(2)}) collective-permute-start(bf16[832,128]{1,0:T(8,128)(2,1)S(1)} %get-tuple-element.60), channel_id=1, source_target_pairs={{0,4},{1,5},{2,6},{3,7},{4,0},{5,1},{6,2},{7,3},{8,12},{9,13},{10,... | collective-permute-start | bytes 638984 | tf_op jit(solution)/shard_map/ppermute | solution.py:330
  11.0 7.3 %collective-permute-start.4 = (bf16[832,128]{1,0:T(8,128)(2,1)S(1)}, bf16[832,128]{1,0:T(8,128)(2,1)S(1)}, u32[]{:S(2)}, u32[]{:S(2)}) collective-permute-start(bf16[832,128]{1,0:T(8,128)(2,1)S(1)} %get-tuple-element.50), channel_id=1, source_target_pairs={{0,2},{1,3},{2,0},{3,1},{4,6},{5,7},{6,4},{7,5},{8,10},{9,11},{10,... | collective-permute-start | bytes 638984 | tf_op jit(solution)/shard_map/ppermute | solution.py:330
  12.4 1.6 %collective-permute-start.3 = (s32[8,128]{1,0:T(8,128)S(1)}, s32[8,128]{1,0:T(8,128)S(1)}, u32[]{:S(2)}, u32[]{:S(2)}) collective-permute-start(s32[8,128]{1,0:T(8,128)S(1)} %get-tuple-element.44), channel_id=1, source_target_pairs={{0,1},{1,0},{2,3},{3,2},{4,5},{5,4},{6,7},{7,6},{8,9},{9,8},{10,11... | collective-permute-start | bytes 12296 | tf_op jit(solution)/shard_map/ppermute | solution.py:288
  12.4 16.6 %collective-permute-start.7 = (bf16[832,128]{1,0:T(8,128)(2,1)S(1)}, bf16[832,128]{1,0:T(8,128)(2,1)S(1)}, u32[]{:S(2)}, u32[]{:S(2)}) collective-permute-start(bf16[832,128]{1,0:T(8,128)(2,1)S(1)} %get-tuple-element.57), channel_id=1, source_target_pairs={{0,6},{1,7},{2,4},{3,5},{4,2},{5,3},{6,0},{7,1},{8,14},{9,15},{10,... | collective-permute-start | bytes 638984 | tf_op jit(solution)/shard_map/ppermute | solution.py:330
  16.4 7.3 %collective-permute-start.10 = (bf16[832,128]{1,0:T(8,128)(2,1)S(1)}, bf16[832,128]{1,0:T(8,128)(2,1)S(1)}, u32[]{:S(2)}, u32[]{:S(2)}) collective-permute-start(bf16[832,128]{1,0:T(8,128)(2,1)S(1)} %get-tuple-element.61), channel_id=1, source_target_pairs={{0,1},{1,0},{2,3},{3,2},{4,5},{5,4},{6,7},{7,6},{8,9},{9,8},{10,11... | collective-permute-start | bytes 638984 | tf_op jit(solution)/shard_map/ppermute | solution.py:330
  16.4 11.9 %collective-permute-start.8 = (bf16[832,128]{1,0:T(8,128)(2,1)S(1)}, bf16[832,128]{1,0:T(8,128)(2,1)S(1)}, u32[]{:S(2)}, u32[]{:S(2)}) collective-permute-start(bf16[832,128]{1,0:T(8,128)(2,1)S(1)} %get-tuple-element.58), channel_id=1, source_target_pairs={{0,5},{1,4},{2,7},{3,6},{4,1},{5,0},{6,3},{7,2},{8,13},{9,12},{10,... | collective-permute-start | bytes 638984 | tf_op jit(solution)/shard_map/ppermute | solution.py:330
  17.2 11.9 %collective-permute-start.6 = (bf16[832,128]{1,0:T(8,128)(2,1)S(1)}, bf16[832,128]{1,0:T(8,128)(2,1)S(1)}, u32[]{:S(2)}, u32[]{:S(2)}) collective-permute-start(bf16[832,128]{1,0:T(8,128)(2,1)S(1)} %get-tuple-element.56), channel_id=1, source_target_pairs={{0,3},{1,2},{2,1},{3,0},{4,7},{5,6},{6,5},{7,4},{8,11},{9,10},{10,... | collective-permute-start | bytes 638984 | tf_op jit(solution)/shard_map/ppermute | solution.py:330
  18.3 12.0 %collective-permute-start.5 = (bf16[832,128]{1,0:T(8,128)(2,1)S(1)}, bf16[832,128]{1,0:T(8,128)(2,1)S(1)}, u32[]{:S(2)}, u32[]{:S(2)}) collective-permute-start(bf16[832,128]{1,0:T(8,128)(2,1)S(1)} %get-tuple-element.51), channel_id=1, source_target_pairs={{0,7},{1,6},{2,5},{3,4},{4,3},{5,2},{6,1},{7,0},{8,15},{9,14},{10,... | collective-permute-start | bytes 638984 | tf_op jit(solution)/shard_map/ppermute | solution.py:330

commit v5 on v4

--- a/solution.py
+++ b/solution.py
@@ -99,7 +99,7 @@
 
 
 def block_start(line):
-    return pl.multiple_of(jnp.max(line) * BA, BA)
+    return pl.multiple_of(line[0, 0] * BA, BA)
 
 
 def even_kernel(plan, depth_tiles, cols, *refs):
@@ -210,7 +210,7 @@
         header = jnp.left_shift(code.astype(jnp.int32), 16) | wanted_ref[owner : owner + 1, :]
         message = jnp.concatenate([pairs, header], axis=0)
         for c in range(copies):
-            at = (c * plan.owners + owner) * size
+            at = (owner * copies + c) * size
             out_ref[at : at + size, :] = message
 
 
@@ -224,7 +224,7 @@
     def add(i, carry):
         part = messages_ref.at[pl.ds(pl.multiple_of(i * batch * size, 8), batch * size), :]
         headers = [part[d * size + half : (d + 1) * size, :] for d in range(batch)]
-        places = [pl.multiple_of(jnp.max(h & 0xFFFF) * BA, BA) for h in headers]
+        places = [pl.multiple_of((h[0, 0] & 0xFFFF) * BA, BA) for h in headers]
         for d in range(batch):
             code = jnp.right_shift(headers[d], 16).astype(jnp.float32)
             scale = jnp.exp2(code * (1.0 / STEPS_PER_OCTAVE)) * (1.0 / FULL)
@@ -344,7 +344,7 @@
         compiler_params=params(14 if small else 60),
         name="terms",
     )(*[held[s] for s in g], turned, bias, scale, total, wanted, *parts)
-    returned = lax.all_to_all(terms[:, None, :], ("samp", "arow", "acol"), 0, 0, tiled=True)[:, 0, :]
+    returned = lax.all_to_all(terms[:, None, :], ("arow", "acol", "samp"), 0, 0, tiled=True)[:, 0, :]
     result = pl.pallas_call(
         functools.partial(sum_kernel, cols),
         out_shape=struct((cols, shard), f32),

time: 55.7 us -> 54.9 us (0.986); the launches traced: 55.4 us -> 53.9 us
  blocking collectives: 21 us -> 19.9 us
    all_to_all x1, blocking collectives: 21 us -> 19.9 us  [per_device(): lax.all_to_all(terms[:, None, :], ('arow', 'acol', 'samp'), 0, 0, tiled=T...]
where the time goes in v5:
time: 54.9 us; the launch traced here: 53.9 us
  blocking collectives  19.9 us (36%)
  Pallas kernels  13.7 us (25%)
  starting transfers between devices  11.4 us (21%)
  waiting for transfers between devices  7.04 us (13%)
  local copies, waits for them, and re-layouts  1.75 us (3%)
    all_to_all x1, blocking collectives, per_device(): lax.all_to_all(terms[:, None, :], ('arow', 'acol', 'samp'), 0, 0, tiled=T...  19.9 us
    ppermute x7, starting transfers between devices, per_device(): held[s] = lax.ppermute(block, here, plan.pairs(s))  6.89 us
    ppermute x7, waiting for transfers between devices, per_device(): held[s] = lax.ppermute(block, here, plan.pairs(s))  5.43 us
    pallas_call x4, Pallas kernels, weigh(): pl.pallas_call(functools.partial(group_kernel, g, sizes), out_shape=(stru...  4.55 us
    ppermute x3, starting transfers between devices, per_device(): lax.ppermute(wanted, here, plan.pairs(s))  4.54 us
    pallas_call x1, Pallas kernels, per_device(): pl.pallas_call(functools.partial(last_kernel, plan, copies, groups, sizes...  2.73 us
    pallas_call x1, Pallas kernels, per_device(): pl.pallas_call(rows_kernel, out_shape=(struct((depth, rows), bf16), struc...  2.71 us
    pallas_call x1, Pallas kernels, per_device(): pl.pallas_call(stage_kernel, out_shape=(struct(anchors.shape, bf16), stru...  1.91 us
  transfers between devices with their start and end apart: 11, of which 3 were waited for; matrix products, arithmetic and copies ran while one was open for 0% of the time, Pallas kernels for 17%

profile of v5, /device:TPU:0, one launch (start us, length us, event | category | flops | bytes accessed | tf_op | source)
XLA Modules:
  0.0 53.9 jit_solution(3058003145613484909)
XLA Ops:
  0.0 0.8 %copy-done.2 = s32[1536,8]{0,1:T(8,128)S(1)} copy-done((s32[1536,8]{0,1:T(8,128)S(1)}, s32[1536,8]{0,1:T(8,128)}, u32[]{:S(2)}) %copy-start.2) | copy-done | bytes 49176
  0.8 0.3 prepare.1
  1.1 3.0 %collective-permute-start.2 = (s32[8,128]{1,0:T(8,128)S(1)}, s32[8,128]{1,0:T(8,128)S(1)}, u32[]{:S(2)}, u32[]{:S(2)}) collective-permute-start(s32[8,128]{1,0:T(8,128)S(1)} %get-tuple-element.41._.refs_0_.refs_5_), channel_id=1, source_target_pairs={{0,2},{1,3},{2,0},{3,1},{4,6},{5,7},{6,4},{7,5},{8,10},{9,11},{10,... | collective-permute-start | bytes 12296 | tf_op jit(solution)/shard_map/ppermute | solution.py:278
  4.1 1.5 %collective-permute-start.1 = (s32[8,128]{1,0:T(8,128)S(1)}, s32[8,128]{1,0:T(8,128)S(1)}, u32[]{:S(2)}, u32[]{:S(2)}) collective-permute-start(s32[8,128]{1,0:T(8,128)S(1)} %get-tuple-element.41._.refs_0_.refs_5_), channel_id=1, source_target_pairs={{0,4},{1,5},{2,6},{3,7},{4,0},{5,1},{6,2},{7,3},{8,12},{9,13},{10,... | collective-permute-start | bytes 12296 | tf_op jit(solution)/shard_map/ppermute | solution.py:278
  5.6 0.0 collective-permute-start
  5.6 0.9 %copy-done.1 = bf16[2048,64]{0,1:T(8,128)(2,1)S(1)} copy-done((bf16[2048,64]{0,1:T(8,128)(2,1)S(1)}, bf16[2048,64]{0,1:T(8,128)(2,1)}, u32[]{:S(2)}) %copy-start.1) | copy-done | bytes 262168
  6.6 1.9 %stage.1 = (bf16[2048,768]{1,0:T(8,128)(2,1)S(1)}, bf16[64,2048]{1,0:T(8,128)(2,1)S(1)}) custom-call(s32[8,128]{1,0:T(8,128)S(1)} %get-tuple-element.41._.refs_0_.refs_5_, bf16[2048,768]{1,0:T(8,128)(2,1)} %anchors_ref.1, bf16[64,2048]{1,0:T(8,128)(2,1)S(1)} %bitcast.9), custom_call_target="tpu_custom_call" | custom-call | flops 1 | bytes 1 | tf_op jit(solution)/shard_map/stage/pallas_call | solution.py:267
  8.5 0.0 collective-permute-done.2.refs_3_
  8.5 1.6 %collective-permute-done.refs_1_ = s32[8,128]{1,0:T(8,128)S(1)} collective-permute-done((s32[8,128]{1,0:T(8,128)S(1)}, s32[8,128]{1,0:T(8,128)S(1)}, u32[]{:S(2)}, u32[]{:S(2)}) %collective-permute-start) | collective-permute-done | bytes 4128 | tf_op jit(solution)/shard_map/ppermute | solution.py:278
  10.1 0.2 cut_even.1
  10.3 0.6 %collective-permute-start.9 = (bf16[832,128]{1,0:T(8,128)(2,1)S(1)}, bf16[832,128]{1,0:T(8,128)(2,1)S(1)}, u32[]{:S(2)}, u32[]{:S(2)}) collective-permute-start(bf16[832,128]{1,0:T(8,128)(2,1)S(1)} %get-tuple-element.60), channel_id=1, source_target_pairs={{0,4},{1,5},{2,6},{3,7},{4,0},{5,1},{6,2},{7,3},{8,12},{9,13},{10,... | collective-permute-start | bytes 638984 | tf_op jit(solution)/shard_map/ppermute | solution.py:330
  10.9 1.4 %collective-permute-start.4 = (bf16[832,128]{1,0:T(8,128)(2,1)S(1)}, bf16[832,128]{1,0:T(8,128)(2,1)S(1)}, u32[]{:S(2)}, u32[]{:S(2)}) collective-permute-start(bf16[832,128]{1,0:T(8,128)(2,1)S(1)} %get-tuple-element.50), channel_id=1, source_target_pairs={{0,2},{1,3},{2,0},{3,1},{4,6},{5,7},{6,4},{7,5},{8,10},{9,11},{10,... | collective-permute-start | bytes 638984 | tf_op jit(solution)/shard_map/ppermute | solution.py:330
  12.3 0.0 collective-permute-start.3
  12.3 1.6 %collective-permute-start.7 = (bf16[832,128]{1,0:T(8,128)(2,1)S(1)}, bf16[832,128]{1,0:T(8,128)(2,1)S(1)}, u32[]{:S(2)}, u32[]{:S(2)}) collective-permute-start(bf16[832,128]{1,0:T(8,128)(2,1)S(1)} %get-tuple-element.57), channel_id=1, source_target_pairs={{0,6},{1,7},{2,4},{3,5},{4,2},{5,3},{6,0},{7,1},{8,14},{9,15},{10,... | collective-permute-start | bytes 638984 | tf_op jit(solution)/shard_map/ppermute | solution.py:330
  13.9 0.0 collective-permute-done.3.passed_ref
  13.9 0.2 cut_odd.1
  14.1 2.2 %collective-permute-done.9.refs_1_ = bf16[832,128]{1,0:T(8,128)(2,1)S(1)} collective-permute-done((bf16[832,128]{1,0:T(8,128)(2,1)S(1)}, bf16[832,128]{1,0:T(8,128)(2,1)S(1)}, u32[]{:S(2)}, u32[]{:S(2)}) %collective-permute-start.9) | collective-permute-done | bytes 213024 | tf_op jit(solution)/shard_map/ppermute | solution.py:330
  16.2 0.8 %collective-permute-start.8 = (bf16[832,128]{1,0:T(8,128)(2,1)S(1)}, bf16[832,128]{1,0:T(8,128)(2,1)S(1)}, u32[]{:S(2)}, u32[]{:S(2)}) collective-permute-start(bf16[832,128]{1,0:T(8,128)(2,1)S(1)} %get-tuple-element.58), channel_id=1, source_target_pairs={{0,5},{1,4},{2,7},{3,6},{4,1},{5,0},{6,3},{7,2},{8,13},{9,12},{10,... | collective-permute-start | bytes 638984 | tf_op jit(solution)/shard_map/ppermute | solution.py:330
  17.0 1.1 %collective-permute-start.6 = (bf16[832,128]{1,0:T(8,128)(2,1)S(1)}, bf16[832,128]{1,0:T(8,128)(2,1)S(1)}, u32[]{:S(2)}, u32[]{:S(2)}) collective-permute-start(bf16[832,128]{1,0:T(8,128)(2,1)S(1)} %get-tuple-element.56), channel_id=1, source_target_pairs={{0,3},{1,2},{2,1},{3,0},{4,7},{5,6},{6,5},{7,4},{8,11},{9,10},{10,... | collective-permute-start | bytes 638984 | tf_op jit(solution)/shard_map/ppermute | solution.py:330
  18.1 0.0 collective-permute-done.4.refs_1_
  18.1 1.4 %collective-permute-start.5 = (bf16[832,128]{1,0:T(8,128)(2,1)S(1)}, bf16[832,128]{1,0:T(8,128)(2,1)S(1)}, u32[]{:S(2)}, u32[]{:S(2)}) collective-permute-start(bf16[832,128]{1,0:T(8,128)(2,1)S(1)} %get-tuple-element.51), channel_id=1, source_target_pairs={{0,7},{1,6},{2,5},{3,4},{4,3},{5,2},{6,1},{7,0},{8,15},{9,14},{10,... | collective-permute-start | bytes 638984 | tf_op jit(solution)/shard_map/ppermute | solution.py:330
  19.6 2.7 %rows.1 = (bf16[768,1536]{1,0:T(8,128)(2,1)S(1)}, f32[8,1536]{1,0:T(8,128)S(1)}, bf16[1024,1536]{1,0:T(8,128)(2,1)S(1)}) custom-call(bf16[1536,768]{1,0:T(8,128)(2,1)S(1)} %copy-done, s32[8,1536]{1,0:T(8,128)S(1)} %get-tuple-element.52.slot_ref), custom_call_target="tpu_custom_call" | custom-call | flops 1 | bytes 1 | tf_op jit(solution)/shard_map/rows/pallas_call | solution.py:300
  22.3 1.3 %weights.4 = (f32[128,1536]{1,0:T(8,128)S(1)}, bf16[256,1536]{1,0:T(8,128)(2,1)S(1)}, bf16[256,1536]{1,0:T(8,128)(2,1)S(1)}) custom-call(bf16[832,128]{1,0:T(8,128)(2,1)S(1)} %get-tuple-element.62.refs_0_, bf16[832,128]{1,0:T(8,128)(2,1)S(1)} %collective-permute-done.4.refs_1_, bf16[768,1536]{1,0:T(8,128)(2,1)S(1)} %get-tuple-element.53.refs_2_.refs_1_, ...), custom_call_target="tpu_custom_call" | custom-call | flops 1 | bytes 1 | tf_op jit(solution)/shard_map/weights/pallas_call | solution.py:314
  23.5 0.0 collective-permute-done.10.refs_0_
  23.5 1.3 %weights.5 = (f32[128,1536]{1,0:T(8,128)S(1)}, bf16[256,1536]{1,0:T(8,128)(2,1)S(1)}, bf16[256,1536]{1,0:T(8,128)(2,1)S(1)}) custom-call(bf16[832,128]{1,0:T(8,128)(2,1)S(1)} %collective-permute-done.10.refs_0_, bf16[832,128]{1,0:T(8,128)(2,1)S(1)} %collective-permute-done.9.refs_1_, bf16[768,1536]{1,0:T(8,128)(2,1)S(1)} %get-tuple-element.53.refs_2_.refs_1_, ...), custom_call_target="tpu_custom_call" | custom-call | flops 1 | bytes 1 | tf_op jit(solution)/shard_map/weights/pallas_call | solution.py:314
  24.8 3.3 %collective-permute-done.8.refs_0_ = bf16[832,128]{1,0:T(8,128)(2,1)S(1)} collective-permute-done((bf16[832,128]{1,0:T(8,128)(2,1)S(1)}, bf16[832,128]{1,0:T(8,128)(2,1)S(1)}, u32[]{:S(2)}, u32[]{:S(2)}) %collective-permute-start.8) | collective-permute-done | bytes 213024 | tf_op jit(solution)/shard_map/ppermute | solution.py:330
  28.1 0.8 %weights.6 = (f32[128,1536]{1,0:T(8,128)S(1)}, bf16[128,1536]{1,0:T(8,128)(2,1)S(1)}, bf16[128,1536]{1,0:T(8,128)(2,1)S(1)}) custom-call(bf16[832,128]{1,0:T(8,128)(2,1)S(1)} %collective-permute-done.8.refs_0_, bf16[768,1536]{1,0:T(8,128)(2,1)S(1)} %get-tuple-element.53.refs_2_.refs_1_, bf16[1024,1536]{1,0:T(8,128)(2,1)S(1)} %get-tuple-element.54.refs_3_.refs_2_, ...), custom_call_target="tpu_custom_call" | custom-call | flops 1 | bytes 1 | tf_op jit(solution)/shard_map/weights/pallas_call | solution.py:314
  28.9 0.0 collective-permute-done.6.refs_0_
  28.9 1.2 %weights.7 = (f32[128,1536]{1,0:T(8,128)S(1)}, bf16[256,1536]{1,0:T(8,128)(2,1)S(1)}, bf16[256,1536]{1,0:T(8,128)(2,1)S(1)}) custom-call(bf16[832,128]{1,0:T(8,128)(2,1)S(1)} %collective-permute-done.6.refs_0_, bf16[832,128]{1,0:T(8,128)(2,1)S(1)} %collective-permute-done.7.refs_1_, bf16[768,1536]{1,0:T(8,128)(2,1)S(1)} %get-tuple-element.53.refs_2_.refs_1_, ...), custom_call_target="tpu_custom_call" | custom-call | flops 1 | bytes 1 | tf_op jit(solution)/shard_map/weights/pallas_call | solution.py:314
  30.2 2.7 %terms.1 = s32[1056,128]{1,0:T(8,128)S(1)} custom-call(bf16[832,128]{1,0:T(8,128)(2,1)S(1)} %collective-permute-done.5.refs_0_, bf16[768,1536]{1,0:T(8,128)(2,1)S(1)} %get-tuple-element.53.refs_2_.refs_1_, bf16[1024,1536]{1,0:T(8,128)(2,1)S(1)} %get-tuple-element.54.refs_3_.refs_2_, f32[8,1536]{1,0:T(8,128)S(1)} %get-tuple-element.55.refs_4_.refs_3_, ...), custom_call_target="tpu_custom_call" | custom-call | flops 1 | bytes 1 | tf_op jit(solution)/shard_map/terms/pallas_call | solution.py:337
  32.9 19.9 %all_to_all.5 = s32[1056,1,128]{2,1,0:T(1,128)S(1)} all-to-all(s32[1056,1,128]{2,1,0:T(1,128)S(1)} %bitcast.7), channel_id=1, replica_groups=mesh['samp'=4,'arow'=4,'acol'=2] {'arow','acol','samp'}, dimensions={0} | all-to-all | bytes 1081344 | tf_op jit(solution)/shard_map/all_to_all | solution.py:347
  52.8 1.1 %sum_terms.1 = f32[64,2048]{1,0:T(8,128)} custom-call(s32[1056,128]{1,0:T(8,128)S(1)} %bitcast.8), custom_call_target="tpu_custom_call" | custom-call | tf_op jit(solution)/shard_map/sum_terms/pallas_call | solution.py:348
  (8 shorter events, 0.0 us)
Async XLA Ops:
  0.0 0.8 %copy-start.2 = (s32[1536,8]{0,1:T(8,128)S(1)}, s32[1536,8]{0,1:T(8,128)}, u32[]{:S(2)}) copy-start(s32[1536,8]{0,1:T(8,128)} %param.7) | copy-start | bytes 147460
  1.1 7.4 %collective-permute-start.2 = (s32[8,128]{1,0:T(8,128)S(1)}, s32[8,128]{1,0:T(8,128)S(1)}, u32[]{:S(2)}, u32[]{:S(2)}) collective-permute-start(s32[8,128]{1,0:T(8,128)S(1)} %get-tuple-element.41._.refs_0_.refs_5_), channel_id=1, source_target_pairs={{0,2},{1,3},{2,0},{3,1},{4,6},{5,7},{6,4},{7,5},{8,10},{9,11},{10,... | collective-permute-start | bytes 12296 | tf_op jit(solution)/shard_map/ppermute | solution.py:278
  4.1 4.4 %collective-permute-start.1 = (s32[8,128]{1,0:T(8,128)S(1)}, s32[8,128]{1,0:T(8,128)S(1)}, u32[]{:S(2)}, u32[]{:S(2)}) collective-permute-start(s32[8,128]{1,0:T(8,128)S(1)} %get-tuple-element.41._.refs_0_.refs_5_), channel_id=1, source_target_pairs={{0,4},{1,5},{2,6},{3,7},{4,0},{5,1},{6,2},{7,3},{8,12},{9,13},{10,... | collective-permute-start | bytes 12296 | tf_op jit(solution)/shard_map/ppermute | solution.py:278
  5.6 4.5 %collective-permute-start = (s32[8,128]{1,0:T(8,128)S(1)}, s32[8,128]{1,0:T(8,128)S(1)}, u32[]{:S(2)}, u32[]{:S(2)}) collective-permute-start(s32[8,128]{1,0:T(8,128)S(1)} %get-tuple-element.41._.refs_0_.refs_5_), channel_id=1, source_target_pairs={{0,6},{1,7},{2,4},{3,5},{4,2},{5,3},{6,0},{7,1},{8,14},{9,15},{10,... | collective-permute-start | bytes 12296 | tf_op jit(solution)/shard_map/ppermute | solution.py:278
  5.6 0.9 %copy-start.1 = (bf16[2048,64]{0,1:T(8,128)(2,1)S(1)}, bf16[2048,64]{0,1:T(8,128)(2,1)}, u32[]{:S(2)}) copy-start(bf16[2048,64]{0,1:T(8,128)(2,1)} %param.6) | copy-start | bytes 786436
  10.1 9.5 %copy-start = (bf16[1536,768]{1,0:T(8,128)(2,1)S(1)}, bf16[1536,768]{1,0:T(8,128)(2,1)}, u32[]{:S(2)}) copy-start(bf16[1536,768]{1,0:T(8,128)(2,1)} %rows_ref.1) | copy-start | bytes 7077892
  10.3 5.9 %collective-permute-start.9 = (bf16[832,128]{1,0:T(8,128)(2,1)S(1)}, bf16[832,128]{1,0:T(8,128)(2,1)S(1)}, u32[]{:S(2)}, u32[]{:S(2)}) collective-permute-start(bf16[832,128]{1,0:T(8,128)(2,1)S(1)} %get-tuple-element.60), channel_id=1, source_target_pairs={{0,4},{1,5},{2,6},{3,7},{4,0},{5,1},{6,2},{7,3},{8,12},{9,13},{10,... | collective-permute-start | bytes 638984 | tf_op jit(solution)/shard_map/ppermute | solution.py:330
  10.9 7.3 %collective-permute-start.4 = (bf16[832,128]{1,0:T(8,128)(2,1)S(1)}, bf16[832,128]{1,0:T(8,128)(2,1)S(1)}, u32[]{:S(2)}, u32[]{:S(2)}) collective-permute-start(bf16[832,128]{1,0:T(8,128)(2,1)S(1)} %get-tuple-element.50), channel_id=1, source_target_pairs={{0,2},{1,3},{2,0},{3,1},{4,6},{5,7},{6,4},{7,5},{8,10},{9,11},{10,... | collective-permute-start | bytes 638984 | tf_op jit(solution)/shard_map/ppermute | solution.py:330
  12.3 1.6 %collective-permute-start.3 = (s32[8,128]{1,0:T(8,128)S(1)}, s32[8,128]{1,0:T(8,128)S(1)}, u32[]{:S(2)}, u32[]{:S(2)}) collective-permute-start(s32[8,128]{1,0:T(8,128)S(1)} %get-tuple-element.44), channel_id=1, source_target_pairs={{0,1},{1,0},{2,3},{3,2},{4,5},{5,4},{6,7},{7,6},{8,9},{9,8},{10,11... | collective-permute-start | bytes 12296 | tf_op jit(solution)/shard_map/ppermute | solution.py:288
  12.3 16.6 %collective-permute-start.7 = (bf16[832,128]{1,0:T(8,128)(2,1)S(1)}, bf16[832,128]{1,0:T(8,128)(2,1)S(1)}, u32[]{:S(2)}, u32[]{:S(2)}) collective-permute-start(bf16[832,128]{1,0:T(8,128)(2,1)S(1)} %get-tuple-element.57), channel_id=1, source_target_pairs={{0,6},{1,7},{2,4},{3,5},{4,2},{5,3},{6,0},{7,1},{8,14},{9,15},{10,... | collective-permute-start | bytes 638984 | tf_op jit(solution)/shard_map/ppermute | solution.py:330
  16.2 7.3 %collective-permute-start.10 = (bf16[832,128]{1,0:T(8,128)(2,1)S(1)}, bf16[832,128]{1,0:T(8,128)(2,1)S(1)}, u32[]{:S(2)}, u32[]{:S(2)}) collective-permute-start(bf16[832,128]{1,0:T(8,128)(2,1)S(1)} %get-tuple-element.61), channel_id=1, source_target_pairs={{0,1},{1,0},{2,3},{3,2},{4,5},{5,4},{6,7},{7,6},{8,9},{9,8},{10,11... | collective-permute-start | bytes 638984 | tf_op jit(solution)/shard_map/ppermute | solution.py:330
  16.2 11.9 %collective-permute-start.8 = (bf16[832,128]{1,0:T(8,128)(2,1)S(1)}, bf16[832,128]{1,0:T(8,128)(2,1)S(1)}, u32[]{:S(2)}, u32[]{:S(2)}) collective-permute-start(bf16[832,128]{1,0:T(8,128)(2,1)S(1)} %get-tuple-element.58), channel_id=1, source_target_pairs={{0,5},{1,4},{2,7},{3,6},{4,1},{5,0},{6,3},{7,2},{8,13},{9,12},{10,... | collective-permute-start | bytes 638984 | tf_op jit(solution)/shard_map/ppermute | solution.py:330
  17.0 11.8 %collective-permute-start.6 = (bf16[832,128]{1,0:T(8,128)(2,1)S(1)}, bf16[832,128]{1,0:T(8,128)(2,1)S(1)}, u32[]{:S(2)}, u32[]{:S(2)}) collective-permute-start(bf16[832,128]{1,0:T(8,128)(2,1)S(1)} %get-tuple-element.56), channel_id=1, source_target_pairs={{0,3},{1,2},{2,1},{3,0},{4,7},{5,6},{6,5},{7,4},{8,11},{9,10},{10,... | collective-permute-start | bytes 638984 | tf_op jit(solution)/shard_map/ppermute | solution.py:330
  18.1 12.0 %collective-permute-start.5 = (bf16[832,128]{1,0:T(8,128)(2,1)S(1)}, bf16[832,128]{1,0:T(8,128)(2,1)S(1)}, u32[]{:S(2)}, u32[]{:S(2)}) collective-permute-start(bf16[832,128]{1,0:T(8,128)(2,1)S(1)} %get-tuple-element.51), channel_id=1, source_target_pairs={{0,7},{1,6},{2,5},{3,4},{4,3},{5,2},{6,1},{7,0},{8,15},{9,14},{10,... | collective-permute-start | bytes 638984 | tf_op jit(solution)/shard_map/ppermute | solution.py:330

commit v6 on v5

--- a/solution.py
+++ b/solution.py
@@ -15,7 +15,6 @@
 MISS = -1e30
 ORDER = [(2, 0), (4, 0), (6, 0), (3, 0), (5, 0), (7, 2), (1, 4)]
 GROUPS = [[0, 2], [1, 4], [5], [3, 6], [7]]
-LIMIT_STAGE = 49
 IN_FLIGHT = 5
 FULL = 32704.0
 STEPS_PER_OCTAVE = 256.0
@@ -25,6 +24,7 @@
 SMEM = pl.BlockSpec(memory_space=pltpu.SMEM)
 ANY = pl.BlockSpec(memory_space=pl.ANY)
 HBM = pl.BlockSpec(memory_space=pltpu.HBM)
+LONG = pl.CostEstimate(flops=2**33, bytes_accessed=2**22, transcendentals=0)
 QUICK = pl.CostEstimate(flops=1, bytes_accessed=1, transcendentals=0)
 
 
@@ -49,7 +49,7 @@
         return lax.axis_index("arow") * self.cols + lax.axis_index("acol")
 
     def even(self):
-        return [0, *range(self.owners - 2, 0, -2)]
+        return list(range(0, self.owners, 2))
 
     def odd(self):
         return list(range(1, self.owners, 2))
@@ -57,7 +57,7 @@
     def order(self):
         if self.owners == 8:
             return ORDER
-        steps = [*self.even()[:0:-1], *self.odd()]
+        steps = [*self.even()[1:], *self.odd()]
         return [(s, steps[i - IN_FLIGHT] if i >= IN_FLIGHT else 0) for i, s in enumerate(steps)]
 
     def groups(self):
@@ -78,17 +78,6 @@
     for o in range(plan.owners):
         picked = jnp.where(owner == o, block, 0)
         wanted_ref[o : o + 1, :] = jnp.full((1, LANES), jnp.max(picked), jnp.int32)
-
-
-def stage_kernel(_, anchors_ref, panel_ref, anchors_out, panel_out, sem):
-    copies = [
-        pltpu.make_async_copy(anchors_ref, anchors_out, sem.at[0]),
-        pltpu.make_async_copy(panel_ref, panel_out, sem.at[1]),
-    ]
-    for copy in copies:
-        copy.start()
-    for copy in copies:
-        copy.wait()
 
 
 def cut(starts, depth_tiles, cols, anchors_ref, panel_ref, out):
@@ -255,6 +244,7 @@
         out_shape=(struct((cand, rows), i32), struct((owners, LANES), i32)),
         in_specs=[VMEM],
         out_specs=(VMEM, VMEM),
+        cost_estimate=LONG,
         compiler_params=params(4),
         name="prepare",
     )(nearest.T)
@@ -264,16 +254,6 @@
     message = struct((depth_tiles * BA + cols, LANES), bf16)
     even, odd = plan.even(), plan.odd()
     half = len(even)
-    staged = pl.pallas_call(
-        stage_kernel,
-        out_shape=(struct(anchors.shape, bf16), struct(panel.shape, bf16)),
-        in_specs=[VMEM, HBM, HBM],
-        out_specs=(VMEM, VMEM),
-        scratch_shapes=[pltpu.SemaphoreType.DMA((2,))],
-        cost_estimate=QUICK,
-        compiler_params=params(LIMIT_STAGE),
-        name="stage",
-    )(wanted, anchors, panel)
     passed = struct((-(-half // 8) * 8, LANES), i32)
     asked = [wanted, *(lax.ppermute(wanted, here, plan.pairs(s)) for s in even[1:])]
     *sent_even, passed = pl.pallas_call(
@@ -284,7 +264,7 @@
         cost_estimate=QUICK,
         compiler_params=params(4),
         name="cut_even",
-    )(*asked, *staged)
+    )(*asked, anchors, panel)
     passed = lax.ppermute(passed, here, plan.pairs(1))
     sent_odd = pl.pallas_call(
         functools.partial(odd_kernel, plan, depth_tiles, cols),
@@ -294,7 +274,7 @@
         cost_estimate=QUICK,
         compiler_params=params(4),
         name="cut_odd",
-    )(passed, *staged)
+    )(passed, anchors, panel)
     slot, *sent_odd = lax.optimization_barrier((slot, *sent_odd))
     sent = {**dict(zip(even, sent_even)), **dict(zip(odd, sent_odd))}
     turned, scale, bias = pl.pallas_call(

time: 54.9 us -> 54.1 us (0.985)
  waiting for transfers between devices: 7.04 us -> 9.62 us
  Pallas kernels: 13.7 us -> 11.8 us
  local copies, waits for them, and re-layouts: 1.75 us -> 0.81 us
    pallas_call x1 -> x0, Pallas kernels: 1.91 us -> none  [per_device(): pl.pallas_call(stage_kernel, out_shape=(struct(anchors.shape, bf16), stru...]
    ppermute x3, waiting for transfers between devices: 1.6 us -> 3.47 us  [per_device(): lax.ppermute(wanted, here, plan.pairs(s))]
    unnamed x6 -> x8, local copies, waits for them, and re-layouts: 1.75 us -> 0.81 us
    ppermute x7, waiting for transfers between devices: 5.43 us -> 6.15 us  [per_device(): held[s] = lax.ppermute(block, here, plan.pairs(s))]
  transfers between devices with their start and end apart: 11 -> 11, of which waited for: 3 -> 7; matrix products, arithmetic and copies ran while one was open for 0% -> 0% of each run, Pallas kernels for 17% -> 14%
where the time goes in v6:
time: 54.1 us; the launch traced here: 53.2 us
  blocking collectives  19.7 us (36%)
  Pallas kernels  11.8 us (22%)
  starting transfers between devices  11.2 us (21%)
  waiting for transfers between devices  9.62 us (18%)
  local copies, waits for them, and re-layouts  0.81 us (1%)
    all_to_all x1, blocking collectives, per_device(): lax.all_to_all(terms[:, None, :], ('arow', 'acol', 'samp'), 0, 0, tiled=T...  19.7 us
    ppermute x7, starting transfers between devices, per_device(): held[s] = lax.ppermute(block, here, plan.pairs(s))  6.55 us
    ppermute x7, waiting for transfers between devices, per_device(): held[s] = lax.ppermute(block, here, plan.pairs(s))  6.15 us
    ppermute x3, starting transfers between devices, per_device(): lax.ppermute(wanted, here, plan.pairs(s))  4.6 us
    pallas_call x4, Pallas kernels, weigh(): pl.pallas_call(functools.partial(group_kernel, g, sizes), out_shape=(stru...  4.55 us
    ppermute x3, waiting for transfers between devices, per_device(): lax.ppermute(wanted, here, plan.pairs(s))  3.47 us
    pallas_call x1, Pallas kernels, per_device(): pl.pallas_call(functools.partial(last_kernel, plan, copies, groups, sizes...  2.72 us
    pallas_call x1, Pallas kernels, per_device(): pl.pallas_call(rows_kernel, out_shape=(struct((depth, rows), bf16), struc...  2.71 us
  transfers between devices with their start and end apart: 11, of which 7 were waited for; matrix products, arithmetic and copies ran while one was open for 0% of the time, Pallas kernels for 14%

profile of v6, /device:TPU:0, one launch (start us, length us, event | category | flops | bytes accessed | tf_op | source)
XLA Modules:
  0.0 53.2 jit_solution(311072959989483835)
XLA Ops:
  0.0 0.8 %copy-done.3 = s32[1536,8]{0,1:T(8,128)S(1)} copy-done((s32[1536,8]{0,1:T(8,128)S(1)}, s32[1536,8]{0,1:T(8,128)}, u32[]{:S(2)}) %copy-start.3) | copy-done | bytes 49176
  0.8 0.3 prepare.1
  1.1 4.0 %collective-permute-start.2 = (s32[8,128]{1,0:T(8,128)S(1)}, s32[8,128]{1,0:T(8,128)S(1)}, u32[]{:S(2)}, u32[]{:S(2)}) collective-permute-start(s32[8,128]{1,0:T(8,128)S(1)} %get-tuple-element.39.refs_0_.refs_5_), channel_id=1, source_target_pairs={{0,6},{1,7},{2,4},{3,5},{4,2},{5,3},{6,0},{7,1},{8,14},{9,15},{10,... | collective-permute-start | bytes 12296 | tf_op jit(solution)/shard_map/ppermute | solution.py:258
  5.0 0.5 collective-permute-start.1
  5.5 0.1 collective-permute-start
  5.7 0.9 %collective-permute-done.2.refs_3_ = s32[8,128]{1,0:T(8,128)S(1)} collective-permute-done((s32[8,128]{1,0:T(8,128)S(1)}, s32[8,128]{1,0:T(8,128)S(1)}, u32[]{:S(2)}, u32[]{:S(2)}) %collective-permute-start.2) | collective-permute-done | bytes 4128 | tf_op jit(solution)/shard_map/ppermute | solution.py:258
  6.6 2.0 %collective-permute-done.1.refs_2_ = s32[8,128]{1,0:T(8,128)S(1)} collective-permute-done((s32[8,128]{1,0:T(8,128)S(1)}, s32[8,128]{1,0:T(8,128)S(1)}, u32[]{:S(2)}, u32[]{:S(2)}) %collective-permute-start.1) | collective-permute-done | bytes 4128 | tf_op jit(solution)/shard_map/ppermute | solution.py:258
  8.6 0.5 collective-permute-done.refs_1_
  9.2 0.2 cut_even.1
  9.4 1.6 %collective-permute-start.9 = (bf16[832,128]{1,0:T(8,128)(2,1)S(1)}, bf16[832,128]{1,0:T(8,128)(2,1)S(1)}, u32[]{:S(2)}, u32[]{:S(2)}) collective-permute-start(bf16[832,128]{1,0:T(8,128)(2,1)S(1)} %get-tuple-element.56), channel_id=1, source_target_pairs={{0,4},{1,5},{2,6},{3,7},{4,0},{5,1},{6,2},{7,3},{8,12},{9,13},{10,... | collective-permute-start | bytes 638984 | tf_op jit(solution)/shard_map/ppermute | solution.py:310
  10.9 0.5 %collective-permute-start.4 = (bf16[832,128]{1,0:T(8,128)(2,1)S(1)}, bf16[832,128]{1,0:T(8,128)(2,1)S(1)}, u32[]{:S(2)}, u32[]{:S(2)}) collective-permute-start(bf16[832,128]{1,0:T(8,128)(2,1)S(1)} %get-tuple-element.46), channel_id=1, source_target_pairs={{0,2},{1,3},{2,0},{3,1},{4,6},{5,7},{6,4},{7,5},{8,10},{9,11},{10,... | collective-permute-start | bytes 638984 | tf_op jit(solution)/shard_map/ppermute | solution.py:310
  11.5 0.0 collective-permute-start.3
  11.5 1.4 %collective-permute-start.7 = (bf16[832,128]{1,0:T(8,128)(2,1)S(1)}, bf16[832,128]{1,0:T(8,128)(2,1)S(1)}, u32[]{:S(2)}, u32[]{:S(2)}) collective-permute-start(bf16[832,128]{1,0:T(8,128)(2,1)S(1)} %get-tuple-element.53), channel_id=1, source_target_pairs={{0,6},{1,7},{2,4},{3,5},{4,2},{5,3},{6,0},{7,1},{8,14},{9,15},{10,... | collective-permute-start | bytes 638984 | tf_op jit(solution)/shard_map/ppermute | solution.py:310
  12.9 0.2 cut_odd.1
  13.1 2.2 %collective-permute-done.9.refs_1_ = bf16[832,128]{1,0:T(8,128)(2,1)S(1)} collective-permute-done((bf16[832,128]{1,0:T(8,128)(2,1)S(1)}, bf16[832,128]{1,0:T(8,128)(2,1)S(1)}, u32[]{:S(2)}, u32[]{:S(2)}) %collective-permute-start.9) | collective-permute-done | bytes 213024 | tf_op jit(solution)/shard_map/ppermute | solution.py:310
  15.3 0.0 collective-permute-start.10
  15.3 2.7 %collective-permute-start.8 = (bf16[832,128]{1,0:T(8,128)(2,1)S(1)}, bf16[832,128]{1,0:T(8,128)(2,1)S(1)}, u32[]{:S(2)}, u32[]{:S(2)}) collective-permute-start(bf16[832,128]{1,0:T(8,128)(2,1)S(1)} %get-tuple-element.54), channel_id=1, source_target_pairs={{0,5},{1,4},{2,7},{3,6},{4,1},{5,0},{6,3},{7,2},{8,13},{9,12},{10,... | collective-permute-start | bytes 638984 | tf_op jit(solution)/shard_map/ppermute | solution.py:310
  18.1 0.0 collective-permute-start.6
  18.1 0.8 %collective-permute-done.4.refs_1_ = bf16[832,128]{1,0:T(8,128)(2,1)S(1)} collective-permute-done((bf16[832,128]{1,0:T(8,128)(2,1)S(1)}, bf16[832,128]{1,0:T(8,128)(2,1)S(1)}, u32[]{:S(2)}, u32[]{:S(2)}) %collective-permute-start.4) | collective-permute-done | bytes 213024 | tf_op jit(solution)/shard_map/ppermute | solution.py:310
  18.9 0.3 collective-permute-start.5
  19.2 2.7 %rows.1 = (bf16[768,1536]{1,0:T(8,128)(2,1)S(1)}, f32[8,1536]{1,0:T(8,128)S(1)}, bf16[1024,1536]{1,0:T(8,128)(2,1)S(1)}) custom-call(bf16[1536,768]{1,0:T(8,128)(2,1)S(1)} %copy-done.1, s32[8,1536]{1,0:T(8,128)S(1)} %get-tuple-element.48.slot_ref), custom_call_target="tpu_custom_call" | custom-call | flops 1 | bytes 1 | tf_op jit(solution)/shard_map/rows/pallas_call | solution.py:280
  21.9 1.3 %weights.4 = (f32[128,1536]{1,0:T(8,128)S(1)}, bf16[256,1536]{1,0:T(8,128)(2,1)S(1)}, bf16[256,1536]{1,0:T(8,128)(2,1)S(1)}) custom-call(bf16[832,128]{1,0:T(8,128)(2,1)S(1)} %get-tuple-element.58.refs_0_, bf16[832,128]{1,0:T(8,128)(2,1)S(1)} %collective-permute-done.4.refs_1_, bf16[768,1536]{1,0:T(8,128)(2,1)S(1)} %get-tuple-element.49.refs_2_.refs_1_, ...), custom_call_target="tpu_custom_call" | custom-call | flops 1 | bytes 1 | tf_op jit(solution)/shard_map/weights/pallas_call | solution.py:294
  23.1 1.2 %weights.5 = (f32[128,1536]{1,0:T(8,128)S(1)}, bf16[256,1536]{1,0:T(8,128)(2,1)S(1)}, bf16[256,1536]{1,0:T(8,128)(2,1)S(1)}) custom-call(bf16[832,128]{1,0:T(8,128)(2,1)S(1)} %collective-permute-done.10.refs_0_, bf16[832,128]{1,0:T(8,128)(2,1)S(1)} %collective-permute-done.9.refs_1_, bf16[768,1536]{1,0:T(8,128)(2,1)S(1)} %get-tuple-element.49.refs_2_.refs_1_, ...), custom_call_target="tpu_custom_call" | custom-call | flops 1 | bytes 1 | tf_op jit(solution)/shard_map/weights/pallas_call | solution.py:294
  24.4 2.3 %collective-permute-done.8.refs_0_ = bf16[832,128]{1,0:T(8,128)(2,1)S(1)} collective-permute-done((bf16[832,128]{1,0:T(8,128)(2,1)S(1)}, bf16[832,128]{1,0:T(8,128)(2,1)S(1)}, u32[]{:S(2)}, u32[]{:S(2)}) %collective-permute-start.8) | collective-permute-done | bytes 213024 | tf_op jit(solution)/shard_map/ppermute | solution.py:310
  26.7 0.8 %weights.6 = (f32[128,1536]{1,0:T(8,128)S(1)}, bf16[128,1536]{1,0:T(8,128)(2,1)S(1)}, bf16[128,1536]{1,0:T(8,128)(2,1)S(1)}) custom-call(bf16[832,128]{1,0:T(8,128)(2,1)S(1)} %collective-permute-done.8.refs_0_, bf16[768,1536]{1,0:T(8,128)(2,1)S(1)} %get-tuple-element.49.refs_2_.refs_1_, bf16[1024,1536]{1,0:T(8,128)(2,1)S(1)} %get-tuple-element.50.refs_3_.refs_2_, ...), custom_call_target="tpu_custom_call" | custom-call | flops 1 | bytes 1 | tf_op jit(solution)/shard_map/weights/pallas_call | solution.py:294
  27.5 0.0 collective-permute-done.7.refs_1_
  27.5 0.0 collective-permute-done.6.refs_0_
  27.5 1.2 %weights.7 = (f32[128,1536]{1,0:T(8,128)S(1)}, bf16[256,1536]{1,0:T(8,128)(2,1)S(1)}, bf16[256,1536]{1,0:T(8,128)(2,1)S(1)}) custom-call(bf16[832,128]{1,0:T(8,128)(2,1)S(1)} %collective-permute-done.6.refs_0_, bf16[832,128]{1,0:T(8,128)(2,1)S(1)} %collective-permute-done.7.refs_1_, bf16[768,1536]{1,0:T(8,128)(2,1)S(1)} %get-tuple-element.49.refs_2_.refs_1_, ...), custom_call_target="tpu_custom_call" | custom-call | flops 1 | bytes 1 | tf_op jit(solution)/shard_map/weights/pallas_call | solution.py:294
  28.8 0.8 %collective-permute-done.5.refs_0_ = bf16[832,128]{1,0:T(8,128)(2,1)S(1)} collective-permute-done((bf16[832,128]{1,0:T(8,128)(2,1)S(1)}, bf16[832,128]{1,0:T(8,128)(2,1)S(1)}, u32[]{:S(2)}, u32[]{:S(2)}) %collective-permute-start.5) | collective-permute-done | bytes 213024 | tf_op jit(solution)/shard_map/ppermute | solution.py:310
  29.6 2.7 %terms.1 = s32[1056,128]{1,0:T(8,128)S(1)} custom-call(bf16[832,128]{1,0:T(8,128)(2,1)S(1)} %collective-permute-done.5.refs_0_, bf16[768,1536]{1,0:T(8,128)(2,1)S(1)} %get-tuple-element.49.refs_2_.refs_1_, bf16[1024,1536]{1,0:T(8,128)(2,1)S(1)} %get-tuple-element.50.refs_3_.refs_2_, f32[8,1536]{1,0:T(8,128)S(1)} %get-tuple-element.51.refs_4_.refs_3_, ...), custom_call_target="tpu_custom_call" | custom-call | flops 1 | bytes 1 | tf_op jit(solution)/shard_map/terms/pallas_call | solution.py:317
  32.3 19.7 %all_to_all.5 = s32[1056,1,128]{2,1,0:T(1,128)S(1)} all-to-all(s32[1056,1,128]{2,1,0:T(1,128)S(1)} %bitcast.7), channel_id=1, replica_groups=mesh['samp'=4,'arow'=4,'acol'=2] {'arow','acol','samp'}, dimensions={0} | all-to-all | bytes 1081344 | tf_op jit(solution)/shard_map/all_to_all | solution.py:327
  52.0 1.1 %sum_terms.1 = f32[64,2048]{1,0:T(8,128)} custom-call(s32[1056,128]{1,0:T(8,128)S(1)} %bitcast.8), custom_call_target="tpu_custom_call" | custom-call | tf_op jit(solution)/shard_map/sum_terms/pallas_call | solution.py:328
  (9 shorter events, 0.0 us)
Async XLA Ops:
  0.0 0.8 %copy-start.3 = (s32[1536,8]{0,1:T(8,128)S(1)}, s32[1536,8]{0,1:T(8,128)}, u32[]{:S(2)}) copy-start(s32[1536,8]{0,1:T(8,128)} %param.7) | copy-start | bytes 147460
  0.8 8.4 %copy-start = (bf16[2048,768]{1,0:T(8,128)(2,1)S(1)}, bf16[2048,768]{1,0:T(8,128)(2,1)}, u32[]{:S(2)}) copy-start(bf16[2048,768]{1,0:T(8,128)(2,1)} %anchors_ref.1) | copy-start | bytes 9437188
  0.8 8.4 %copy-start.2 = (bf16[2048,64]{0,1:T(8,128)(2,1)S(1)}, bf16[2048,64]{0,1:T(8,128)(2,1)}, u32[]{:S(2)}) copy-start(bf16[2048,64]{0,1:T(8,128)(2,1)} %param.6) | copy-start | bytes 786436
  1.1 5.5 %collective-permute-start.2 = (s32[8,128]{1,0:T(8,128)S(1)}, s32[8,128]{1,0:T(8,128)S(1)}, u32[]{:S(2)}, u32[]{:S(2)}) collective-permute-start(s32[8,128]{1,0:T(8,128)S(1)} %get-tuple-element.39.refs_0_.refs_5_), channel_id=1, source_target_pairs={{0,6},{1,7},{2,4},{3,5},{4,2},{5,3},{6,0},{7,1},{8,14},{9,15},{10,... | collective-permute-start | bytes 12296 | tf_op jit(solution)/shard_map/ppermute | solution.py:258
  5.0 3.6 %collective-permute-start.1 = (s32[8,128]{1,0:T(8,128)S(1)}, s32[8,128]{1,0:T(8,128)S(1)}, u32[]{:S(2)}, u32[]{:S(2)}) collective-permute-start(s32[8,128]{1,0:T(8,128)S(1)} %get-tuple-element.39.refs_0_.refs_5_), channel_id=1, source_target_pairs={{0,4},{1,5},{2,6},{3,7},{4,0},{5,1},{6,2},{7,3},{8,12},{9,13},{10,... | collective-permute-start | bytes 12296 | tf_op jit(solution)/shard_map/ppermute | solution.py:258
  5.5 3.6 %collective-permute-start = (s32[8,128]{1,0:T(8,128)S(1)}, s32[8,128]{1,0:T(8,128)S(1)}, u32[]{:S(2)}, u32[]{:S(2)}) collective-permute-start(s32[8,128]{1,0:T(8,128)S(1)} %get-tuple-element.39.refs_0_.refs_5_), channel_id=1, source_target_pairs={{0,2},{1,3},{2,0},{3,1},{4,6},{5,7},{6,4},{7,5},{8,10},{9,11},{10,... | collective-permute-start | bytes 12296 | tf_op jit(solution)/shard_map/ppermute | solution.py:258
  9.2 10.0 %copy-start.1 = (bf16[1536,768]{1,0:T(8,128)(2,1)S(1)}, bf16[1536,768]{1,0:T(8,128)(2,1)}, u32[]{:S(2)}) copy-start(bf16[1536,768]{1,0:T(8,128)(2,1)} %rows_ref.1) | copy-start | bytes 7077892
  9.4 6.0 %collective-permute-start.9 = (bf16[832,128]{1,0:T(8,128)(2,1)S(1)}, bf16[832,128]{1,0:T(8,128)(2,1)S(1)}, u32[]{:S(2)}, u32[]{:S(2)}) collective-permute-start(bf16[832,128]{1,0:T(8,128)(2,1)S(1)} %get-tuple-element.56), channel_id=1, source_target_pairs={{0,4},{1,5},{2,6},{3,7},{4,0},{5,1},{6,2},{7,3},{8,12},{9,13},{10,... | collective-permute-start | bytes 638984 | tf_op jit(solution)/shard_map/ppermute | solution.py:310
  10.9 8.0 %collective-permute-start.4 = (bf16[832,128]{1,0:T(8,128)(2,1)S(1)}, bf16[832,128]{1,0:T(8,128)(2,1)S(1)}, u32[]{:S(2)}, u32[]{:S(2)}) collective-permute-start(bf16[832,128]{1,0:T(8,128)(2,1)S(1)} %get-tuple-element.46), channel_id=1, source_target_pairs={{0,2},{1,3},{2,0},{3,1},{4,6},{5,7},{6,4},{7,5},{8,10},{9,11},{10,... | collective-permute-start | bytes 638984 | tf_op jit(solution)/shard_map/ppermute | solution.py:310
  11.5 1.4 %collective-permute-start.3 = (s32[8,128]{1,0:T(8,128)S(1)}, s32[8,128]{1,0:T(8,128)S(1)}, u32[]{:S(2)}, u32[]{:S(2)}) collective-permute-start(s32[8,128]{1,0:T(8,128)S(1)} %get-tuple-element.40), channel_id=1, source_target_pairs={{0,1},{1,0},{2,3},{3,2},{4,5},{5,4},{6,7},{7,6},{8,9},{9,8},{10,11... | collective-permute-start | bytes 12296 | tf_op jit(solution)/shard_map/ppermute | solution.py:268
  11.5 16.0 %collective-permute-start.7 = (bf16[832,128]{1,0:T(8,128)(2,1)S(1)}, bf16[832,128]{1,0:T(8,128)(2,1)S(1)}, u32[]{:S(2)}, u32[]{:S(2)}) collective-permute-start(bf16[832,128]{1,0:T(8,128)(2,1)S(1)} %get-tuple-element.53), channel_id=1, source_target_pairs={{0,6},{1,7},{2,4},{3,5},{4,2},{5,3},{6,0},{7,1},{8,14},{9,15},{10,... | collective-permute-start | bytes 638984 | tf_op jit(solution)/shard_map/ppermute | solution.py:310
  15.3 7.8 %collective-permute-start.10 = (bf16[832,128]{1,0:T(8,128)(2,1)S(1)}, bf16[832,128]{1,0:T(8,128)(2,1)S(1)}, u32[]{:S(2)}, u32[]{:S(2)}) collective-permute-start(bf16[832,128]{1,0:T(8,128)(2,1)S(1)} %get-tuple-element.57), channel_id=1, source_target_pairs={{0,1},{1,0},{2,3},{3,2},{4,5},{5,4},{6,7},{7,6},{8,9},{9,8},{10,11... | collective-permute-start | bytes 638984 | tf_op jit(solution)/shard_map/ppermute | solution.py:310
  15.3 11.3 %collective-permute-start.8 = (bf16[832,128]{1,0:T(8,128)(2,1)S(1)}, bf16[832,128]{1,0:T(8,128)(2,1)S(1)}, u32[]{:S(2)}, u32[]{:S(2)}) collective-permute-start(bf16[832,128]{1,0:T(8,128)(2,1)S(1)} %get-tuple-element.54), channel_id=1, source_target_pairs={{0,5},{1,4},{2,7},{3,6},{4,1},{5,0},{6,3},{7,2},{8,13},{9,12},{10,... | collective-permute-start | bytes 638984 | tf_op jit(solution)/shard_map/ppermute | solution.py:310
  18.1 9.4 %collective-permute-start.6 = (bf16[832,128]{1,0:T(8,128)(2,1)S(1)}, bf16[832,128]{1,0:T(8,128)(2,1)S(1)}, u32[]{:S(2)}, u32[]{:S(2)}) collective-permute-start(bf16[832,128]{1,0:T(8,128)(2,1)S(1)} %get-tuple-element.52), channel_id=1, source_target_pairs={{0,3},{1,2},{2,1},{3,0},{4,7},{5,6},{6,5},{7,4},{8,11},{9,10},{10,... | collective-permute-start | bytes 638984 | tf_op jit(solution)/shard_map/ppermute | solution.py:310
  18.9 10.7 %collective-permute-start.5 = (bf16[832,128]{1,0:T(8,128)(2,1)S(1)}, bf16[832,128]{1,0:T(8,128)(2,1)S(1)}, u32[]{:S(2)}, u32[]{:S(2)}) collective-permute-start(bf16[832,128]{1,0:T(8,128)(2,1)S(1)} %get-tuple-element.47), channel_id=1, source_target_pairs={{0,7},{1,6},{2,5},{3,4},{4,3},{5,2},{6,1},{7,0},{8,15},{9,14},{10,... | collective-permute-start | bytes 638984 | tf_op jit(solution)/shard_map/ppermute | solution.py:310

commit v7 on v6

--- a/solution.py
+++ b/solution.py
@@ -13,8 +13,8 @@
 TEMPERATURE = 0.05
 LANES = 128
 MISS = -1e30
-ORDER = [(2, 0), (4, 0), (6, 0), (3, 0), (5, 0), (7, 2), (1, 4)]
-GROUPS = [[0, 2], [1, 4], [5], [3, 6], [7]]
+ORDER = [(2, 0), (4, 0), (6, 0), (3, 0), (5, 0), (7, 4), (1, 4)]
+GROUPS = [[0, 2], [4], [1, 3], [5, 6], [7]]
 IN_FLIGHT = 5
 FULL = 32704.0
 STEPS_PER_OCTAVE = 256.0
@@ -149,6 +149,7 @@
     anchor_scale = jnp.concatenate(scales, axis=0)
     panel = jnp.concatenate(panels, axis=1)
     panel = jnp.concatenate([panel, jnp.ones((cols, count), jnp.bfloat16)], axis=0)
+    twice = jnp.concatenate([panel, panel], axis=1)
     for t in range(rows_ref.shape[1] // tile):
         span = slice(t * tile, (t + 1) * tile)
         dots = jnp.dot(block, rows_ref[:, span], preferred_element_type=jnp.float32)
@@ -158,8 +159,12 @@
         low_ref[:, span] = low
     for t in range(rows_ref.shape[1] // tile):
         span = slice(t * tile, (t + 1) * tile)
-        part = jnp.dot(panel, high_ref[:, span], preferred_element_type=jnp.float32)
-        part += jnp.dot(panel, low_ref[:, span], preferred_element_type=jnp.float32)
+        if count < 2 * BA:
+            weights = jnp.concatenate([high_ref[:, span], low_ref[:, span]], axis=0)
+            part = jnp.dot(twice, weights, preferred_element_type=jnp.float32)
+        else:
+            part = jnp.dot(panel, high_ref[:, span], preferred_element_type=jnp.float32)
+            part += jnp.dot(panel, low_ref[:, span], preferred_element_type=jnp.float32)
         total_ref[:, span] = part if before is None else before[:, span] + part
 
 

time: 54.1 us -> 54 us (level)
  blocking collectives: 19.7 us -> 18.3 us
  starting transfers between devices: 11.2 us -> 12 us
  waiting for transfers between devices: 9.62 us -> 10.2 us
    all_to_all x1, blocking collectives: 19.7 us -> 18.3 us  [per_device(): lax.all_to_all(terms[:, None, :], ('arow', 'acol', 'samp'), 0, 0, tiled=T...]
    ppermute x7, starting transfers between devices: 6.55 us -> 7.35 us  [per_device(): held[s] = lax.ppermute(block, here, plan.pairs(s))]
    ppermute x7, waiting for transfers between devices: 6.15 us -> 6.78 us  [per_device(): held[s] = lax.ppermute(block, here, plan.pairs(s))]
where the time goes in v7:
time: 54 us; the launch traced here: 53.1 us
  blocking collectives  18.3 us (34%)
  starting transfers between devices  12 us (22%)
  Pallas kernels  11.7 us (22%)
  waiting for transfers between devices  10.2 us (19%)
  local copies, waits for them, and re-layouts  0.81 us (2%)
    all_to_all x1, blocking collectives, per_device(): lax.all_to_all(terms[:, None, :], ('arow', 'acol', 'samp'), 0, 0, tiled=T...  18.3 us
    ppermute x7, starting transfers between devices, per_device(): held[s] = lax.ppermute(block, here, plan.pairs(s))  7.35 us
    ppermute x7, waiting for transfers between devices, per_device(): held[s] = lax.ppermute(block, here, plan.pairs(s))  6.78 us
    ppermute x3, starting transfers between devices, per_device(): lax.ppermute(wanted, here, plan.pairs(s))  4.6 us
    pallas_call x4, Pallas kernels, weigh(): pl.pallas_call(functools.partial(group_kernel, g, sizes), out_shape=(stru...  4.48 us
    ppermute x3, waiting for transfers between devices, per_device(): lax.ppermute(wanted, here, plan.pairs(s))  3.47 us
    pallas_call x1, Pallas kernels, per_device(): pl.pallas_call(rows_kernel, out_shape=(struct((depth, rows), bf16), struc...  2.71 us
    pallas_call x1, Pallas kernels, per_device(): pl.pallas_call(functools.partial(last_kernel, plan, copies, groups, sizes...  2.68 us
  transfers between devices with their start and end apart: 11, of which 7 were waited for; matrix products, arithmetic and copies ran while one was open for 0% of the time, Pallas kernels for 14%

profile of v7, /device:TPU:0, one launch (start us, length us, event | category | flops | bytes accessed | tf_op | source)
XLA Modules:
  0.0 53.1 jit_solution(9753142046318827933)
XLA Ops:
  0.0 0.8 %copy-done.3 = s32[1536,8]{0,1:T(8,128)S(1)} copy-done((s32[1536,8]{0,1:T(8,128)S(1)}, s32[1536,8]{0,1:T(8,128)}, u32[]{:S(2)}) %copy-start.3) | copy-done | bytes 49176
  0.8 0.3 prepare.1
  1.1 4.0 %collective-permute-start.2 = (s32[8,128]{1,0:T(8,128)S(1)}, s32[8,128]{1,0:T(8,128)S(1)}, u32[]{:S(2)}, u32[]{:S(2)}) collective-permute-start(s32[8,128]{1,0:T(8,128)S(1)} %get-tuple-element.39.refs_0_.refs_5_), channel_id=1, source_target_pairs={{0,6},{1,7},{2,4},{3,5},{4,2},{5,3},{6,0},{7,1},{8,14},{9,15},{10,... | collective-permute-start | bytes 12296 | tf_op jit(solution)/shard_map/ppermute | solution.py:263
  5.0 0.5 collective-permute-start.1
  5.5 0.1 collective-permute-start
  5.7 0.9 %collective-permute-done.2.refs_3_ = s32[8,128]{1,0:T(8,128)S(1)} collective-permute-done((s32[8,128]{1,0:T(8,128)S(1)}, s32[8,128]{1,0:T(8,128)S(1)}, u32[]{:S(2)}, u32[]{:S(2)}) %collective-permute-start.2) | collective-permute-done | bytes 4128 | tf_op jit(solution)/shard_map/ppermute | solution.py:263
  6.6 2.0 %collective-permute-done.1.refs_2_ = s32[8,128]{1,0:T(8,128)S(1)} collective-permute-done((s32[8,128]{1,0:T(8,128)S(1)}, s32[8,128]{1,0:T(8,128)S(1)}, u32[]{:S(2)}, u32[]{:S(2)}) %collective-permute-start.1) | collective-permute-done | bytes 4128 | tf_op jit(solution)/shard_map/ppermute | solution.py:263
  8.6 0.5 collective-permute-done.refs_1_
  9.2 0.2 cut_even.1
  9.4 1.6 %collective-permute-start.4 = (bf16[832,128]{1,0:T(8,128)(2,1)S(1)}, bf16[832,128]{1,0:T(8,128)(2,1)S(1)}, u32[]{:S(2)}, u32[]{:S(2)}) collective-permute-start(bf16[832,128]{1,0:T(8,128)(2,1)S(1)} %get-tuple-element.46), channel_id=1, source_target_pairs={{0,4},{1,5},{2,6},{3,7},{4,0},{5,1},{6,2},{7,3},{8,12},{9,13},{10,... | collective-permute-start | bytes 638984 | tf_op jit(solution)/shard_map/ppermute | solution.py:315
  10.9 0.5 %collective-permute-start.10 = (bf16[832,128]{1,0:T(8,128)(2,1)S(1)}, bf16[832,128]{1,0:T(8,128)(2,1)S(1)}, u32[]{:S(2)}, u32[]{:S(2)}) collective-permute-start(bf16[832,128]{1,0:T(8,128)(2,1)S(1)} %get-tuple-element.58), channel_id=1, source_target_pairs={{0,2},{1,3},{2,0},{3,1},{4,6},{5,7},{6,4},{7,5},{8,10},{9,11},{10,... | collective-permute-start | bytes 638984 | tf_op jit(solution)/shard_map/ppermute | solution.py:315
  11.5 0.0 collective-permute-start.3
  11.5 1.4 %collective-permute-start.7 = (bf16[832,128]{1,0:T(8,128)(2,1)S(1)}, bf16[832,128]{1,0:T(8,128)(2,1)S(1)}, u32[]{:S(2)}, u32[]{:S(2)}) collective-permute-start(bf16[832,128]{1,0:T(8,128)(2,1)S(1)} %get-tuple-element.53), channel_id=1, source_target_pairs={{0,6},{1,7},{2,4},{3,5},{4,2},{5,3},{6,0},{7,1},{8,14},{9,15},{10,... | collective-permute-start | bytes 638984 | tf_op jit(solution)/shard_map/ppermute | solution.py:315
  12.9 0.0 collective-permute-done.3.passed_ref
  12.9 0.2 cut_odd.1
  13.1 1.1 %collective-permute-start.9 = (bf16[832,128]{1,0:T(8,128)(2,1)S(1)}, bf16[832,128]{1,0:T(8,128)(2,1)S(1)}, u32[]{:S(2)}, u32[]{:S(2)}) collective-permute-start(bf16[832,128]{1,0:T(8,128)(2,1)S(1)} %get-tuple-element.56), channel_id=1, source_target_pairs={{0,3},{1,2},{2,1},{3,0},{4,7},{5,6},{6,5},{7,4},{8,11},{9,10},{10,... | collective-permute-start | bytes 638984 | tf_op jit(solution)/shard_map/ppermute | solution.py:315
  14.2 1.2 %collective-permute-done.4.refs_0_ = bf16[832,128]{1,0:T(8,128)(2,1)S(1)} collective-permute-done((bf16[832,128]{1,0:T(8,128)(2,1)S(1)}, bf16[832,128]{1,0:T(8,128)(2,1)S(1)}, u32[]{:S(2)}, u32[]{:S(2)}) %collective-permute-start.4) | collective-permute-done | bytes 213024 | tf_op jit(solution)/shard_map/ppermute | solution.py:315
  15.3 0.0 collective-permute-start.8
  15.3 2.7 %collective-permute-start.6 = (bf16[832,128]{1,0:T(8,128)(2,1)S(1)}, bf16[832,128]{1,0:T(8,128)(2,1)S(1)}, u32[]{:S(2)}, u32[]{:S(2)}) collective-permute-start(bf16[832,128]{1,0:T(8,128)(2,1)S(1)} %get-tuple-element.52), channel_id=1, source_target_pairs={{0,5},{1,4},{2,7},{3,6},{4,1},{5,0},{6,3},{7,2},{8,13},{9,12},{10,... | collective-permute-start | bytes 638984 | tf_op jit(solution)/shard_map/ppermute | solution.py:315
  18.1 1.0 %collective-permute-done.10.refs_1_ = bf16[832,128]{1,0:T(8,128)(2,1)S(1)} collective-permute-done((bf16[832,128]{1,0:T(8,128)(2,1)S(1)}, bf16[832,128]{1,0:T(8,128)(2,1)S(1)}, u32[]{:S(2)}, u32[]{:S(2)}) %collective-permute-start.10) | collective-permute-done | bytes 213024 | tf_op jit(solution)/shard_map/ppermute | solution.py:315
  19.1 2.7 %rows.1 = (bf16[768,1536]{1,0:T(8,128)(2,1)S(1)}, f32[8,1536]{1,0:T(8,128)S(1)}, bf16[1024,1536]{1,0:T(8,128)(2,1)S(1)}) custom-call(bf16[1536,768]{1,0:T(8,128)(2,1)S(1)} %copy-done.1, s32[8,1536]{1,0:T(8,128)S(1)} %get-tuple-element.48.slot_ref), custom_call_target="tpu_custom_call" | custom-call | flops 1 | bytes 1 | tf_op jit(solution)/shard_map/rows/pallas_call | solution.py:285
  21.8 1.3 %weights.4 = (f32[128,1536]{1,0:T(8,128)S(1)}, bf16[256,1536]{1,0:T(8,128)(2,1)S(1)}, bf16[256,1536]{1,0:T(8,128)(2,1)S(1)}) custom-call(bf16[832,128]{1,0:T(8,128)(2,1)S(1)} %get-tuple-element.57.refs_0_, bf16[832,128]{1,0:T(8,128)(2,1)S(1)} %collective-permute-done.10.refs_1_, bf16[768,1536]{1,0:T(8,128)(2,1)S(1)} %get-tuple-element.49.refs_2_.refs_1_, ...), custom_call_target="tpu_custom_call" | custom-call | flops 1 | bytes 1 | tf_op jit(solution)/shard_map/weights/pallas_call | solution.py:299
  23.1 0.8 %weights.5 = (f32[128,1536]{1,0:T(8,128)S(1)}, bf16[128,1536]{1,0:T(8,128)(2,1)S(1)}, bf16[128,1536]{1,0:T(8,128)(2,1)S(1)}) custom-call(bf16[832,128]{1,0:T(8,128)(2,1)S(1)} %collective-permute-done.4.refs_0_, bf16[768,1536]{1,0:T(8,128)(2,1)S(1)} %get-tuple-element.49.refs_2_.refs_1_, bf16[1024,1536]{1,0:T(8,128)(2,1)S(1)} %get-tuple-element.50.refs_3_.refs_2_, ...), custom_call_target="tpu_custom_call" | custom-call | flops 1 | bytes 1 | tf_op jit(solution)/shard_map/weights/pallas_call | solution.py:299
  23.9 1.5 %collective-permute-done.9.refs_1_ = bf16[832,128]{1,0:T(8,128)(2,1)S(1)} collective-permute-done((bf16[832,128]{1,0:T(8,128)(2,1)S(1)}, bf16[832,128]{1,0:T(8,128)(2,1)S(1)}, u32[]{:S(2)}, u32[]{:S(2)}) %collective-permute-start.9) | collective-permute-done | bytes 213024 | tf_op jit(solution)/shard_map/ppermute | solution.py:315
  25.3 0.0 collective-permute-done.8.refs_0_
  25.3 1.2 %weights.6 = (f32[128,1536]{1,0:T(8,128)S(1)}, bf16[256,1536]{1,0:T(8,128)(2,1)S(1)}, bf16[256,1536]{1,0:T(8,128)(2,1)S(1)}) custom-call(bf16[832,128]{1,0:T(8,128)(2,1)S(1)} %collective-permute-done.8.refs_0_, bf16[832,128]{1,0:T(8,128)(2,1)S(1)} %collective-permute-done.9.refs_1_, bf16[768,1536]{1,0:T(8,128)(2,1)S(1)} %get-tuple-element.49.refs_2_.refs_1_, ...), custom_call_target="tpu_custom_call" | custom-call | flops 1 | bytes 1 | tf_op jit(solution)/shard_map/weights/pallas_call | solution.py:299
  26.6 3.2 %collective-permute-done.6.refs_0_ = bf16[832,128]{1,0:T(8,128)(2,1)S(1)} collective-permute-done((bf16[832,128]{1,0:T(8,128)(2,1)S(1)}, bf16[832,128]{1,0:T(8,128)(2,1)S(1)}, u32[]{:S(2)}, u32[]{:S(2)}) %collective-permute-start.6) | collective-permute-done | bytes 213024 | tf_op jit(solution)/shard_map/ppermute | solution.py:315
  29.7 1.2 %weights.7 = (f32[128,1536]{1,0:T(8,128)S(1)}, bf16[256,1536]{1,0:T(8,128)(2,1)S(1)}, bf16[256,1536]{1,0:T(8,128)(2,1)S(1)}) custom-call(bf16[832,128]{1,0:T(8,128)(2,1)S(1)} %collective-permute-done.6.refs_0_, bf16[832,128]{1,0:T(8,128)(2,1)S(1)} %collective-permute-done.7.refs_1_, bf16[768,1536]{1,0:T(8,128)(2,1)S(1)} %get-tuple-element.49.refs_2_.refs_1_, ...), custom_call_target="tpu_custom_call" | custom-call | flops 1 | bytes 1 | tf_op jit(solution)/shard_map/weights/pallas_call | solution.py:299
  30.9 0.0 collective-permute-done.5.refs_0_
  30.9 2.7 %terms.1 = s32[1056,128]{1,0:T(8,128)S(1)} custom-call(bf16[832,128]{1,0:T(8,128)(2,1)S(1)} %collective-permute-done.5.refs_0_, bf16[768,1536]{1,0:T(8,128)(2,1)S(1)} %get-tuple-element.49.refs_2_.refs_1_, bf16[1024,1536]{1,0:T(8,128)(2,1)S(1)} %get-tuple-element.50.refs_3_.refs_2_, f32[8,1536]{1,0:T(8,128)S(1)} %get-tuple-element.51.refs_4_.refs_3_, ...), custom_call_target="tpu_custom_call" | custom-call | flops 1 | bytes 1 | tf_op jit(solution)/shard_map/terms/pallas_call | solution.py:322
  33.6 18.3 %all_to_all.5 = s32[1056,1,128]{2,1,0:T(1,128)S(1)} all-to-all(s32[1056,1,128]{2,1,0:T(1,128)S(1)} %bitcast.7), channel_id=1, replica_groups=mesh['samp'=4,'arow'=4,'acol'=2] {'arow','acol','samp'}, dimensions={0} | all-to-all | bytes 1081344 | tf_op jit(solution)/shard_map/all_to_all | solution.py:332
  52.0 1.1 %sum_terms.1 = f32[64,2048]{1,0:T(8,128)} custom-call(s32[1056,128]{1,0:T(8,128)S(1)} %bitcast.8), custom_call_target="tpu_custom_call" | custom-call | tf_op jit(solution)/shard_map/sum_terms/pallas_call | solution.py:333
  (9 shorter events, 0.0 us)
Async XLA Ops:
  0.0 0.8 %copy-start.3 = (s32[1536,8]{0,1:T(8,128)S(1)}, s32[1536,8]{0,1:T(8,128)}, u32[]{:S(2)}) copy-start(s32[1536,8]{0,1:T(8,128)} %param.7) | copy-start | bytes 147460
  0.8 8.4 %copy-start = (bf16[2048,768]{1,0:T(8,128)(2,1)S(1)}, bf16[2048,768]{1,0:T(8,128)(2,1)}, u32[]{:S(2)}) copy-start(bf16[2048,768]{1,0:T(8,128)(2,1)} %anchors_ref.1) | copy-start | bytes 9437188
  0.8 8.4 %copy-start.2 = (bf16[2048,64]{0,1:T(8,128)(2,1)S(1)}, bf16[2048,64]{0,1:T(8,128)(2,1)}, u32[]{:S(2)}) copy-start(bf16[2048,64]{0,1:T(8,128)(2,1)} %param.6) | copy-start | bytes 786436
  1.1 5.5 %collective-permute-start.2 = (s32[8,128]{1,0:T(8,128)S(1)}, s32[8,128]{1,0:T(8,128)S(1)}, u32[]{:S(2)}, u32[]{:S(2)}) collective-permute-start(s32[8,128]{1,0:T(8,128)S(1)} %get-tuple-element.39.refs_0_.refs_5_), channel_id=1, source_target_pairs={{0,6},{1,7},{2,4},{3,5},{4,2},{5,3},{6,0},{7,1},{8,14},{9,15},{10,... | collective-permute-start | bytes 12296 | tf_op jit(solution)/shard_map/ppermute | solution.py:263
  5.0 3.6 %collective-permute-start.1 = (s32[8,128]{1,0:T(8,128)S(1)}, s32[8,128]{1,0:T(8,128)S(1)}, u32[]{:S(2)}, u32[]{:S(2)}) collective-permute-start(s32[8,128]{1,0:T(8,128)S(1)} %get-tuple-element.39.refs_0_.refs_5_), channel_id=1, source_target_pairs={{0,4},{1,5},{2,6},{3,7},{4,0},{5,1},{6,2},{7,3},{8,12},{9,13},{10,... | collective-permute-start | bytes 12296 | tf_op jit(solution)/shard_map/ppermute | solution.py:263
  5.5 3.6 %collective-permute-start = (s32[8,128]{1,0:T(8,128)S(1)}, s32[8,128]{1,0:T(8,128)S(1)}, u32[]{:S(2)}, u32[]{:S(2)}) collective-permute-start(s32[8,128]{1,0:T(8,128)S(1)} %get-tuple-element.39.refs_0_.refs_5_), channel_id=1, source_target_pairs={{0,2},{1,3},{2,0},{3,1},{4,6},{5,7},{6,4},{7,5},{8,10},{9,11},{10,... | collective-permute-start | bytes 12296 | tf_op jit(solution)/shard_map/ppermute | solution.py:263
  9.2 9.9 %copy-start.1 = (bf16[1536,768]{1,0:T(8,128)(2,1)S(1)}, bf16[1536,768]{1,0:T(8,128)(2,1)}, u32[]{:S(2)}) copy-start(bf16[1536,768]{1,0:T(8,128)(2,1)} %rows_ref.1) | copy-start | bytes 7077892
  9.4 6.0 %collective-permute-start.4 = (bf16[832,128]{1,0:T(8,128)(2,1)S(1)}, bf16[832,128]{1,0:T(8,128)(2,1)S(1)}, u32[]{:S(2)}, u32[]{:S(2)}) collective-permute-start(bf16[832,128]{1,0:T(8,128)(2,1)S(1)} %get-tuple-element.46), channel_id=1, source_target_pairs={{0,4},{1,5},{2,6},{3,7},{4,0},{5,1},{6,2},{7,3},{8,12},{9,13},{10,... | collective-permute-start | bytes 638984 | tf_op jit(solution)/shard_map/ppermute | solution.py:315
  10.9 8.1 %collective-permute-start.10 = (bf16[832,128]{1,0:T(8,128)(2,1)S(1)}, bf16[832,128]{1,0:T(8,128)(2,1)S(1)}, u32[]{:S(2)}, u32[]{:S(2)}) collective-permute-start(bf16[832,128]{1,0:T(8,128)(2,1)S(1)} %get-tuple-element.58), channel_id=1, source_target_pairs={{0,2},{1,3},{2,0},{3,1},{4,6},{5,7},{6,4},{7,5},{8,10},{9,11},{10,... | collective-permute-start | bytes 638984 | tf_op jit(solution)/shard_map/ppermute | solution.py:315
  11.5 1.4 %collective-permute-start.3 = (s32[8,128]{1,0:T(8,128)S(1)}, s32[8,128]{1,0:T(8,128)S(1)}, u32[]{:S(2)}, u32[]{:S(2)}) collective-permute-start(s32[8,128]{1,0:T(8,128)S(1)} %get-tuple-element.40), channel_id=1, source_target_pairs={{0,1},{1,0},{2,3},{3,2},{4,5},{5,4},{6,7},{7,6},{8,9},{9,8},{10,11... | collective-permute-start | bytes 12296 | tf_op jit(solution)/shard_map/ppermute | solution.py:273
  11.5 15.1 %collective-permute-start.7 = (bf16[832,128]{1,0:T(8,128)(2,1)S(1)}, bf16[832,128]{1,0:T(8,128)(2,1)S(1)}, u32[]{:S(2)}, u32[]{:S(2)}) collective-permute-start(bf16[832,128]{1,0:T(8,128)(2,1)S(1)} %get-tuple-element.53), channel_id=1, source_target_pairs={{0,6},{1,7},{2,4},{3,5},{4,2},{5,3},{6,0},{7,1},{8,14},{9,15},{10,... | collective-permute-start | bytes 638984 | tf_op jit(solution)/shard_map/ppermute | solution.py:315
  13.1 12.2 %collective-permute-start.9 = (bf16[832,128]{1,0:T(8,128)(2,1)S(1)}, bf16[832,128]{1,0:T(8,128)(2,1)S(1)}, u32[]{:S(2)}, u32[]{:S(2)}) collective-permute-start(bf16[832,128]{1,0:T(8,128)(2,1)S(1)} %get-tuple-element.56), channel_id=1, source_target_pairs={{0,3},{1,2},{2,1},{3,0},{4,7},{5,6},{6,5},{7,4},{8,11},{9,10},{10,... | collective-permute-start | bytes 638984 | tf_op jit(solution)/shard_map/ppermute | solution.py:315
  15.3 10.0 %collective-permute-start.8 = (bf16[832,128]{1,0:T(8,128)(2,1)S(1)}, bf16[832,128]{1,0:T(8,128)(2,1)S(1)}, u32[]{:S(2)}, u32[]{:S(2)}) collective-permute-start(bf16[832,128]{1,0:T(8,128)(2,1)S(1)} %get-tuple-element.55), channel_id=1, source_target_pairs={{0,1},{1,0},{2,3},{3,2},{4,5},{5,4},{6,7},{7,6},{8,9},{9,8},{10,11... | collective-permute-start | bytes 638984 | tf_op jit(solution)/shard_map/ppermute | solution.py:315
  15.3 14.4 %collective-permute-start.6 = (bf16[832,128]{1,0:T(8,128)(2,1)S(1)}, bf16[832,128]{1,0:T(8,128)(2,1)S(1)}, u32[]{:S(2)}, u32[]{:S(2)}) collective-permute-start(bf16[832,128]{1,0:T(8,128)(2,1)S(1)} %get-tuple-element.52), channel_id=1, source_target_pairs={{0,5},{1,4},{2,7},{3,6},{4,1},{5,0},{6,3},{7,2},{8,13},{9,12},{10,... | collective-permute-start | bytes 638984 | tf_op jit(solution)/shard_map/ppermute | solution.py:315
  19.1 11.9 %collective-permute-start.5 = (bf16[832,128]{1,0:T(8,128)(2,1)S(1)}, bf16[832,128]{1,0:T(8,128)(2,1)S(1)}, u32[]{:S(2)}, u32[]{:S(2)}) collective-permute-start(bf16[832,128]{1,0:T(8,128)(2,1)S(1)} %get-tuple-element.47), channel_id=1, source_target_pairs={{0,7},{1,6},{2,5},{3,4},{4,3},{5,2},{6,1},{7,0},{8,15},{9,14},{10,... | collective-permute-start | bytes 638984 | tf_op jit(solution)/shard_map/ppermute | solution.py:315

commit v8 on v7

--- a/solution.py
+++ b/solution.py
@@ -14,7 +14,7 @@
 LANES = 128
 MISS = -1e30
 ORDER = [(2, 0), (4, 0), (6, 0), (3, 0), (5, 0), (7, 4), (1, 4)]
-GROUPS = [[0, 2], [4], [1, 3], [5, 6], [7]]
+GROUPS = [[0, 4], [2], [1, 3], [5, 6], [7]]
 IN_FLIGHT = 5
 FULL = 32704.0
 STEPS_PER_OCTAVE = 256.0

time: 54 us -> 54 us (level)
  no operation moved by 1% of the time
where the time goes in v8:
time: 54 us; the launch traced here: 53.1 us
  blocking collectives  18.3 us (34%)
  starting transfers between devices  12 us (22%)
  Pallas kernels  11.6 us (21%)
  waiting for transfers between devices  10.2 us (19%)
  local copies, waits for them, and re-layouts  0.81 us (2%)
    all_to_all x1, blocking collectives, per_device(): lax.all_to_all(terms[:, None, :], ('arow', 'acol', 'samp'), 0, 0, tiled=T...  18.3 us
    ppermute x7, starting transfers between devices, per_device(): held[s] = lax.ppermute(block, here, plan.pairs(s))  7.35 us
    ppermute x7, waiting for transfers between devices, per_device(): held[s] = lax.ppermute(block, here, plan.pairs(s))  6.78 us
    ppermute x3, starting transfers between devices, per_device(): lax.ppermute(wanted, here, plan.pairs(s))  4.6 us
    pallas_call x4, Pallas kernels, weigh(): pl.pallas_call(functools.partial(group_kernel, g, sizes), out_shape=(stru...  4.48 us
    ppermute x3, waiting for transfers between devices, per_device(): lax.ppermute(wanted, here, plan.pairs(s))  3.47 us
    pallas_call x1, Pallas kernels, per_device(): pl.pallas_call(rows_kernel, out_shape=(struct((depth, rows), bf16), struc...  2.71 us
    pallas_call x1, Pallas kernels, per_device(): pl.pallas_call(functools.partial(last_kernel, plan, copies, groups, sizes...  2.68 us
  transfers between devices with their start and end apart: 11, of which 7 were waited for; matrix products, arithmetic and copies ran while one was open for 0% of the time, Pallas kernels for 14%

profile of v8, /device:TPU:0, one launch (start us, length us, event | category | flops | bytes accessed | tf_op | source)
XLA Modules:
  0.0 53.1 jit_solution(13698535581653085849)
XLA Ops:
  0.0 0.8 %copy-done.3 = s32[1536,8]{0,1:T(8,128)S(1)} copy-done((s32[1536,8]{0,1:T(8,128)S(1)}, s32[1536,8]{0,1:T(8,128)}, u32[]{:S(2)}) %copy-start.3) | copy-done | bytes 49176
  0.8 0.3 prepare.1
  1.1 4.0 %collective-permute-start.2 = (s32[8,128]{1,0:T(8,128)S(1)}, s32[8,128]{1,0:T(8,128)S(1)}, u32[]{:S(2)}, u32[]{:S(2)}) collective-permute-start(s32[8,128]{1,0:T(8,128)S(1)} %get-tuple-element.39.refs_0_.refs_5_), channel_id=1, source_target_pairs={{0,6},{1,7},{2,4},{3,5},{4,2},{5,3},{6,0},{7,1},{8,14},{9,15},{10,... | collective-permute-start | bytes 12296 | tf_op jit(solution)/shard_map/ppermute | solution.py:263
  5.0 0.5 collective-permute-start.1
  5.5 0.1 collective-permute-start
  5.7 0.9 %collective-permute-done.2.refs_3_ = s32[8,128]{1,0:T(8,128)S(1)} collective-permute-done((s32[8,128]{1,0:T(8,128)S(1)}, s32[8,128]{1,0:T(8,128)S(1)}, u32[]{:S(2)}, u32[]{:S(2)}) %collective-permute-start.2) | collective-permute-done | bytes 4128 | tf_op jit(solution)/shard_map/ppermute | solution.py:263
  6.6 2.0 %collective-permute-done.1.refs_2_ = s32[8,128]{1,0:T(8,128)S(1)} collective-permute-done((s32[8,128]{1,0:T(8,128)S(1)}, s32[8,128]{1,0:T(8,128)S(1)}, u32[]{:S(2)}, u32[]{:S(2)}) %collective-permute-start.1) | collective-permute-done | bytes 4128 | tf_op jit(solution)/shard_map/ppermute | solution.py:263
  8.6 0.5 collective-permute-done.refs_1_
  9.2 0.2 cut_even.1
  9.4 1.6 %collective-permute-start.4 = (bf16[832,128]{1,0:T(8,128)(2,1)S(1)}, bf16[832,128]{1,0:T(8,128)(2,1)S(1)}, u32[]{:S(2)}, u32[]{:S(2)}) collective-permute-start(bf16[832,128]{1,0:T(8,128)(2,1)S(1)} %get-tuple-element.46), channel_id=1, source_target_pairs={{0,4},{1,5},{2,6},{3,7},{4,0},{5,1},{6,2},{7,3},{8,12},{9,13},{10,... | collective-permute-start | bytes 638984 | tf_op jit(solution)/shard_map/ppermute | solution.py:315
  10.9 0.5 %collective-permute-start.10 = (bf16[832,128]{1,0:T(8,128)(2,1)S(1)}, bf16[832,128]{1,0:T(8,128)(2,1)S(1)}, u32[]{:S(2)}, u32[]{:S(2)}) collective-permute-start(bf16[832,128]{1,0:T(8,128)(2,1)S(1)} %get-tuple-element.57), channel_id=1, source_target_pairs={{0,2},{1,3},{2,0},{3,1},{4,6},{5,7},{6,4},{7,5},{8,10},{9,11},{10,... | collective-permute-start | bytes 638984 | tf_op jit(solution)/shard_map/ppermute | solution.py:315
  11.5 0.0 collective-permute-start.3
  11.5 1.4 %collective-permute-start.7 = (bf16[832,128]{1,0:T(8,128)(2,1)S(1)}, bf16[832,128]{1,0:T(8,128)(2,1)S(1)}, u32[]{:S(2)}, u32[]{:S(2)}) collective-permute-start(bf16[832,128]{1,0:T(8,128)(2,1)S(1)} %get-tuple-element.53), channel_id=1, source_target_pairs={{0,6},{1,7},{2,4},{3,5},{4,2},{5,3},{6,0},{7,1},{8,14},{9,15},{10,... | collective-permute-start | bytes 638984 | tf_op jit(solution)/shard_map/ppermute | solution.py:315
  12.9 0.0 collective-permute-done.3.passed_ref
  12.9 0.2 cut_odd.1
  13.1 1.1 %collective-permute-start.9 = (bf16[832,128]{1,0:T(8,128)(2,1)S(1)}, bf16[832,128]{1,0:T(8,128)(2,1)S(1)}, u32[]{:S(2)}, u32[]{:S(2)}) collective-permute-start(bf16[832,128]{1,0:T(8,128)(2,1)S(1)} %get-tuple-element.56), channel_id=1, source_target_pairs={{0,3},{1,2},{2,1},{3,0},{4,7},{5,6},{6,5},{7,4},{8,11},{9,10},{10,... | collective-permute-start | bytes 638984 | tf_op jit(solution)/shard_map/ppermute | solution.py:315
  14.2 1.2 %collective-permute-done.4.refs_1_ = bf16[832,128]{1,0:T(8,128)(2,1)S(1)} collective-permute-done((bf16[832,128]{1,0:T(8,128)(2,1)S(1)}, bf16[832,128]{1,0:T(8,128)(2,1)S(1)}, u32[]{:S(2)}, u32[]{:S(2)}) %collective-permute-start.4) | collective-permute-done | bytes 213024 | tf_op jit(solution)/shard_map/ppermute | solution.py:315
  15.3 0.0 collective-permute-start.8
  15.3 2.7 %collective-permute-start.6 = (bf16[832,128]{1,0:T(8,128)(2,1)S(1)}, bf16[832,128]{1,0:T(8,128)(2,1)S(1)}, u32[]{:S(2)}, u32[]{:S(2)}) collective-permute-start(bf16[832,128]{1,0:T(8,128)(2,1)S(1)} %get-tuple-element.52), channel_id=1, source_target_pairs={{0,5},{1,4},{2,7},{3,6},{4,1},{5,0},{6,3},{7,2},{8,13},{9,12},{10,... | collective-permute-start | bytes 638984 | tf_op jit(solution)/shard_map/ppermute | solution.py:315
  18.1 1.0 %collective-permute-done.10.refs_0_ = bf16[832,128]{1,0:T(8,128)(2,1)S(1)} collective-permute-done((bf16[832,128]{1,0:T(8,128)(2,1)S(1)}, bf16[832,128]{1,0:T(8,128)(2,1)S(1)}, u32[]{:S(2)}, u32[]{:S(2)}) %collective-permute-start.10) | collective-permute-done | bytes 213024 | tf_op jit(solution)/shard_map/ppermute | solution.py:315
  19.1 2.7 %rows.1 = (bf16[768,1536]{1,0:T(8,128)(2,1)S(1)}, f32[8,1536]{1,0:T(8,128)S(1)}, bf16[1024,1536]{1,0:T(8,128)(2,1)S(1)}) custom-call(bf16[1536,768]{1,0:T(8,128)(2,1)S(1)} %copy-done.1, s32[8,1536]{1,0:T(8,128)S(1)} %get-tuple-element.48.slot_ref), custom_call_target="tpu_custom_call" | custom-call | flops 1 | bytes 1 | tf_op jit(solution)/shard_map/rows/pallas_call | solution.py:285
  21.8 1.3 %weights.4 = (f32[128,1536]{1,0:T(8,128)S(1)}, bf16[256,1536]{1,0:T(8,128)(2,1)S(1)}, bf16[256,1536]{1,0:T(8,128)(2,1)S(1)}) custom-call(bf16[832,128]{1,0:T(8,128)(2,1)S(1)} %get-tuple-element.58.refs_0_, bf16[832,128]{1,0:T(8,128)(2,1)S(1)} %collective-permute-done.4.refs_1_, bf16[768,1536]{1,0:T(8,128)(2,1)S(1)} %get-tuple-element.49.refs_2_.refs_1_, ...), custom_call_target="tpu_custom_call" | custom-call | flops 1 | bytes 1 | tf_op jit(solution)/shard_map/weights/pallas_call | solution.py:299
  23.1 0.8 %weights.5 = (f32[128,1536]{1,0:T(8,128)S(1)}, bf16[128,1536]{1,0:T(8,128)(2,1)S(1)}, bf16[128,1536]{1,0:T(8,128)(2,1)S(1)}) custom-call(bf16[832,128]{1,0:T(8,128)(2,1)S(1)} %collective-permute-done.10.refs_0_, bf16[768,1536]{1,0:T(8,128)(2,1)S(1)} %get-tuple-element.49.refs_2_.refs_1_, bf16[1024,1536]{1,0:T(8,128)(2,1)S(1)} %get-tuple-element.50.refs_3_.refs_2_, ...), custom_call_target="tpu_custom_call" | custom-call | flops 1 | bytes 1 | tf_op jit(solution)/shard_map/weights/pallas_call | solution.py:299
  23.9 1.5 %collective-permute-done.9.refs_1_ = bf16[832,128]{1,0:T(8,128)(2,1)S(1)} collective-permute-done((bf16[832,128]{1,0:T(8,128)(2,1)S(1)}, bf16[832,128]{1,0:T(8,128)(2,1)S(1)}, u32[]{:S(2)}, u32[]{:S(2)}) %collective-permute-start.9) | collective-permute-done | bytes 213024 | tf_op jit(solution)/shard_map/ppermute | solution.py:315
  25.3 0.0 collective-permute-done.8.refs_0_
  25.3 1.2 %weights.6 = (f32[128,1536]{1,0:T(8,128)S(1)}, bf16[256,1536]{1,0:T(8,128)(2,1)S(1)}, bf16[256,1536]{1,0:T(8,128)(2,1)S(1)}) custom-call(bf16[832,128]{1,0:T(8,128)(2,1)S(1)} %collective-permute-done.8.refs_0_, bf16[832,128]{1,0:T(8,128)(2,1)S(1)} %collective-permute-done.9.refs_1_, bf16[768,1536]{1,0:T(8,128)(2,1)S(1)} %get-tuple-element.49.refs_2_.refs_1_, ...), custom_call_target="tpu_custom_call" | custom-call | flops 1 | bytes 1 | tf_op jit(solution)/shard_map/weights/pallas_call | solution.py:299
  26.6 3.2 %collective-permute-done.6.refs_0_ = bf16[832,128]{1,0:T(8,128)(2,1)S(1)} collective-permute-done((bf16[832,128]{1,0:T(8,128)(2,1)S(1)}, bf16[832,128]{1,0:T(8,128)(2,1)S(1)}, u32[]{:S(2)}, u32[]{:S(2)}) %collective-permute-start.6) | collective-permute-done | bytes 213024 | tf_op jit(solution)/shard_map/ppermute | solution.py:315
  29.7 1.2 %weights.7 = (f32[128,1536]{1,0:T(8,128)S(1)}, bf16[256,1536]{1,0:T(8,128)(2,1)S(1)}, bf16[256,1536]{1,0:T(8,128)(2,1)S(1)}) custom-call(bf16[832,128]{1,0:T(8,128)(2,1)S(1)} %collective-permute-done.6.refs_0_, bf16[832,128]{1,0:T(8,128)(2,1)S(1)} %collective-permute-done.7.refs_1_, bf16[768,1536]{1,0:T(8,128)(2,1)S(1)} %get-tuple-element.49.refs_2_.refs_1_, ...), custom_call_target="tpu_custom_call" | custom-call | flops 1 | bytes 1 | tf_op jit(solution)/shard_map/weights/pallas_call | solution.py:299
  30.9 0.0 collective-permute-done.5.refs_0_
  30.9 2.7 %terms.1 = s32[1056,128]{1,0:T(8,128)S(1)} custom-call(bf16[832,128]{1,0:T(8,128)(2,1)S(1)} %collective-permute-done.5.refs_0_, bf16[768,1536]{1,0:T(8,128)(2,1)S(1)} %get-tuple-element.49.refs_2_.refs_1_, bf16[1024,1536]{1,0:T(8,128)(2,1)S(1)} %get-tuple-element.50.refs_3_.refs_2_, f32[8,1536]{1,0:T(8,128)S(1)} %get-tuple-element.51.refs_4_.refs_3_, ...), custom_call_target="tpu_custom_call" | custom-call | flops 1 | bytes 1 | tf_op jit(solution)/shard_map/terms/pallas_call | solution.py:322
  33.6 18.3 %all_to_all.5 = s32[1056,1,128]{2,1,0:T(1,128)S(1)} all-to-all(s32[1056,1,128]{2,1,0:T(1,128)S(1)} %bitcast.7), channel_id=1, replica_groups=mesh['samp'=4,'arow'=4,'acol'=2] {'arow','acol','samp'}, dimensions={0} | all-to-all | bytes 1081344 | tf_op jit(solution)/shard_map/all_to_all | solution.py:332
  52.0 1.1 %sum_terms.1 = f32[64,2048]{1,0:T(8,128)} custom-call(s32[1056,128]{1,0:T(8,128)S(1)} %bitcast.8), custom_call_target="tpu_custom_call" | custom-call | tf_op jit(solution)/shard_map/sum_terms/pallas_call | solution.py:333
  (9 shorter events, 0.0 us)
Async XLA Ops:
  0.0 0.8 %copy-start.3 = (s32[1536,8]{0,1:T(8,128)S(1)}, s32[1536,8]{0,1:T(8,128)}, u32[]{:S(2)}) copy-start(s32[1536,8]{0,1:T(8,128)} %param.7) | copy-start | bytes 147460
  0.8 8.4 %copy-start = (bf16[2048,768]{1,0:T(8,128)(2,1)S(1)}, bf16[2048,768]{1,0:T(8,128)(2,1)}, u32[]{:S(2)}) copy-start(bf16[2048,768]{1,0:T(8,128)(2,1)} %anchors_ref.1) | copy-start | bytes 9437188
  0.8 8.4 %copy-start.2 = (bf16[2048,64]{0,1:T(8,128)(2,1)S(1)}, bf16[2048,64]{0,1:T(8,128)(2,1)}, u32[]{:S(2)}) copy-start(bf16[2048,64]{0,1:T(8,128)(2,1)} %param.6) | copy-start | bytes 786436
  1.1 5.5 %collective-permute-start.2 = (s32[8,128]{1,0:T(8,128)S(1)}, s32[8,128]{1,0:T(8,128)S(1)}, u32[]{:S(2)}, u32[]{:S(2)}) collective-permute-start(s32[8,128]{1,0:T(8,128)S(1)} %get-tuple-element.39.refs_0_.refs_5_), channel_id=1, source_target_pairs={{0,6},{1,7},{2,4},{3,5},{4,2},{5,3},{6,0},{7,1},{8,14},{9,15},{10,... | collective-permute-start | bytes 12296 | tf_op jit(solution)/shard_map/ppermute | solution.py:263
  5.0 3.6 %collective-permute-start.1 = (s32[8,128]{1,0:T(8,128)S(1)}, s32[8,128]{1,0:T(8,128)S(1)}, u32[]{:S(2)}, u32[]{:S(2)}) collective-permute-start(s32[8,128]{1,0:T(8,128)S(1)} %get-tuple-element.39.refs_0_.refs_5_), channel_id=1, source_target_pairs={{0,4},{1,5},{2,6},{3,7},{4,0},{5,1},{6,2},{7,3},{8,12},{9,13},{10,... | collective-permute-start | bytes 12296 | tf_op jit(solution)/shard_map/ppermute | solution.py:263
  5.5 3.6 %collective-permute-start = (s32[8,128]{1,0:T(8,128)S(1)}, s32[8,128]{1,0:T(8,128)S(1)}, u32[]{:S(2)}, u32[]{:S(2)}) collective-permute-start(s32[8,128]{1,0:T(8,128)S(1)} %get-tuple-element.39.refs_0_.refs_5_), channel_id=1, source_target_pairs={{0,2},{1,3},{2,0},{3,1},{4,6},{5,7},{6,4},{7,5},{8,10},{9,11},{10,... | collective-permute-start | bytes 12296 | tf_op jit(solution)/shard_map/ppermute | solution.py:263
  9.2 9.9 %copy-start.1 = (bf16[1536,768]{1,0:T(8,128)(2,1)S(1)}, bf16[1536,768]{1,0:T(8,128)(2,1)}, u32[]{:S(2)}) copy-start(bf16[1536,768]{1,0:T(8,128)(2,1)} %rows_ref.1) | copy-start | bytes 7077892
  9.4 6.0 %collective-permute-start.4 = (bf16[832,128]{1,0:T(8,128)(2,1)S(1)}, bf16[832,128]{1,0:T(8,128)(2,1)S(1)}, u32[]{:S(2)}, u32[]{:S(2)}) collective-permute-start(bf16[832,128]{1,0:T(8,128)(2,1)S(1)} %get-tuple-element.46), channel_id=1, source_target_pairs={{0,4},{1,5},{2,6},{3,7},{4,0},{5,1},{6,2},{7,3},{8,12},{9,13},{10,... | collective-permute-start | bytes 638984 | tf_op jit(solution)/shard_map/ppermute | solution.py:315
  10.9 8.1 %collective-permute-start.10 = (bf16[832,128]{1,0:T(8,128)(2,1)S(1)}, bf16[832,128]{1,0:T(8,128)(2,1)S(1)}, u32[]{:S(2)}, u32[]{:S(2)}) collective-permute-start(bf16[832,128]{1,0:T(8,128)(2,1)S(1)} %get-tuple-element.57), channel_id=1, source_target_pairs={{0,2},{1,3},{2,0},{3,1},{4,6},{5,7},{6,4},{7,5},{8,10},{9,11},{10,... | collective-permute-start | bytes 638984 | tf_op jit(solution)/shard_map/ppermute | solution.py:315
  11.5 1.4 %collective-permute-start.3 = (s32[8,128]{1,0:T(8,128)S(1)}, s32[8,128]{1,0:T(8,128)S(1)}, u32[]{:S(2)}, u32[]{:S(2)}) collective-permute-start(s32[8,128]{1,0:T(8,128)S(1)} %get-tuple-element.40), channel_id=1, source_target_pairs={{0,1},{1,0},{2,3},{3,2},{4,5},{5,4},{6,7},{7,6},{8,9},{9,8},{10,11... | collective-permute-start | bytes 12296 | tf_op jit(solution)/shard_map/ppermute | solution.py:273
  11.5 15.1 %collective-permute-start.7 = (bf16[832,128]{1,0:T(8,128)(2,1)S(1)}, bf16[832,128]{1,0:T(8,128)(2,1)S(1)}, u32[]{:S(2)}, u32[]{:S(2)}) collective-permute-start(bf16[832,128]{1,0:T(8,128)(2,1)S(1)} %get-tuple-element.53), channel_id=1, source_target_pairs={{0,6},{1,7},{2,4},{3,5},{4,2},{5,3},{6,0},{7,1},{8,14},{9,15},{10,... | collective-permute-start | bytes 638984 | tf_op jit(solution)/shard_map/ppermute | solution.py:315
  13.1 12.2 %collective-permute-start.9 = (bf16[832,128]{1,0:T(8,128)(2,1)S(1)}, bf16[832,128]{1,0:T(8,128)(2,1)S(1)}, u32[]{:S(2)}, u32[]{:S(2)}) collective-permute-start(bf16[832,128]{1,0:T(8,128)(2,1)S(1)} %get-tuple-element.56), channel_id=1, source_target_pairs={{0,3},{1,2},{2,1},{3,0},{4,7},{5,6},{6,5},{7,4},{8,11},{9,10},{10,... | collective-permute-start | bytes 638984 | tf_op jit(solution)/shard_map/ppermute | solution.py:315
  15.3 10.0 %collective-permute-start.8 = (bf16[832,128]{1,0:T(8,128)(2,1)S(1)}, bf16[832,128]{1,0:T(8,128)(2,1)S(1)}, u32[]{:S(2)}, u32[]{:S(2)}) collective-permute-start(bf16[832,128]{1,0:T(8,128)(2,1)S(1)} %get-tuple-element.55), channel_id=1, source_target_pairs={{0,1},{1,0},{2,3},{3,2},{4,5},{5,4},{6,7},{7,6},{8,9},{9,8},{10,11... | collective-permute-start | bytes 638984 | tf_op jit(solution)/shard_map/ppermute | solution.py:315
  15.3 14.4 %collective-permute-start.6 = (bf16[832,128]{1,0:T(8,128)(2,1)S(1)}, bf16[832,128]{1,0:T(8,128)(2,1)S(1)}, u32[]{:S(2)}, u32[]{:S(2)}) collective-permute-start(bf16[832,128]{1,0:T(8,128)(2,1)S(1)} %get-tuple-element.52), channel_id=1, source_target_pairs={{0,5},{1,4},{2,7},{3,6},{4,1},{5,0},{6,3},{7,2},{8,13},{9,12},{10,... | collective-permute-start | bytes 638984 | tf_op jit(solution)/shard_map/ppermute | solution.py:315
  19.1 11.9 %collective-permute-start.5 = (bf16[832,128]{1,0:T(8,128)(2,1)S(1)}, bf16[832,128]{1,0:T(8,128)(2,1)S(1)}, u32[]{:S(2)}, u32[]{:S(2)}) collective-permute-start(bf16[832,128]{1,0:T(8,128)(2,1)S(1)} %get-tuple-element.47), channel_id=1, source_target_pairs={{0,7},{1,6},{2,5},{3,4},{4,3},{5,2},{6,1},{7,0},{8,15},{9,14},{10,... | collective-permute-start | bytes 638984 | tf_op jit(solution)/shard_map/ppermute | solution.py:315
